TPU v7x, 512 devices: a whole 4x8x8 slice. The times are simulated.
512 devices in a mesh: dp: 16 (over y, core), expert: 32 (over z, x).
Axes of the slice: x: 4, y: 8, z: 8, core: 2. Of those that a mesh axis runs over, the one named last changes fastest.
Arguments:
- tokens: bfloat16 [65536, 2048], P(('dp', 'expert')), may hold values from -6 to 6
- routes: int32 [65536, 8], P(('dp', 'expert')), may hold values from 0 to 127, as said below
- cotangent: bfloat16 [65536, 8, 384], P(('dp', 'expert')), may hold values from -6 to 6
- gate_weight: bfloat16 [32, 2048, 384], P('expert', 'dp'), may hold values from -0.125 to 0.125
- up_weight: bfloat16 [32, 2048, 384], P('expert', 'dp'), may hold values from -0.125 to 0.125
Outputs:
- token_grad: bfloat16 [65536, 2048], P(('dp', 'expert'))
- gate_grad: float32 [32, 2048, 384], P('expert', 'dp')
- up_grad: float32 [32, 2048, 384], P('expert', 'dp')
Inputs may be any that keep to these rules, and one draw needn't show every extreme that they name: `routes`: each row names 8 different experts. In the rows of one device no expert is named by more than 20 rows, and some expert below 32 is named by exactly 20 rows on every device.
All inputs are finite; a program needn't handle non-finite values.
Results may differ from a plain program's by a relative error of at most 0.02.
Values may be sent and summed in bfloat16 or wider, within the bound.
No kernel may reach another device: no remote copies, remote signals or barrier semaphores. Data moves between devices by JAX's collectives and lax.ppermute only.
A program may use at most 64 MiB of HBM per device.

v0:
```python
import jax
import jax.numpy as jnp
from jax import lax
from jax.sharding import PartitionSpec as P

CAP = 20


def times_transposed(left, matrix):
    return lax.dot_general(
        left, matrix, (((1,), (1,)), ((), ())), preferred_element_type=jnp.float32
    )


def make_deltas(grad_out, gate_pre, up_pre):
    sigmoid_gate = jax.nn.sigmoid(gate_pre)
    gate_delta = (
        grad_out * up_pre * sigmoid_gate * (1.0 + gate_pre * (1.0 - sigmoid_gate))
    ).astype(jnp.bfloat16)
    up_delta = (grad_out * gate_pre * sigmoid_gate).astype(jnp.bfloat16)
    return (gate_delta, up_delta)


def on_device(tokens, routes, cotangent, gate_weight, up_weight):
    peer_count = lax.axis_size("expert")
    token_count = tokens.shape[0]
    top_count = routes.shape[1]
    model_width = tokens.shape[1]
    hidden_width = cotangent.shape[2]
    capacity = CAP
    flat_ids = routes.reshape(-1)
    in_window = flat_ids < peer_count
    one_hot = (flat_ids[:, None] == jnp.arange(peer_count, dtype=jnp.int32)[None, :]).astype(
        jnp.int32
    )
    rank_table = jnp.cumsum(one_hot, axis=0) - one_hot
    own_rank = jnp.sum(rank_table * one_hot, axis=1)
    slot_index = jnp.where(in_window, flat_ids * capacity + own_rank, peer_count * capacity)
    buffer_rows = peer_count * capacity + 1
    repeated = jnp.repeat(tokens, top_count, axis=0)
    send_tokens = jnp.zeros((buffer_rows, model_width), jnp.bfloat16).at[slot_index].set(repeated)
    send_cot = (
        jnp.zeros((buffer_rows, hidden_width), jnp.bfloat16)
        .at[slot_index]
        .set(cotangent.reshape(-1, hidden_width))
    )
    send_tokens = send_tokens[:-1].reshape(peer_count, capacity, model_width)
    send_cot = send_cot[:-1].reshape(peer_count, capacity, hidden_width)
    stacked = jnp.concatenate((gate_weight, up_weight), axis=0)
    recv_tokens, recv_cot = (
        lax.all_to_all(send_tokens, "expert", split_axis=0, concat_axis=0, tiled=True),
        lax.all_to_all(send_cot, "expert", split_axis=0, concat_axis=0, tiled=True),
    )
    received = recv_tokens.reshape(-1, model_width)
    grad_out = recv_cot.reshape(-1, hidden_width).astype(jnp.float32)
    piece = lax.all_gather(stacked, "dp", axis=1, tiled=True)
    columns = received
    gate_pre = jnp.dot(columns, piece[0], preferred_element_type=jnp.float32)
    up_pre = jnp.dot(columns, piece[1], preferred_element_type=jnp.float32)
    gate_delta, up_delta = make_deltas(grad_out, gate_pre, up_pre)
    piece = lax.all_gather(stacked, "dp", axis=1, tiled=True)
    slot_grad = times_transposed(gate_delta, piece[0]) + times_transposed(up_delta, piece[1])
    slot_grad = slot_grad.astype(jnp.bfloat16).reshape(peer_count, capacity, model_width)
    returned = lax.all_to_all(slot_grad, "expert", split_axis=0, concat_axis=0, tiled=True)
    both_deltas = jnp.concatenate((gate_delta, up_delta), axis=1)
    padded = jnp.concatenate(
        (returned.reshape(-1, model_width), jnp.zeros((1, model_width), jnp.bfloat16)), axis=0
    )
    picked = padded[slot_index].astype(jnp.float32).reshape(token_count, top_count, model_width)
    token_grad = jnp.sum(picked, axis=1).astype(jnp.bfloat16)
    group_count = lax.axis_size("dp")
    share = model_width // group_count
    columns = received
    summed = lax.psum_scatter(
        lax.dot_general(
            columns, both_deltas, (((0,), (0,)), ((), ())), preferred_element_type=jnp.float32
        ).astype(jnp.bfloat16),
        "dp",
        scatter_dimension=0,
        tiled=True,
    ).astype(jnp.float32) * (1.0 / group_count)
    gate_grad = summed[:, :hidden_width].reshape(1, share, hidden_width)
    up_grad = summed[:, hidden_width:].reshape(1, share, hidden_width)
    return (token_grad, gate_grad, up_grad)


def solution(mesh):
    placed = (
        P(("dp", "expert"), None),
        P(("dp", "expert"), None),
        P(("dp", "expert"), None, None),
        P("expert", "dp", None),
        P("expert", "dp", None),
    )
    return jax.shard_map(
        on_device,
        mesh=mesh,
        in_specs=placed,
        out_specs=(P(("dp", "expert"), None), P("expert", "dp", None), P("expert", "dp", None)),
        check_vma=False,
    )
```

profile of v0, /device:TPU:58, one launch (start us, length us, event | category | flops | bytes accessed | tf_op | source)
XLA Modules:
  0.0 263.6 jit_solution(1229549674761401306)
XLA Ops:
  7.2 0.8 broadcast_compare_fusion
  8.6 0.8 copy.10
  10.1 9.0 %reduce-window.6 = s32[32,8,128]{2,1,0:T(8,128)S(1)} reduce-window(s32[32,8,128]{2,1,0:T(8,128)S(1)} %fusion.20, s32[]{:T(128)} %constant.11.clone.1), window={size=1x1x128 pad=0_0x0_0x127_0}, to_apply=%region_0.0 | reduce-window | flops 4161536 | bytes 262148 | tf_op jit(solution)/shard_map/reduce-window
  19.6 5.1 %scatter_custom_fusion = bf16[641,384]{1,0:T(8,128)(2,1)S(1)} fusion(s32[1024]{0:T(1024)S(1)} %bitcast.60, bf16[128,8,384]{2,1,0:T(8,128)(2,1)S(1)} %copy-done, bf16[]{:T(256)} %constant.8.clone.1), kind=kCustom, calls=%fused_computation.24 | custom fusion | bytes 1278722 | tf_op jit(solution)/shard_map/scatter | solution.py:45
  24.7 0.9 reshape.100
  25.7 13.5 %all-to-all-start = ((bf16[32,20,384]{2,1,0:T(8,128)(2,1)}), bf16[32,20,384]{2,1,0:T(8,128)(2,1)}, u32[]{:S(2)}, u32[]{:S(2)}) async-start(bf16[32,20,384]{2,1,0:T(8,128)(2,1)} %reshape.100), calls=%async_computation | async-start | bytes 1179648 | tf_op jit(solution)/shard_map/all_to_all | solution.py:52
  39.3 0.7 pad_maximum_fusion
  40.0 7.7 %scatter_custom_fusion.1 = bf16[641,2048]{1,0:T(8,128)(2,1)S(1)} fusion(s32[1024]{0:T(1024)S(1)} %bitcast.61, bf16[128,2048]{1,0:T(8,128)(2,1)} %param.5, bf16[]{:T(256)} %constant.8.clone.1), kind=kCustom, calls=%fused_computation.5 | custom fusion | bytes 3149826 | tf_op jit(solution)/shard_map/scatter | solution.py:41
  47.7 1.7 slice.39
  49.4 5.1 %reshape.102 = bf16[32,20,2048]{2,1,0:T(8,128)(2,1)} reshape(bf16[640,2048]{1,0:T(8,128)(2,1)} %slice.39) | data formatting | bytes 5242880 | tf_op jit(solution)/shard_map/reshape | solution.py:47
  54.5 2.9 %all-to-all-done = bf16[32,20,384]{2,1,0:T(8,128)(2,1)} async-done(((bf16[32,20,384]{2,1,0:T(8,128)(2,1)}), bf16[32,20,384]{2,1,0:T(8,128)(2,1)}, u32[]{:S(2)}, u32[]{:S(2)}) %all-to-all-start) | async-done | bytes 491552 | tf_op jit(solution)/shard_map/all_to_all | solution.py:52
  57.5 6.9 %all-to-all-start.1 = ((bf16[32,20,2048]{2,1,0:T(8,128)(2,1)}), bf16[32,20,2048]{2,1,0:T(8,128)(2,1)}, u32[]{:S(2)}, u32[]{:S(2)}) async-start(bf16[32,20,2048]{2,1,0:T(8,128)(2,1)} %reshape.102), calls=%async_computation.1 | async-start | bytes 6291456 | tf_op jit(solution)/shard_map/all_to_all | solution.py:51
  64.6 1.2 reshape.108
  65.8 1.3 copy.14
  67.1 68.0 %all-to-all-done.1 = bf16[32,20,2048]{2,1,0:T(8,128)(2,1)} async-done(((bf16[32,20,2048]{2,1,0:T(8,128)(2,1)}), bf16[32,20,2048]{2,1,0:T(8,128)(2,1)}, u32[]{:S(2)}, u32[]{:S(2)}) %all-to-all-start.1) | async-done | bytes 2621472 | tf_op jit(solution)/shard_map/all_to_all | solution.py:51
  135.0 3.6 %reshape.103 = bf16[640,2048]{1,0:T(8,128)(2,1)S(1)} reshape(bf16[32,20,2048]{2,1,0:T(8,128)(2,1)} %all-to-all-done.1) | data formatting | bytes 5242880 | tf_op jit(solution)/shard_map/reshape | solution.py:54
  138.7 3.3 %multiply_convert_fusion = (bf16[640,384]{0,1:T(8,128)(2,1)S(1)}, f32[640,384]{0,1:T(8,128)S(1)}) fusion(f32[640,384]{0,1:T(8,128)} %copy.14, bf16[640,2048]{1,0:T(8,128)(2,1)S(1)} %reshape.103, bf16[2,2048,384]{2,1,0:T(8,128)(2,1)} %all-gather.2.cloned.1.call-done), kind=kOutput, calls=%fused_computation.22 | convolution fusion | flops 1008107520 | bytes 6651904 | tf_op jit(solution)/shard_map/dot_general | solution.py:58
  142.1 1.6 fusion.10
  143.7 0.8 copy-done.4
  144.5 4.1 %convolution_convert_fusion = bf16[2048,768]{1,0:T(8,128)(2,1)} fusion(bf16[640,2048]{1,0:T(8,128)(2,1)S(1)} %reshape.103, bf16[640,384]{0,1:T(8,128)(2,1)S(1)} %get-tuple-element.5, bf16[640,384]{0,1:T(8,128)(2,1)S(1)} %fusion.10), kind=kOutput, calls=%fused_computation.7 | convolution fusion | flops 2016804864 | bytes 6750208 | tf_op jit(solution)/shard_map/dot_general | solution.py:75
  148.6 1.0 copy-done.5
  149.6 3.1 %fusion.4 = f32[640,2048]{1,0:T(8,128)S(1)} fusion(bf16[640,384]{0,1:T(8,128)(2,1)S(1)} %copy-done.5, bf16[2,2048,384]{2,1,0:T(8,128)(2,1)} %all-gather.2.cloned.1.call-done), kind=kOutput, calls=%fused_computation.12 | convolution fusion | flops 1006632960 | bytes 7307264 | tf_op jit(solution)/shard_map/dot_general | solution.py:10
  152.7 1.6 add_convert_fusion
  154.3 2.4 reshape.104
  156.7 7.8 %all-to-all-start.2 = ((bf16[32,20,2048]{2,1,0:T(8,128)(2,1)}), bf16[32,20,2048]{2,1,0:T(8,128)(2,1)}, u32[]{:S(2)}, u32[]{:S(2)}) async-start(bf16[32,20,2048]{2,1,0:T(8,128)(2,1)} %reshape.104), calls=%async_computation.2 | async-start | bytes 6291456 | tf_op jit(solution)/shard_map/all_to_all | solution.py:64
  164.5 71.5 %all-to-all-done.2 = bf16[32,20,2048]{2,1,0:T(8,128)(2,1)} async-done(((bf16[32,20,2048]{2,1,0:T(8,128)(2,1)}), bf16[32,20,2048]{2,1,0:T(8,128)(2,1)}, u32[]{:S(2)}, u32[]{:S(2)}) %all-to-all-start.2) | async-done | bytes 2621472 | tf_op jit(solution)/shard_map/all_to_all | solution.py:64
  236.0 5.2 %reshape.105 = bf16[640,2048]{1,0:T(8,128)(2,1)} reshape(bf16[32,20,2048]{2,1,0:T(8,128)(2,1)} %all-to-all-done.2) | data formatting | bytes 5242880 | tf_op jit(solution)/shard_map/reshape | solution.py:67
  241.3 1.9 concatenate.10
  243.2 6.0 %gather_fusion = bf16[1024,2048]{1,0:T(8,128)(2,1)} fusion(bf16[641,2048]{1,0:T(8,128)(2,1)S(1)} %concatenate.10, s32[1024]{0:T(1024)S(1)} %broadcast_clamp_fusion), kind=kCustom, calls=%fused_computation | custom fusion | bytes 8392704 | tf_op jit(solution)/shard_map/gather | solution.py:69
  249.2 5.9 %bitcast_reduce_fusion = bf16[128,2048]{1,0:T(8,128)(2,1)} fusion(bf16[1024,2048]{1,0:T(8,128)(2,1)} %gather_fusion), kind=kLoop, calls=%fused_computation.4 | loop fusion | flops 1835008 | bytes 4718592 | tf_op jit(solution)/shard_map/reduce_sum | solution.py:70
  255.0 1.0 convert_multiply_fusion
  256.0 0.8 slice_bitcast_fusion.14
  (42 shorter events, 2.2 us)
Async XLA Ops:
  7.2 12.4 %copy-start = (bf16[128,8,384]{2,1,0:T(8,128)(2,1)S(1)}, bf16[128,8,384]{2,1,0:T(8,128)(2,1)}, u32[]{:S(2)}) copy-start(bf16[128,8,384]{2,1,0:T(8,128)(2,1)} %param.7) | copy-start | bytes 2359300
  19.1 20.2 %copy-start.8 = (bf16[1,128,384]{2,1,0:T(8,128)(2,1)S(1)}, bf16[1,128,384]{2,1,0:T(8,128)(2,1)}, u32[]{:S(2)}) copy-start(bf16[1,128,384]{2,1,0:T(8,128)(2,1)} %param.9) | copy-start | bytes 294916
  19.1 20.2 %copy-start.9 = (bf16[1,128,384]{2,1,0:T(8,128)(2,1)S(1)}, bf16[1,128,384]{2,1,0:T(8,128)(2,1)}, u32[]{:S(2)}) copy-start(bf16[1,128,384]{2,1,0:T(8,128)(2,1)} %param.8) | copy-start | bytes 294916
  25.7 31.8 %all-to-all-start = ((bf16[32,20,384]{2,1,0:T(8,128)(2,1)}), bf16[32,20,384]{2,1,0:T(8,128)(2,1)}, u32[]{:S(2)}, u32[]{:S(2)}) async-start(bf16[32,20,384]{2,1,0:T(8,128)(2,1)} %reshape.100), calls=%async_computation | async-start | bytes 1179648 | tf_op jit(solution)/shard_map/all_to_all | solution.py:52
  39.2 99.5 %all-gather.2.cloned.1.call-start = ((), (), s32[]{:S(2)}) async-start(), calls=%async_computation.4 | async-start | bytes 3342336 | tf_op jit(solution)/shard_map/all_gather | solution.py:56
  57.5 77.6 %all-to-all-start.1 = ((bf16[32,20,2048]{2,1,0:T(8,128)(2,1)}), bf16[32,20,2048]{2,1,0:T(8,128)(2,1)}, u32[]{:S(2)}, u32[]{:S(2)}) async-start(bf16[32,20,2048]{2,1,0:T(8,128)(2,1)} %reshape.102), calls=%async_computation.1 | async-start | bytes 6291456 | tf_op jit(solution)/shard_map/all_to_all | solution.py:51
  64.4 190.7 %reduce-scatter.2.cloned.1.call-start = ((), (), s32[]{:S(2)}) async-start(), calls=%async_computation.5 | async-start | bytes 3342336 | tf_op jit(solution)/shard_map/reduce_scatter | solution.py:74
  138.7 3.4 %copy-start.1 = (bf16[2,2048,384]{2,1,0:T(8,128)(2,1)S(1)}, bf16[2,2048,384]{2,1,0:T(8,128)(2,1)}, u32[]{:S(2)}) copy-start(bf16[2,2048,384]{2,1,0:T(8,128)(2,1)} %all-gather.2.cloned.1.call-done) | copy-start | bytes 9437188
  138.7 3.4 %copy-start.3 = (f32[640,384]{0,1:T(8,128)S(1)}, f32[640,384]{0,1:T(8,128)}, u32[]{:S(2)}) copy-start(f32[640,384]{0,1:T(8,128)} %copy.14) | copy-start | bytes 2949124
  142.1 1.6 copy-start.6
  143.7 0.8 copy-start.4
  148.6 1.0 copy-start.5
  149.6 3.1 %copy-start.2 = (bf16[2,2048,384]{2,1,0:T(8,128)(2,1)S(1)}, bf16[2,2048,384]{2,1,0:T(8,128)(2,1)}, u32[]{:S(2)}) copy-start(bf16[2,2048,384]{2,1,0:T(8,128)(2,1)} %all-gather.2.cloned.1.call-done) | copy-start | bytes 9437188
  149.6 3.1 %copy-start.7 = (bf16[640,384]{0,1:T(8,128)(2,1)S(1)}, bf16[640,384]{0,1:T(8,128)(2,1)}, u32[]{:S(2)}) copy-start(bf16[640,384]{0,1:T(8,128)(2,1)} %copy-done.6) | copy-start | bytes 1474564
  156.7 79.3 %all-to-all-start.2 = ((bf16[32,20,2048]{2,1,0:T(8,128)(2,1)}), bf16[32,20,2048]{2,1,0:T(8,128)(2,1)}, u32[]{:S(2)}, u32[]{:S(2)}) async-start(bf16[32,20,2048]{2,1,0:T(8,128)(2,1)} %reshape.104), calls=%async_computation.2 | async-start | bytes 6291456 | tf_op jit(solution)/shard_map/all_to_all | solution.py:64
Sparse Core Ops, SparseCore 0:
  42.7 42.8 all-gather.1
  148.7 59.6 reduce-scatter.1
where the time goes:
time: 264 us
  waiting for transfers between devices  142 us (54%)
  local copies, waits for them, and re-layouts  46.5 us (18%)
  starting transfers between devices  28.5 us (11%)
  other arithmetic  18.2 us (7%)
  between operations  14.3 us (5%)
  matrix products  13.7 us (5%)
    all_to_all x1, waiting for transfers between devices, on_device(): lax.all_to_all(slot_grad, 'expert', split_axis=0, concat_axis=0, tiled=True)  71.5 us
    all_to_all x1, waiting for transfers between devices, on_device(): lax.all_to_all(send_tokens, 'expert', split_axis=0, concat_axis=0, tiled=...  68 us
    all_to_all x1, starting transfers between devices, on_device(): lax.all_to_all(send_cot, 'expert', split_axis=0, concat_axis=0, tiled=True)  13.5 us
    another operation x3, other arithmetic  9.15 us
    all_to_all x1, starting transfers between devices, on_device(): lax.all_to_all(slot_grad, 'expert', split_axis=0, concat_axis=0, tiled=True)  7.78 us
    scatter x1, local copies, waits for them, and re-layouts, on_device(): jnp.zeros((buffer_rows, model_width), jnp.bfloat16).at[slot_index]  7.7 us
    all_to_all x1, starting transfers between devices, on_device(): lax.all_to_all(send_tokens, 'expert', split_axis=0, concat_axis=0, tiled=...  6.9 us
    gather x1, local copies, waits for them, and re-layouts, on_device(): padded[slot_index].astype(jnp.float32)  5.98 us
  transfers between devices with their start and end apart: 5, of which 3 were waited for; matrix products, arithmetic and copies ran while one was open for 18% of the time, Pallas kernels for 0%

commit v1 on v0

v1 whole, which is shorter than its diff:
```python
import jax
import jax.numpy as jnp
from jax import lax
from jax.experimental import pallas as pl
from jax.experimental.pallas import tpu as pltpu
from jax.sharding import PartitionSpec as P

CAP = 20
BLOCK = 24
TAIL = 4
PER_ROW = 5
BACK = 40
VMEM = 40 * 2**20


def iota(shape, axis):
    return lax.broadcasted_iota(jnp.int32, shape, axis)


def one_if(condition):
    return jnp.where(condition, 1.0, 0.0).astype(jnp.bfloat16)


def dot(left, right):
    return jnp.dot(left, right, preferred_element_type=jnp.float32)


def times_transposed(left, right):
    return lax.dot_general(
        left, right, (((1,), (1,)), ((), ())), preferred_element_type=jnp.float32
    )


def ranks(routes, experts):
    top, count = routes.shape
    expert = iota((experts, count), 0)
    routed = jnp.zeros((experts, count), jnp.float32)
    for k in range(top):
        routed += jnp.where(routes[k : k + 1, :] == expert, 1.0, 0.0)
    earlier = one_if(iota((count, count), 0) < iota((count, count), 1))
    rank = dot(routed.astype(jnp.bfloat16), earlier)
    return rank, jnp.where(routed > 0.5, rank, -1.0)


def repeat_rows(experts, rows):
    row = iota((experts * rows, experts), 0)
    first = iota((experts * rows, experts), 1) * rows
    return one_if((row >= first) & (row < first + rows))


def pack_kernel(experts, routes_ref, tokens_ref, cot_ref, out_ref):
    routes = routes_ref[...]
    top, count = routes.shape
    width = tokens_ref.shape[1]
    hidden = cot_ref.shape[1]
    rank, place = ranks(routes, experts)
    at = dot(repeat_rows(experts, BLOCK), place.astype(jnp.bfloat16))
    row = iota((experts, BLOCK, count), 1).reshape(experts * BLOCK, count)
    pick = one_if(at == row.astype(jnp.float32))
    slots = count * top
    spread = one_if(lax.shift_right_logical(iota((count, slots), 1), 3) == iota((count, slots), 0))
    both = jnp.concatenate((routes.astype(jnp.float32), rank), axis=0).astype(jnp.bfloat16)
    wide = dot(both, spread)
    own = iota((top, slots), 0) == (iota((top, slots), 1) & (top - 1))
    named = jnp.sum(jnp.where(own, wide[:top], 0.0), axis=0, keepdims=True)
    slot_place = jnp.where(
        named == iota((experts, slots), 0).astype(jnp.float32), wide[top:], -1.0
    )
    slot_at = dot(repeat_rows(experts, 8), slot_place.astype(jnp.bfloat16))
    tail_row = iota((experts, 8, slots), 1).reshape(experts * 8, slots) - TAIL
    offset = jnp.where(tail_row >= 0, slot_at - tail_row.astype(jnp.float32), -1.0)
    cot = cot_ref[...]
    for i in range(PER_ROW + 1):
        low, high = i * hidden, min((i + 1) * hidden, width)
        rows = dot(pick, tokens_ref[:, low:high])
        if i < PER_ROW:
            tail = dot(one_if(offset == float(TAIL * i)), cot)
            rows = rows.reshape(experts, BLOCK, hidden)
            last = rows[:, BLOCK - 8 :] + tail.reshape(experts, 8, hidden)
            rows = jnp.concatenate((rows[:, : BLOCK - 8], last), axis=1)
            rows = rows.reshape(experts * BLOCK, hidden)
        out_ref[:, low:high] = rows.astype(jnp.bfloat16)


def combine_matrix_kernel(experts, routes_ref, out_ref):
    _, place = ranks(routes_ref[...], experts)
    count = place.shape[1]
    lane = iota((experts, experts * BACK), 1)
    first = iota((experts, experts * BACK), 0) * BACK
    mine = (lane >= first) & (lane < first + BACK)
    at = dot(place.T.astype(jnp.bfloat16), one_if(mine))
    within = jnp.sum(jnp.where(mine, lane - first, 0), axis=0, keepdims=True).astype(jnp.float32)
    low = jnp.where(within < CAP, within, -2.0)
    high = jnp.where(within < BLOCK, within - TAIL, within - BLOCK)
    high = jnp.where(within < CAP, -2.0, high)
    out_ref[:count] = one_if(at == low)
    out_ref[count:] = one_if(at == high)


def middle_kernel(received_ref, weight_ref, delta_ref, back_ref):
    rows, width = received_ref.shape
    hidden = weight_ref.shape[1] // 2
    blocks = rows // BLOCK
    received = received_ref[...]
    pre = dot(received, weight_ref[...])
    gate_pre, up_pre = pre[:, :hidden], pre[:, hidden:]
    tail = received.astype(jnp.float32).reshape(blocks, BLOCK, width)[:, BLOCK - 8 :]
    first = iota((blocks, 8, hidden), 1) < TAIL

    def cot(i):
        return tail[:, :, i * hidden : (i + 1) * hidden]

    grad_out = jnp.concatenate(
        (
            jnp.where(first, pltpu.roll(cot(0), TAIL, 1), cot(1)),
            jnp.where(first, pltpu.roll(cot(2), TAIL, 1), cot(3)),
            jnp.where(first, pltpu.roll(cot(4), TAIL, 1), 0.0),
        ),
        axis=1,
    ).reshape(rows, hidden)
    sigmoid_gate = jax.nn.sigmoid(gate_pre)
    gate_delta = grad_out * up_pre * sigmoid_gate * (1.0 + gate_pre * (1.0 - sigmoid_gate))
    up_delta = grad_out * gate_pre * sigmoid_gate
    delta = jnp.concatenate((gate_delta, up_delta), axis=1)
    delta_ref[...] = delta.astype(jnp.bfloat16)
    delta = delta.reshape(blocks, BLOCK, 2 * hidden)
    last = delta[:, BLOCK - 8 :]
    first = iota(last.shape, 1) < TAIL
    last = jnp.where(first, last, pltpu.roll(last, TAIL, 1))
    delta = jnp.concatenate((delta[:, : BLOCK - 8], last), axis=1)
    delta = delta.reshape(rows, 2 * hidden).astype(jnp.bfloat16)
    half = width // 2
    low = times_transposed(delta, weight_ref[:half]).reshape(blocks, BLOCK, half)
    high = times_transposed(delta, weight_ref[half:]).reshape(blocks, BLOCK, half)
    full = BLOCK - 8
    shared = jnp.where(iota((blocks, 8, half), 1) < TAIL, low[:, full:], high[:, full:])
    back = jnp.concatenate((low[:, :full], shared, high[:, :full]), axis=1)
    back_ref[...] = back.reshape(blocks * BACK, half).astype(jnp.bfloat16)


def combine_kernel(matrix_ref, returned_ref, out_ref):
    count = out_ref.shape[0]
    half = returned_ref.shape[1]
    returned = returned_ref[...]
    out_ref[:, :half] = dot(matrix_ref[:count], returned).astype(jnp.bfloat16)
    out_ref[:, half:] = dot(matrix_ref[count:], returned).astype(jnp.bfloat16)


def whole():
    return pl.BlockSpec(memory_space=pltpu.VMEM)


def call(kernel, out_shape, flops, moved, vmem=VMEM, **more):
    return pl.pallas_call(
        kernel,
        out_shape=out_shape,
        compiler_params=pltpu.CompilerParams(vmem_limit_bytes=vmem),
        cost_estimate=pl.CostEstimate(flops=flops, bytes_accessed=moved, transcendentals=0),
        **more,
    )


def on_device(tokens, routes, cotangent, gate_weight, up_weight):
    peers = lax.axis_size("expert")
    groups = lax.axis_size("dp")
    count, width = tokens.shape
    top = routes.shape[1]
    hidden = cotangent.shape[2]
    half = width // 2
    share = width // groups
    bf16 = jnp.bfloat16
    routes = routes.T
    stacked = jnp.concatenate((gate_weight[0], up_weight[0]), axis=1)
    weight = lax.all_gather(stacked, "dp", axis=0, tiled=True)
    rows = peers * BLOCK
    packed = call(
        lambda *refs: pack_kernel(peers, *refs),
        jax.ShapeDtypeStruct((rows, width), bf16),
        3 * 10**9,
        5 * 10**6,
        60 * 2**20,
        in_specs=[whole()] * 3,
        out_specs=whole(),
    )(routes, tokens, cotangent.reshape(count * top, hidden))
    received = lax.all_to_all(
        packed.reshape(peers, BLOCK, width), "expert", split_axis=0, concat_axis=0, tiled=True
    ).reshape(rows, width)
    matrix = call(
        lambda *refs: combine_matrix_kernel(peers, *refs),
        jax.ShapeDtypeStruct((2 * count, peers * BACK), bf16),
        10**8,
        10**6,
        in_specs=[whole()],
        out_specs=whole(),
    )(routes)
    steps = 2
    delta, back = call(
        middle_kernel,
        (
            jax.ShapeDtypeStruct((rows, 2 * hidden), bf16),
            jax.ShapeDtypeStruct((peers * BACK, half), bf16),
        ),
        5 * 10**9,
        10**7,
        grid=(steps,),
        in_specs=[
            pl.BlockSpec((rows // steps, width), lambda i: (i, 0)),
            pl.BlockSpec((width, 2 * hidden), lambda i: (0, 0)),
        ],
        out_specs=(
            pl.BlockSpec((rows // steps, 2 * hidden), lambda i: (i, 0)),
            pl.BlockSpec((peers * BACK // steps, half), lambda i: (i, 0)),
        ),
    )(received, weight)
    returned = lax.all_to_all(
        back.reshape(peers, BACK, half), "expert", split_axis=0, concat_axis=0, tiled=True
    ).reshape(peers * BACK, half)
    token_grad = call(
        combine_kernel,
        jax.ShapeDtypeStruct((count, width), bf16),
        10**9,
        4 * 10**6,
        in_specs=[whole()] * 2,
        out_specs=whole(),
    )(matrix, returned)
    weight_grad = lax.dot_general(
        received, delta, (((0,), (0,)), ((), ())), preferred_element_type=jnp.float32
    ).astype(bf16)
    summed = lax.psum_scatter(weight_grad, "dp", scatter_dimension=0, tiled=True)
    summed = summed.astype(jnp.float32) * (1.0 / groups)
    gate_grad = summed[:, :hidden].reshape(1, share, hidden)
    up_grad = summed[:, hidden:].reshape(1, share, hidden)
    return (token_grad, gate_grad, up_grad)


def solution(mesh):
    placed = (
        P(("dp", "expert"), None),
        P(("dp", "expert"), None),
        P(("dp", "expert"), None, None),
        P("expert", "dp", None),
        P("expert", "dp", None),
    )
    return jax.shard_map(
        on_device,
        mesh=mesh,
        in_specs=placed,
        out_specs=(P(("dp", "expert"), None), P("expert", "dp", None), P("expert", "dp", None)),
        check_vma=False,
    )
```

time: 264 us -> 190 us (0.72)
  the two profiles are of different devices: /device:TPU:58 before, /device:TPU:13 now
where the time goes in v1:
time: 190 us
  waiting for transfers between devices  132 us (69%)
  starting transfers between devices  19.5 us (10%)
  Pallas kernels  14.5 us (8%)
  between operations  14.1 us (7%)
  local copies, waits for them, and re-layouts  4.18 us (2%)
  matrix products  4.02 us (2%)
    all_to_all x1, waiting for transfers between devices, on_device(): lax.all_to_all(back.reshape(peers, BACK, half), 'expert', split_axis=0, c...  61.1 us
    all_gather x1, waiting for transfers between devices, on_device(): weight = lax.all_gather(stacked, 'dp', axis=0, tiled=True)  47.9 us
    all_to_all x1, waiting for transfers between devices, on_device(): lax.all_to_all(packed.reshape(peers, BLOCK, width), 'expert', split_axis=...  23 us
    all_to_all x1, starting transfers between devices, on_device(): lax.all_to_all(packed.reshape(peers, BLOCK, width), 'expert', split_axis=...  13 us
    pallas_call x1, Pallas kernels, on_device(): call(middle_kernel, (jax.ShapeDtypeStruct((rows, 2 * hidden), bf16), jax....  6.61 us
    all_to_all x1, starting transfers between devices, on_device(): lax.all_to_all(back.reshape(peers, BACK, half), 'expert', split_axis=0, c...  6.42 us
    pallas_call x1, Pallas kernels, on_device(): call(lambda *refs: pack_kernel(peers, *refs), jax.ShapeDtypeStruct((rows,...  5.79 us
    dot_general x1, matrix products, on_device(): lax.dot_general(received, delta, (((0,), (0,)), ((), ())), preferred_elem...  4.02 us
  transfers between devices with their start and end apart: 4, of which 3 were waited for; matrix products, arithmetic and copies ran while one was open for 0% of the time, Pallas kernels for 1%

profile of v1, /device:TPU:13, one launch (start us, length us, event | category | flops | bytes accessed | tf_op | source)
XLA Modules:
  0.0 190.1 jit_solution(17304233987483324419)
XLA Ops:
  7.2 5.8 %shard_map.77 = bf16[768,2048]{1,0:T(8,128)(2,1)} custom-call(s32[8,128]{1,0:T(8,128)} %bitcast.18, bf16[128,2048]{1,0:T(8,128)(2,1)} %refs_1_.1, bf16[1024,384]{1,0:T(8,128)(2,1)} %bitcast.23), custom_call_target="tpu_custom_call" | custom-call | flops 3000000000 | bytes 5000000 | tf_op jit(solution)/shard_map/pallas_call | solution.py:176
  13.0 0.0 copy-start.3
  13.0 0.0 copy-start.4
  13.0 13.0 %all-to-all-start = ((bf16[32,24,2048]{2,1,0:T(8,128)(2,1)}), bf16[32,24,2048]{2,1,0:T(8,128)(2,1)S(1)}, u32[]{:S(2)}, u32[]{:S(2)}) async-start(bf16[32,24,2048]{2,1,0:T(8,128)(2,1)} %bitcast.20), calls=%async_computation | async-start | bytes 6291456 | tf_op jit(solution)/shard_map/all_to_all | solution.py:185
  26.0 0.0 all-gather.2.cloned.1.call-start
  26.0 0.0 copy-done.3
  26.0 0.0 copy-done.4
  26.0 0.7 pad_maximum_fusion
  26.7 0.0 all-gather.2.cloned.1.call-update
  26.8 0.0 reduce-scatter.2.cloned.1.call-start
  26.8 47.9 %all-gather.2.cloned.1.call-done.weight_ref = bf16[2048,768]{1,0:T(8,128)(2,1)} async-done(((bf16[128,768]{1,0:T(8,128)(2,1)}), bf16[2048,768]{1,0:T(8,128)(2,1)}) %all-gather.2.cloned.1.call-update) | async-done | bytes 3145744 | tf_op jit(solution)/shard_map/all_gather | solution.py:174
  74.7 23.0 %all-to-all-done = bf16[32,24,2048]{2,1,0:T(8,128)(2,1)S(1)} async-done(((bf16[32,24,2048]{2,1,0:T(8,128)(2,1)}), bf16[32,24,2048]{2,1,0:T(8,128)(2,1)S(1)}, u32[]{:S(2)}, u32[]{:S(2)}) %all-to-all-start) | async-done | bytes 3145760 | tf_op jit(solution)/shard_map/all_to_all | solution.py:185
  97.8 0.0 copy-start.2
  97.8 1.9 copy-done.2
  99.7 6.6 %shard_map.78 = (bf16[768,768]{1,0:T(8,128)(2,1)S(1)}, bf16[1280,1024]{1,0:T(8,128)(2,1)S(1)}) custom-call(bf16[768,2048]{1,0:T(8,128)(2,1)S(1)} %bitcast.15, bf16[2048,768]{1,0:T(8,128)(2,1)S(1)} %copy-done.2), custom_call_target="tpu_custom_call" | custom-call | flops 5000000000 | bytes 10000000 | tf_op jit(solution)/shard_map/pallas_call | solution.py:197
  106.3 0.0 copy-start
  106.3 1.5 copy-done
  107.8 4.0 %convolution_convert_fusion = bf16[2048,768]{1,0:T(8,128)(2,1)} fusion(bf16[768,2048]{1,0:T(8,128)(2,1)S(1)} %bitcast.16, bf16[768,768]{1,0:T(8,128)(2,1)S(1)} %get-tuple-element.6), kind=kOutput, calls=%fused_computation | convolution fusion | flops 2417491968 | bytes 7471104 | tf_op jit(solution)/shard_map/dot_general | solution.py:226
  111.8 0.0 reduce-scatter.2.cloned.1.call-update
  111.9 0.0 copy-start.1
  111.9 6.4 %all-to-all-start.1 = ((bf16[32,40,1024]{2,1,0:T(8,128)(2,1)}), bf16[32,40,1024]{2,1,0:T(8,128)(2,1)S(1)}, u32[]{:S(2)}, u32[]{:S(2)}) async-start(bf16[32,40,1024]{2,1,0:T(8,128)(2,1)} %bitcast.17), calls=%async_computation.1 | async-start | bytes 5242880 | tf_op jit(solution)/shard_map/all_to_all | solution.py:215
  118.3 0.0 copy-done.1
  118.3 0.5 shard_map.76.matrix_ref
  118.8 61.1 %all-to-all-done.1 = bf16[32,40,1024]{2,1,0:T(8,128)(2,1)S(1)} async-done(((bf16[32,40,1024]{2,1,0:T(8,128)(2,1)}), bf16[32,40,1024]{2,1,0:T(8,128)(2,1)S(1)}, u32[]{:S(2)}, u32[]{:S(2)}) %all-to-all-start.1) | async-done | bytes 2621472 | tf_op jit(solution)/shard_map/all_to_all | solution.py:215
  179.8 1.7 shard_map.79
  181.5 0.0 reduce-scatter.2.cloned.1.call-done
  181.5 1.0 convert_multiply_fusion
  182.5 0.8 slice_bitcast_fusion
Async XLA Ops:
  13.0 13.1 %copy-start.3 = (bf16[1,128,384]{2,1,0:T(8,128)(2,1)S(1)}, bf16[1,128,384]{2,1,0:T(8,128)(2,1)}, u32[]{:S(2)}) copy-start(bf16[1,128,384]{2,1,0:T(8,128)(2,1)} %param.9) | copy-start | bytes 294916
  13.0 13.1 %copy-start.4 = (bf16[1,128,384]{2,1,0:T(8,128)(2,1)S(1)}, bf16[1,128,384]{2,1,0:T(8,128)(2,1)}, u32[]{:S(2)}) copy-start(bf16[1,128,384]{2,1,0:T(8,128)(2,1)} %param.8) | copy-start | bytes 294916
  13.0 84.8 %all-to-all-start = ((bf16[32,24,2048]{2,1,0:T(8,128)(2,1)}), bf16[32,24,2048]{2,1,0:T(8,128)(2,1)S(1)}, u32[]{:S(2)}, u32[]{:S(2)}) async-start(bf16[32,24,2048]{2,1,0:T(8,128)(2,1)} %bitcast.20), calls=%async_computation | async-start | bytes 6291456 | tf_op jit(solution)/shard_map/all_to_all | solution.py:185
  26.0 48.8 %all-gather.2.cloned.1.call-start = ((), (), s32[]{:S(2)}) async-start(), calls=%async_computation.3 | async-start | bytes 3342336 | tf_op jit(solution)/shard_map/all_gather | solution.py:174
  26.8 154.7 %reduce-scatter.2.cloned.1.call-start = ((), (), s32[]{:S(2)}) async-start(), calls=%async_computation.4 | async-start | bytes 3342336 | tf_op jit(solution)/shard_map/reduce_scatter | solution.py:229
  97.8 1.9 copy-start.2
  106.3 1.5 copy-start
  111.9 6.4 %copy-start.1 = (s32[128,8]{0,1:T(8,128)S(1)}, s32[128,8]{0,1:T(8,128)}, u32[]{:S(2)}) copy-start(s32[128,8]{0,1:T(8,128)} %param.6) | copy-start | bytes 12292
  111.9 68.0 %all-to-all-start.1 = ((bf16[32,40,1024]{2,1,0:T(8,128)(2,1)}), bf16[32,40,1024]{2,1,0:T(8,128)(2,1)S(1)}, u32[]{:S(2)}, u32[]{:S(2)}) async-start(bf16[32,40,1024]{2,1,0:T(8,128)(2,1)} %bitcast.17), calls=%async_computation.1 | async-start | bytes 5242880 | tf_op jit(solution)/shard_map/all_to_all | solution.py:215
Sparse Core Ops, SparseCore 0:
  29.5 45.1 all-gather.1
  112.0 59.3 reduce-scatter.1

commit v2 on v1

v2 whole, which is shorter than its diff:
```python
import jax
import jax.numpy as jnp
from jax import lax
from jax.experimental import pallas as pl
from jax.experimental.pallas import tpu as pltpu
from jax.sharding import PartitionSpec as P

CAP = 20
BLOCK = 24
TAIL = 4
PER_ROW = 5
BACK = 40
STEPS = 2
CORES = 2
FETCHES = 4
VMEM = 32 * 2**20
BIG = 60 * 2**20
MIDDLE = 46 * 2**20


def iota(shape, axis):
    return lax.broadcasted_iota(jnp.int32, shape, axis)


def one_if(condition):
    return jnp.where(condition, 1.0, 0.0).astype(jnp.bfloat16)


def dot(left, right):
    return jnp.dot(left, right, preferred_element_type=jnp.float32)


def times_transposed(left, right):
    return lax.dot_general(
        left, right, (((1,), (1,)), ((), ())), preferred_element_type=jnp.float32
    )


def transposed_times(left, right):
    return lax.dot_general(
        left, right, (((0,), (0,)), ((), ())), preferred_element_type=jnp.float32
    )


def ranks(routes, experts):
    top, count = routes.shape
    expert = iota((experts, count), 0)
    routed = jnp.zeros((experts, count), jnp.float32)
    for k in range(top):
        routed += jnp.where(routes[k : k + 1, :] == expert, 1.0, 0.0)
    earlier = one_if(iota((count, count), 0) < iota((count, count), 1))
    rank = dot(routed.astype(jnp.bfloat16), earlier)
    return rank, jnp.where(routed > 0.5, rank, -1.0)


def repeat_rows(experts, rows):
    row = iota((experts * rows, experts), 0)
    first = iota((experts * rows, experts), 1) * rows
    return one_if((row >= first) & (row < first + rows))


def pack_kernel(experts, routes_ref, tokens_ref, cot_ref, out_ref, held, sems):
    routes = routes_ref[...]
    top, count = routes.shape
    width = tokens_ref.shape[1]
    hidden = cot_ref.shape[1]
    rank, place = ranks(routes, experts)
    at = dot(repeat_rows(experts, BLOCK), place.astype(jnp.bfloat16))
    row = iota((experts, BLOCK, count), 1).reshape(experts * BLOCK, count)
    pick = one_if(at == row.astype(jnp.float32))
    slots = count * top
    spread = one_if(lax.shift_right_logical(iota((count, slots), 1), 3) == iota((count, slots), 0))
    both = jnp.concatenate((routes.astype(jnp.float32), rank), axis=0).astype(jnp.bfloat16)
    wide = dot(both, spread)
    own = iota((top, slots), 0) == (iota((top, slots), 1) & (top - 1))
    named = jnp.sum(jnp.where(own, wide[:top], 0.0), axis=0, keepdims=True)
    slot_place = jnp.where(
        named == iota((experts, slots), 0).astype(jnp.float32), wide[top:], -8.0
    )
    slot_at = dot(repeat_rows(experts, TAIL), slot_place.astype(jnp.bfloat16))
    offset = slot_at - (iota(slot_at.shape, 0) & (TAIL - 1)).astype(jnp.float32)
    cot = cot_ref[...]
    copies = []
    for i in range(PER_ROW + 1):
        low, high = i * hidden, min((i + 1) * hidden, width)
        rows = dot(pick, tokens_ref[:, low:high])
        if i < PER_ROW:
            tail = dot(one_if(offset == float(TAIL * i)), cot).reshape(experts // 2, 8, hidden)
            tail = jnp.stack((pltpu.roll(tail, TAIL, 1), tail), axis=1).reshape(experts, 8, hidden)
            rows = rows.reshape(experts, BLOCK, hidden)
            last = rows[:, BLOCK - 8 :]
            last = jnp.where(iota(last.shape, 1) < TAIL, last, tail)
            rows = jnp.concatenate((rows[:, : BLOCK - 8], last), axis=1)
            rows = rows.reshape(experts * BLOCK, hidden)
        held[:, low:high] = rows.astype(jnp.bfloat16)
        at = pl.ds(low, high - low)
        copy = pltpu.make_async_copy(held.at[:, at], out_ref.at[:, at], sems.at[i])
        copy.start()
        copies.append(copy)
    for copy in copies:
        copy.wait()


def prepare_kernel(experts, routes_ref, gate_ref, up_ref, out_ref, stacked_ref):
    _, place = ranks(routes_ref[...], experts)
    count = place.shape[1]
    lane = iota((experts, experts * BACK), 1)
    first = iota((experts, experts * BACK), 0) * BACK
    mine = (lane >= first) & (lane < first + BACK)
    at = dot(place.T.astype(jnp.bfloat16), one_if(mine))
    within = jnp.sum(jnp.where(mine, lane - first, 0), axis=0, keepdims=True).astype(jnp.float32)
    low = jnp.where(within < CAP, within, -2.0)
    high = jnp.where(within < BLOCK, within - TAIL, within - BLOCK)
    high = jnp.where(within < CAP, -2.0, high)
    out_ref[:count] = one_if(at == low)
    out_ref[count:] = one_if(at == high)
    stacked_ref[...] = jnp.concatenate((gate_ref[...], up_ref[...]), axis=1)


def middle_kernel(received_ref, source_ref, delta_ref, back_ref, held, sems, weight_ref, weight_sems):
    rows = received_ref.shape[0] // STEPS
    width = received_ref.shape[1]
    hidden = weight_ref.shape[1] // 2
    blocks = rows // BLOCK
    half = width // 2
    full = BLOCK - 8
    copies = []
    depth = width // FETCHES
    fetches = []
    for k in range(FETCHES):
        at = pl.ds(k * depth, depth)
        fetch = pltpu.make_async_copy(source_ref.at[at], weight_ref.at[at], weight_sems.at[k])
        fetch.start()
        fetches.append(fetch)
    for step in range(STEPS):
        part = slice(step * rows, (step + 1) * rows)
        received = received_ref[part]
        pre = jnp.zeros((rows, 2 * hidden), jnp.float32)
        for k, fetch in enumerate(fetches):
            if step == 0:
                fetch.wait()
            at = slice(k * depth, (k + 1) * depth)
            pre += dot(received[:, at], weight_ref[at])
        gate_pre, up_pre = pre[:, :hidden], pre[:, hidden:]
        tail = received.astype(jnp.float32).reshape(blocks, BLOCK, width)[:, full:]
        first = iota((blocks, 8, hidden), 1) < TAIL

        def cot(i, tail=tail):
            return tail[:, :, i * hidden : (i + 1) * hidden]

        grad_out = jnp.concatenate(
            (
                jnp.where(first, pltpu.roll(cot(0), TAIL, 1), cot(1)),
                jnp.where(first, pltpu.roll(cot(2), TAIL, 1), cot(3)),
                jnp.where(first, pltpu.roll(cot(4), TAIL, 1), 0.0),
            ),
            axis=1,
        ).reshape(rows, hidden)
        sigmoid_gate = jax.nn.sigmoid(gate_pre)
        gate_delta = grad_out * up_pre * sigmoid_gate * (1.0 + gate_pre * (1.0 - sigmoid_gate))
        up_delta = grad_out * gate_pre * sigmoid_gate
        delta = jnp.concatenate((gate_delta, up_delta), axis=1)
        delta_ref[part] = delta.astype(jnp.bfloat16)
        delta = delta.reshape(blocks, BLOCK, 2 * hidden)
        last = delta[:, full:]
        last = jnp.where(iota(last.shape, 1) < TAIL, last, pltpu.roll(last, TAIL, 1))
        delta = jnp.concatenate((delta[:, :full], last), axis=1)
        delta = delta.reshape(rows, 2 * hidden).astype(jnp.bfloat16)
        low = times_transposed(delta, weight_ref[:half]).reshape(blocks, BLOCK, half)
        high = times_transposed(delta, weight_ref[half:]).reshape(blocks, BLOCK, half)
        shared = jnp.where(iota((blocks, 8, half), 1) < TAIL, low[:, full:], high[:, full:])
        back = jnp.concatenate((low[:, :full], shared, high[:, :full]), axis=1)
        size = blocks * BACK
        held[step * size : (step + 1) * size] = back.reshape(size, half).astype(jnp.bfloat16)
        at = pl.ds(step * size, size)
        copy = pltpu.make_async_copy(held.at[at], back_ref.at[at], sems.at[step])
        copy.start()
        copies.append(copy)
    for copy in copies:
        copy.wait()


def combine_kernel(matrix_ref, returned_ref, out_ref):
    count = out_ref.shape[0]
    half = returned_ref.shape[1]
    returned = returned_ref[...]
    out_ref[:, :half] = dot(matrix_ref[:count], returned).astype(jnp.bfloat16)
    out_ref[:, half:] = dot(matrix_ref[count:], returned).astype(jnp.bfloat16)


def aligned(index, size):
    return pl.ds(pl.multiple_of(index * size, size), size)


def collect_kernel(place_ref, *refs):
    *blocks, out_ref = refs
    size = blocks[0].shape[0]
    for k, block in enumerate(blocks):
        at = lax.rem(place_ref[0] + len(blocks) - k, len(blocks))
        out_ref[aligned(at, size)] = block[...]


def assemble_kernel(size, place_ref, mine_ref, other_ref, out_ref):
    core = place_ref[1]
    for y in range(mine_ref.shape[0] // size):
        rows = slice(y * size, (y + 1) * size)
        out_ref[aligned(CORES * y + core, size)] = mine_ref[rows]
        out_ref[aligned(CORES * y + 1 - core, size)] = other_ref[rows]


def weight_grad_kernel(other, share, place_ref, received_ref, delta_ref, out_ref):
    core = 1 - place_ref[1] if other else place_ref[1]
    delta = delta_ref[...]
    batch = min(4, out_ref.shape[0] // share)
    for first in range(0, out_ref.shape[0] // share, batch):
        columns = [
            received_ref[:, aligned(CORES * y + core, share)] for y in range(first, first + batch)
        ]
        grad = transposed_times(jnp.concatenate(columns, axis=1), delta)
        out_ref[first * share : (first + batch) * share] = grad.astype(jnp.bfloat16)


def add_kernel(place_ref, mine_ref, other_ref, *out_refs):
    size = out_refs[0].shape[0]
    for k, out_ref in enumerate(out_refs):
        at = aligned(lax.rem(place_ref[0] + k, len(out_refs)), size)
        total = mine_ref[at].astype(jnp.float32) + other_ref[at].astype(jnp.float32)
        out_ref[...] = total.astype(jnp.bfloat16)


def total_kernel(groups, *refs):
    *terms, gate_ref, up_ref = refs
    hidden = gate_ref.shape[1]
    total = terms[0][...].astype(jnp.float32)
    for term in terms[1:]:
        total += term[...].astype(jnp.float32)
    total *= 1.0 / groups
    gate_ref[...] = total[:, :hidden]
    up_ref[...] = total[:, hidden:]


def whole():
    return pl.BlockSpec(memory_space=pltpu.VMEM)


def in_hbm():
    return pl.BlockSpec(memory_space=pltpu.HBM)


def call(kernel, out_shape, flops, moved, vmem=VMEM, **more):
    return pl.pallas_call(
        kernel,
        out_shape=out_shape,
        compiler_params=pltpu.CompilerParams(vmem_limit_bytes=vmem),
        cost_estimate=pl.CostEstimate(flops=flops, bytes_accessed=moved, transcendentals=0),
        **more,
    )


def held_and_sems(shape, count):
    return [pltpu.VMEM(shape, jnp.bfloat16), pltpu.SemaphoreType.DMA((count,))]


def on_device(tokens, routes, cotangent, gate_weight, up_weight):
    peers = lax.axis_size("expert")
    groups = lax.axis_size("dp")
    ys = groups // CORES
    count, width = tokens.shape
    top = routes.shape[1]
    hidden = cotangent.shape[2]
    share = width // groups
    half = width // 2
    bf16 = jnp.bfloat16
    rows = peers * BLOCK
    routes = routes.T
    mine = lax.axis_index("dp")
    place = jnp.stack((mine // CORES, mine % CORES)).astype(jnp.int32)
    scalars = pl.BlockSpec(memory_space=pltpu.SMEM)

    def shape(*dims, kind=bf16):
        return jax.ShapeDtypeStruct(dims, kind)

    def exchange(block, size):
        out = lax.all_to_all(
            block.reshape(peers, size, -1), "expert", split_axis=0, concat_axis=0, tiled=True
        )
        return out.reshape(peers * size, -1)

    def along_y(block, k):
        pairs = [
            (y * CORES + c, (y + k) % ys * CORES + c) for y in range(ys) for c in range(CORES)
        ]
        return lax.ppermute(block, "dp", pairs)

    def other_core(block):
        return lax.ppermute(block, "dp", [(d, d ^ 1) for d in range(groups)])

    packed = call(
        lambda *refs: pack_kernel(peers, *refs),
        shape(rows, width),
        2 * 10**9,
        5 * 10**6,
        BIG,
        in_specs=[whole()] * 3,
        out_specs=in_hbm(),
        scratch_shapes=held_and_sems((rows, width), PER_ROW + 1),
    )(routes, tokens, cotangent.reshape(count * top, hidden))
    received = exchange(packed, BLOCK)
    matrix, stacked = call(
        lambda *refs: prepare_kernel(peers, *refs),
        (shape(2 * count, peers * BACK), shape(share, 2 * hidden)),
        2 * 10**9,
        10**6,
        in_specs=[whole()] * 3,
        out_specs=(whole(), whole()),
    )(routes, gate_weight[0], up_weight[0])
    blocks = [stacked] + [along_y(stacked, k) for k in range(1, ys)]
    of_core = call(
        collect_kernel,
        shape(ys * share, 2 * hidden),
        10**6,
        3 * 10**6,
        in_specs=[scalars] + [whole()] * ys,
        out_specs=whole(),
    )(place, *blocks)
    weight = call(
        lambda *refs: assemble_kernel(share, *refs),
        shape(width, 2 * hidden),
        10**6,
        6 * 10**6,
        in_specs=[scalars] + [whole()] * 2,
        out_specs=whole(),
    )(place, of_core, other_core(of_core))
    delta, back = call(
        middle_kernel,
        (shape(rows, 2 * hidden), shape(peers * BACK, half)),
        5 * 10**9,
        10**7,
        MIDDLE,
        in_specs=[whole(), pl.BlockSpec(memory_space=pl.ANY)],
        out_specs=(whole(), in_hbm()),
        scratch_shapes=held_and_sems((peers * BACK, half), STEPS)
        + held_and_sems((width, 2 * hidden), FETCHES),
    )(received, weight)
    returned = exchange(back, BACK)
    grads = [
        call(
            lambda *refs, other=other: weight_grad_kernel(other, share, *refs),
            shape(ys * share, 2 * hidden),
            2 * 10**9,
            5 * 10**6,
            in_specs=[scalars] + [whole()] * 2,
            out_specs=whole(),
        )(place, received, delta)
        for other in (True, False)
    ]
    sums = call(
        add_kernel,
        (shape(share, 2 * hidden),) * ys,
        10**6,
        5 * 10**6,
        in_specs=[scalars] + [whole()] * 2,
        out_specs=(whole(),) * ys,
    )(place, grads[1], other_core(grads[0]))
    terms = [sums[0]] + [along_y(sums[k], k) for k in range(1, ys)]
    weight_shape = shape(share, hidden, kind=jnp.float32)
    gate_grad, up_grad = call(
        lambda *refs: total_kernel(groups, *refs),
        (weight_shape, weight_shape),
        10**6,
        2 * 10**6,
        in_specs=[whole()] * ys,
        out_specs=(whole(), whole()),
    )(*terms)
    token_grad = call(
        combine_kernel,
        shape(count, width),
        10**9,
        4 * 10**6,
        in_specs=[whole()] * 2,
        out_specs=whole(),
    )(matrix, returned)
    return (token_grad, gate_grad[None], up_grad[None])


def solution(mesh):
    placed = (
        P(("dp", "expert"), None),
        P(("dp", "expert"), None),
        P(("dp", "expert"), None, None),
        P("expert", "dp", None),
        P("expert", "dp", None),
    )
    return jax.shard_map(
        on_device,
        mesh=mesh,
        in_specs=placed,
        out_specs=(P(("dp", "expert"), None), P("expert", "dp", None), P("expert", "dp", None)),
        check_vma=False,
    )
```

time: 190 us -> 179 us (0.942)
  the two profiles are of different devices: /device:TPU:13 before, /device:TPU:11 now
where the time goes in v2:
time: 179 us; the launch traced here: 178 us
  starting transfers between devices  80.6 us (45%)
  waiting for transfers between devices  61.2 us (34%)
  Pallas kernels  24 us (13%)
  local copies, waits for them, and re-layouts  10.9 us (6%)
    ppermute x14, starting transfers between devices, along_y(): return lax.ppermute(block, 'dp', pairs)  53.8 us
    ppermute x14, waiting for transfers between devices, along_y(): return lax.ppermute(block, 'dp', pairs)  49.7 us
    all_to_all x2, starting transfers between devices, exchange(): lax.all_to_all(block.reshape(peers, size, -1), 'expert', split_axis=0, co...  19.6 us
    unnamed x26, local copies, waits for them, and re-layouts  10.9 us
    pallas_call x1, Pallas kernels, on_device(): call(middle_kernel, (shape(rows, 2 * hidden), shape(peers * BACK, half)),...  9.64 us
    all_to_all x2, waiting for transfers between devices, exchange(): lax.all_to_all(block.reshape(peers, size, -1), 'expert', split_axis=0, co...  7.65 us
    ppermute x2, starting transfers between devices, other_core(): return lax.ppermute(block, 'dp', [(d, d ^ 1) for d in range(groups)])  7.23 us
    pallas_call x1, Pallas kernels, on_device(): call(lambda *refs: pack_kernel(peers, *refs), shape(rows, width), 2 * 10...  4.31 us
  transfers between devices with their start and end apart: 18, of which 10 were waited for; matrix products, arithmetic and copies ran while one was open for 0% of the time, Pallas kernels for 5%

profile of v2, /device:TPU:11, one launch (start us, length us, event | category | flops | bytes accessed | tf_op | source)
XLA Modules:
  0.0 177.7 jit_solution(10551450416875713930)
XLA Ops:
  0.6 4.3 %shard_map.77 = bf16[768,2048]{1,0:T(8,128)(2,1)} custom-call(s32[8,128]{1,0:T(8,128)} %bitcast.19, bf16[128,2048]{1,0:T(8,128)(2,1)} %refs_1_.1, bf16[1024,384]{1,0:T(8,128)(2,1)} %bitcast.22), custom_call_target="tpu_custom_call" | custom-call | flops 2000000000 | bytes 5000000 | tf_op jit(solution)/shard_map/pallas_call | solution.py:298
  5.0 13.0 %all-to-all-start = ((bf16[32,24,2048]{2,1,0:T(8,128)(2,1)}), bf16[32,24,2048]{2,1,0:T(8,128)(2,1)S(1)}, u32[]{:S(2)}, u32[]{:S(2)}) async-start(bf16[32,24,2048]{2,1,0:T(8,128)(2,1)} %bitcast.21), calls=%async_computation | async-start | bytes 6291456 | tf_op jit(solution)/shard_map/all_to_all | solution.py:284
  19.4 2.1 %collective-permute-start.6 = (bf16[128,768]{1,0:T(8,128)(2,1)S(1)}, bf16[128,768]{1,0:T(8,128)(2,1)S(1)}, u32[]{:S(2)}, u32[]{:S(2)}) collective-permute-start(bf16[128,768]{1,0:T(8,128)(2,1)S(1)} %get-tuple-element.18.refs_0_), channel_id=1, source_target_pairs={{0,448},{32,480},{64,0},{96,32},{128,64},{160,96},{192,128},{224,1... | collective-permute-start | bytes 589832 | tf_op jit(solution)/shard_map/ppermute | solution.py:293
  21.5 5.9 %collective-permute-start.5 = (bf16[128,768]{1,0:T(8,128)(2,1)S(1)}, bf16[128,768]{1,0:T(8,128)(2,1)S(1)}, u32[]{:S(2)}, u32[]{:S(2)}) collective-permute-start(bf16[128,768]{1,0:T(8,128)(2,1)S(1)} %get-tuple-element.18.refs_0_), channel_id=1, source_target_pairs={{0,384},{32,416},{64,448},{96,480},{128,0},{160,32},{192,64},{224,... | collective-permute-start | bytes 589832 | tf_op jit(solution)/shard_map/ppermute | solution.py:293
  27.4 3.6 %collective-permute-start.4 = (bf16[128,768]{1,0:T(8,128)(2,1)S(1)}, bf16[128,768]{1,0:T(8,128)(2,1)}, u32[]{:S(2)}, u32[]{:S(2)}) collective-permute-start(bf16[128,768]{1,0:T(8,128)(2,1)S(1)} %get-tuple-element.18.refs_0_), channel_id=1, source_target_pairs={{0,320},{32,352},{64,384},{96,416},{128,448},{160,480},{192,0},{22... | collective-permute-start | bytes 589832 | tf_op jit(solution)/shard_map/ppermute | solution.py:293
  31.0 4.8 %collective-permute-start.3 = (bf16[128,768]{1,0:T(8,128)(2,1)S(1)}, bf16[128,768]{1,0:T(8,128)(2,1)}, u32[]{:S(2)}, u32[]{:S(2)}) collective-permute-start(bf16[128,768]{1,0:T(8,128)(2,1)S(1)} %get-tuple-element.18.refs_0_), channel_id=1, source_target_pairs={{0,256},{32,288},{64,320},{96,352},{128,384},{160,416},{192,448},{... | collective-permute-start | bytes 589832 | tf_op jit(solution)/shard_map/ppermute | solution.py:293
  35.8 3.4 %collective-permute-start.2 = (bf16[128,768]{1,0:T(8,128)(2,1)S(1)}, bf16[128,768]{1,0:T(8,128)(2,1)}, u32[]{:S(2)}, u32[]{:S(2)}) collective-permute-start(bf16[128,768]{1,0:T(8,128)(2,1)S(1)} %get-tuple-element.18.refs_0_), channel_id=1, source_target_pairs={{0,192},{32,224},{64,256},{96,288},{128,320},{160,352},{192,384},{... | collective-permute-start | bytes 589832 | tf_op jit(solution)/shard_map/ppermute | solution.py:293
  39.2 4.2 %collective-permute-start.1 = (bf16[128,768]{1,0:T(8,128)(2,1)S(1)}, bf16[128,768]{1,0:T(8,128)(2,1)}, u32[]{:S(2)}, u32[]{:S(2)}) collective-permute-start(bf16[128,768]{1,0:T(8,128)(2,1)S(1)} %get-tuple-element.18.refs_0_), channel_id=1, source_target_pairs={{0,128},{32,160},{64,192},{96,224},{128,256},{160,288},{192,320},{... | collective-permute-start | bytes 589832 | tf_op jit(solution)/shard_map/ppermute | solution.py:293
  44.1 2.3 %collective-permute-start = (bf16[128,768]{1,0:T(8,128)(2,1)S(1)}, bf16[128,768]{1,0:T(8,128)(2,1)}, u32[]{:S(2)}, u32[]{:S(2)}) collective-permute-start(bf16[128,768]{1,0:T(8,128)(2,1)S(1)} %get-tuple-element.18.refs_0_), channel_id=1, source_target_pairs={{0,64},{32,96},{64,128},{96,160},{128,192},{160,224},{192,256},{22... | collective-permute-start | bytes 589832 | tf_op jit(solution)/shard_map/ppermute | solution.py:293
  46.5 13.7 %collective-permute-done.3.refs_4_ = bf16[128,768]{1,0:T(8,128)(2,1)} collective-permute-done((bf16[128,768]{1,0:T(8,128)(2,1)S(1)}, bf16[128,768]{1,0:T(8,128)(2,1)}, u32[]{:S(2)}, u32[]{:S(2)}) %collective-permute-start.3) | collective-permute-done | bytes 196640 | tf_op jit(solution)/shard_map/ppermute | solution.py:293
  60.3 8.0 %collective-permute-done.1.refs_2_ = bf16[128,768]{1,0:T(8,128)(2,1)} collective-permute-done((bf16[128,768]{1,0:T(8,128)(2,1)S(1)}, bf16[128,768]{1,0:T(8,128)(2,1)}, u32[]{:S(2)}, u32[]{:S(2)}) %collective-permute-start.1) | collective-permute-done | bytes 196640 | tf_op jit(solution)/shard_map/ppermute | solution.py:293
  68.3 2.5 %collective-permute-done.refs_1_ = bf16[128,768]{1,0:T(8,128)(2,1)} collective-permute-done((bf16[128,768]{1,0:T(8,128)(2,1)S(1)}, bf16[128,768]{1,0:T(8,128)(2,1)}, u32[]{:S(2)}, u32[]{:S(2)}) %collective-permute-start) | collective-permute-done | bytes 196640 | tf_op jit(solution)/shard_map/ppermute | solution.py:293
  73.1 3.5 %collective-permute-start.7 = (bf16[1024,768]{1,0:T(8,128)(2,1)S(1)}, bf16[1024,768]{1,0:T(8,128)(2,1)S(1)}, u32[]{:S(2)}, u32[]{:S(2)}) collective-permute-start(bf16[1024,768]{1,0:T(8,128)(2,1)S(1)} %shard_map.78.refs_1_), channel_id=1, source_target_pairs={{0,32},{32,0},{64,96},{96,64},{128,160},{160,128},{192,224},{224,1... | collective-permute-start | bytes 4718600 | tf_op jit(solution)/shard_map/ppermute | solution.py:296
  76.6 3.0 %collective-permute-done.7.refs_2_ = bf16[1024,768]{1,0:T(8,128)(2,1)S(1)} collective-permute-done((bf16[1024,768]{1,0:T(8,128)(2,1)S(1)}, bf16[1024,768]{1,0:T(8,128)(2,1)S(1)}, u32[]{:S(2)}, u32[]{:S(2)}) %collective-permute-start.7) | collective-permute-done | bytes 1572896 | tf_op jit(solution)/shard_map/ppermute | solution.py:296
  82.1 7.6 %all-to-all-done = bf16[32,24,2048]{2,1,0:T(8,128)(2,1)S(1)} async-done(((bf16[32,24,2048]{2,1,0:T(8,128)(2,1)}), bf16[32,24,2048]{2,1,0:T(8,128)(2,1)S(1)}, u32[]{:S(2)}, u32[]{:S(2)}) %all-to-all-start) | async-done | bytes 3145760 | tf_op jit(solution)/shard_map/all_to_all | solution.py:284
  89.7 9.6 %shard_map.80 = (bf16[768,768]{1,0:T(8,128)(2,1)S(1)}, bf16[1280,1024]{1,0:T(8,128)(2,1)S(1)}) custom-call(bf16[768,2048]{1,0:T(8,128)(2,1)S(1)} %bitcast.13, bf16[2048,768]{1,0:T(8,128)(2,1)} %copy-done.2), custom_call_target="tpu_custom_call" | custom-call | flops 5000000000 | bytes 10000000 | tf_op jit(solution)/shard_map/pallas_call | solution.py:334
  101.9 6.5 %all-to-all-start.1 = ((bf16[32,40,1024]{2,1,0:T(8,128)(2,1)}), bf16[32,40,1024]{2,1,0:T(8,128)(2,1)S(1)}, u32[]{:S(2)}, u32[]{:S(2)}) async-start(bf16[32,40,1024]{2,1,0:T(8,128)(2,1)} %bitcast.16), calls=%async_computation.1 | async-start | bytes 5242880 | tf_op jit(solution)/shard_map/all_to_all | solution.py:284
  108.5 1.9 %copy-done.1 = bf16[32,24,2048]{2,1,0:T(8,128)(2,1)S(1)} copy-done((bf16[32,24,2048]{2,1,0:T(8,128)(2,1)S(1)}, bf16[32,24,2048]{2,1,0:T(8,128)(2,1)}, u32[]{:S(2)}) %copy-start.1) | copy-done | bytes 3145752
  111.6 2.0 %shard_map.83 = bf16[1024,768]{1,0:T(8,128)(2,1)S(1)} custom-call(s32[2]{0:T(128)S(1)} %pad_add_fusion.place_ref.refs_0_, bf16[768,2048]{1,0:T(8,128)(2,1)S(1)} %bitcast.14, bf16[768,768]{1,0:T(8,128)(2,1)S(1)} %copy-done.12), custom_call_target="tpu_custom_call" | custom-call | flops 2000000000 | bytes 5000000 | tf_op jit(solution)/shard_map/pallas_call | solution.py:347
  113.6 3.7 %collective-permute-start.8 = (bf16[1024,768]{1,0:T(8,128)(2,1)S(1)}, bf16[1024,768]{1,0:T(8,128)(2,1)S(1)}, u32[]{:S(2)}, u32[]{:S(2)}) collective-permute-start(bf16[1024,768]{1,0:T(8,128)(2,1)S(1)} %shard_map.83), channel_id=1, source_target_pairs={{0,32},{32,0},{64,96},{96,64},{128,160},{160,128},{192,224},{224,1... | collective-permute-start | bytes 4718600 | tf_op jit(solution)/shard_map/ppermute | solution.py:296
  117.3 2.0 %shard_map.82.mine_ref = bf16[1024,768]{1,0:T(8,128)(2,1)S(1)} custom-call(s32[2]{0:T(128)S(1)} %pad_add_fusion.place_ref.refs_0_, bf16[768,2048]{1,0:T(8,128)(2,1)S(1)} %bitcast.15, bf16[768,768]{1,0:T(8,128)(2,1)S(1)} %copy-done.12), custom_call_target="tpu_custom_call" | custom-call | flops 2000000000 | bytes 5000000 | tf_op jit(solution)/shard_map/pallas_call | solution.py:347
  121.0 3.2 %collective-permute-start.9 = (bf16[128,768]{1,0:T(8,128)(2,1)S(1)}, bf16[128,768]{1,0:T(8,128)(2,1)S(1)}, u32[]{:S(2)}, u32[]{:S(2)}) collective-permute-start(bf16[128,768]{1,0:T(8,128)(2,1)S(1)} %get-tuple-element.22), channel_id=1, source_target_pairs={{0,64},{32,96},{64,128},{96,160},{128,192},{160,224},{192,256},{22... | collective-permute-start | bytes 589832 | tf_op jit(solution)/shard_map/ppermute | solution.py:293
  124.2 5.4 %collective-permute-start.10 = (bf16[128,768]{1,0:T(8,128)(2,1)S(1)}, bf16[128,768]{1,0:T(8,128)(2,1)S(1)}, u32[]{:S(2)}, u32[]{:S(2)}) collective-permute-start(bf16[128,768]{1,0:T(8,128)(2,1)S(1)} %get-tuple-element.23), channel_id=1, source_target_pairs={{0,128},{32,160},{64,192},{96,224},{128,256},{160,288},{192,320},{... | collective-permute-start | bytes 589832 | tf_op jit(solution)/shard_map/ppermute | solution.py:293
  129.7 2.5 %collective-permute-start.11 = (bf16[128,768]{1,0:T(8,128)(2,1)S(1)}, bf16[128,768]{1,0:T(8,128)(2,1)S(1)}, u32[]{:S(2)}, u32[]{:S(2)}) collective-permute-start(bf16[128,768]{1,0:T(8,128)(2,1)S(1)} %get-tuple-element.24), channel_id=1, source_target_pairs={{0,192},{32,224},{64,256},{96,288},{128,320},{160,352},{192,384},{... | collective-permute-start | bytes 589832 | tf_op jit(solution)/shard_map/ppermute | solution.py:293
  132.2 4.4 %collective-permute-start.12 = (bf16[128,768]{1,0:T(8,128)(2,1)S(1)}, bf16[128,768]{1,0:T(8,128)(2,1)S(1)}, u32[]{:S(2)}, u32[]{:S(2)}) collective-permute-start(bf16[128,768]{1,0:T(8,128)(2,1)S(1)} %get-tuple-element.25), channel_id=1, source_target_pairs={{0,256},{32,288},{64,320},{96,352},{128,384},{160,416},{192,448},{... | collective-permute-start | bytes 589832 | tf_op jit(solution)/shard_map/ppermute | solution.py:293
  136.7 3.6 %collective-permute-start.13 = (bf16[128,768]{1,0:T(8,128)(2,1)S(1)}, bf16[128,768]{1,0:T(8,128)(2,1)S(1)}, u32[]{:S(2)}, u32[]{:S(2)}) collective-permute-start(bf16[128,768]{1,0:T(8,128)(2,1)S(1)} %get-tuple-element.26), channel_id=1, source_target_pairs={{0,320},{32,352},{64,384},{96,416},{128,448},{160,480},{192,0},{22... | collective-permute-start | bytes 589832 | tf_op jit(solution)/shard_map/ppermute | solution.py:293
  140.3 4.2 %collective-permute-start.14 = (bf16[128,768]{1,0:T(8,128)(2,1)S(1)}, bf16[128,768]{1,0:T(8,128)(2,1)S(1)}, u32[]{:S(2)}, u32[]{:S(2)}) collective-permute-start(bf16[128,768]{1,0:T(8,128)(2,1)S(1)} %get-tuple-element.27), channel_id=1, source_target_pairs={{0,384},{32,416},{64,448},{96,480},{128,0},{160,32},{192,64},{224,... | collective-permute-start | bytes 589832 | tf_op jit(solution)/shard_map/ppermute | solution.py:293
  144.4 4.2 %collective-permute-start.15 = (bf16[128,768]{1,0:T(8,128)(2,1)S(1)}, bf16[128,768]{1,0:T(8,128)(2,1)S(1)}, u32[]{:S(2)}, u32[]{:S(2)}) collective-permute-start(bf16[128,768]{1,0:T(8,128)(2,1)S(1)} %get-tuple-element.28), channel_id=1, source_target_pairs={{0,448},{32,480},{64,0},{96,32},{128,64},{160,96},{192,128},{224,1... | collective-permute-start | bytes 589832 | tf_op jit(solution)/shard_map/ppermute | solution.py:293
  148.6 4.7 %collective-permute-done.11.refs_3_ = bf16[128,768]{1,0:T(8,128)(2,1)S(1)} collective-permute-done((bf16[128,768]{1,0:T(8,128)(2,1)S(1)}, bf16[128,768]{1,0:T(8,128)(2,1)S(1)}, u32[]{:S(2)}, u32[]{:S(2)}) %collective-permute-start.11) | collective-permute-done | bytes 196640 | tf_op jit(solution)/shard_map/ppermute | solution.py:293
  153.4 9.1 %collective-permute-done.13.refs_5_ = bf16[128,768]{1,0:T(8,128)(2,1)S(1)} collective-permute-done((bf16[128,768]{1,0:T(8,128)(2,1)S(1)}, bf16[128,768]{1,0:T(8,128)(2,1)S(1)}, u32[]{:S(2)}, u32[]{:S(2)}) %collective-permute-start.13) | collective-permute-done | bytes 196640 | tf_op jit(solution)/shard_map/ppermute | solution.py:293
  162.4 2.7 %collective-permute-done.14.refs_6_ = bf16[128,768]{1,0:T(8,128)(2,1)S(1)} collective-permute-done((bf16[128,768]{1,0:T(8,128)(2,1)S(1)}, bf16[128,768]{1,0:T(8,128)(2,1)S(1)}, u32[]{:S(2)}, u32[]{:S(2)}) %collective-permute-start.14) | collective-permute-done | bytes 196640 | tf_op jit(solution)/shard_map/ppermute | solution.py:293
  165.1 9.0 %collective-permute-done.15.refs_7_ = bf16[128,768]{1,0:T(8,128)(2,1)S(1)} collective-permute-done((bf16[128,768]{1,0:T(8,128)(2,1)S(1)}, bf16[128,768]{1,0:T(8,128)(2,1)S(1)}, u32[]{:S(2)}, u32[]{:S(2)}) %collective-permute-start.15) | collective-permute-done | bytes 196640 | tf_op jit(solution)/shard_map/ppermute | solution.py:293
  (41 shorter events, 16.0 us)
Async XLA Ops:
  4.9 13.1 %copy-start.8 = (bf16[1,128,384]{2,1,0:T(8,128)(2,1)S(1)}, bf16[1,128,384]{2,1,0:T(8,128)(2,1)}, u32[]{:S(2)}) copy-start(bf16[1,128,384]{2,1,0:T(8,128)(2,1)} %param.8) | copy-start | bytes 294916
  5.0 13.1 %copy-start.9 = (bf16[1,128,384]{2,1,0:T(8,128)(2,1)S(1)}, bf16[1,128,384]{2,1,0:T(8,128)(2,1)}, u32[]{:S(2)}) copy-start(bf16[1,128,384]{2,1,0:T(8,128)(2,1)} %param.9) | copy-start | bytes 294916
  5.0 13.1 %copy-start.10 = (s32[128,8]{0,1:T(8,128)S(1)}, s32[128,8]{0,1:T(8,128)}, u32[]{:S(2)}) copy-start(s32[128,8]{0,1:T(8,128)} %param.6) | copy-start | bytes 12292
  5.0 84.8 %all-to-all-start = ((bf16[32,24,2048]{2,1,0:T(8,128)(2,1)}), bf16[32,24,2048]{2,1,0:T(8,128)(2,1)S(1)}, u32[]{:S(2)}, u32[]{:S(2)}) async-start(bf16[32,24,2048]{2,1,0:T(8,128)(2,1)} %bitcast.21), calls=%async_computation | async-start | bytes 6291456 | tf_op jit(solution)/shard_map/all_to_all | solution.py:284
  18.5 0.9 copy-start.4
  19.4 19.8 %collective-permute-start.6 = (bf16[128,768]{1,0:T(8,128)(2,1)S(1)}, bf16[128,768]{1,0:T(8,128)(2,1)S(1)}, u32[]{:S(2)}, u32[]{:S(2)}) collective-permute-start(bf16[128,768]{1,0:T(8,128)(2,1)S(1)} %get-tuple-element.18.refs_0_), channel_id=1, source_target_pairs={{0,448},{32,480},{64,0},{96,32},{128,64},{160,96},{192,128},{224,1... | collective-permute-start | bytes 589832 | tf_op jit(solution)/shard_map/ppermute | solution.py:293
  21.5 22.0 %collective-permute-start.5 = (bf16[128,768]{1,0:T(8,128)(2,1)S(1)}, bf16[128,768]{1,0:T(8,128)(2,1)S(1)}, u32[]{:S(2)}, u32[]{:S(2)}) collective-permute-start(bf16[128,768]{1,0:T(8,128)(2,1)S(1)} %get-tuple-element.18.refs_0_), channel_id=1, source_target_pairs={{0,384},{32,416},{64,448},{96,480},{128,0},{160,32},{192,64},{224,... | collective-permute-start | bytes 589832 | tf_op jit(solution)/shard_map/ppermute | solution.py:293
  27.4 19.2 %collective-permute-start.4 = (bf16[128,768]{1,0:T(8,128)(2,1)S(1)}, bf16[128,768]{1,0:T(8,128)(2,1)}, u32[]{:S(2)}, u32[]{:S(2)}) collective-permute-start(bf16[128,768]{1,0:T(8,128)(2,1)S(1)} %get-tuple-element.18.refs_0_), channel_id=1, source_target_pairs={{0,320},{32,352},{64,384},{96,416},{128,448},{160,480},{192,0},{22... | collective-permute-start | bytes 589832 | tf_op jit(solution)/shard_map/ppermute | solution.py:293
  31.0 29.3 %collective-permute-start.3 = (bf16[128,768]{1,0:T(8,128)(2,1)S(1)}, bf16[128,768]{1,0:T(8,128)(2,1)}, u32[]{:S(2)}, u32[]{:S(2)}) collective-permute-start(bf16[128,768]{1,0:T(8,128)(2,1)S(1)} %get-tuple-element.18.refs_0_), channel_id=1, source_target_pairs={{0,256},{32,288},{64,320},{96,352},{128,384},{160,416},{192,448},{... | collective-permute-start | bytes 589832 | tf_op jit(solution)/shard_map/ppermute | solution.py:293
  35.8 24.5 %collective-permute-start.2 = (bf16[128,768]{1,0:T(8,128)(2,1)S(1)}, bf16[128,768]{1,0:T(8,128)(2,1)}, u32[]{:S(2)}, u32[]{:S(2)}) collective-permute-start(bf16[128,768]{1,0:T(8,128)(2,1)S(1)} %get-tuple-element.18.refs_0_), channel_id=1, source_target_pairs={{0,192},{32,224},{64,256},{96,288},{128,320},{160,352},{192,384},{... | collective-permute-start | bytes 589832 | tf_op jit(solution)/shard_map/ppermute | solution.py:293
  39.2 29.0 %collective-permute-start.1 = (bf16[128,768]{1,0:T(8,128)(2,1)S(1)}, bf16[128,768]{1,0:T(8,128)(2,1)}, u32[]{:S(2)}, u32[]{:S(2)}) collective-permute-start(bf16[128,768]{1,0:T(8,128)(2,1)S(1)} %get-tuple-element.18.refs_0_), channel_id=1, source_target_pairs={{0,128},{32,160},{64,192},{96,224},{128,256},{160,288},{192,320},{... | collective-permute-start | bytes 589832 | tf_op jit(solution)/shard_map/ppermute | solution.py:293
  43.5 0.7 copy-start.6
  44.1 26.6 %collective-permute-start = (bf16[128,768]{1,0:T(8,128)(2,1)S(1)}, bf16[128,768]{1,0:T(8,128)(2,1)}, u32[]{:S(2)}, u32[]{:S(2)}) collective-permute-start(bf16[128,768]{1,0:T(8,128)(2,1)S(1)} %get-tuple-element.18.refs_0_), channel_id=1, source_target_pairs={{0,64},{32,96},{64,128},{96,160},{128,192},{160,224},{192,256},{22... | collective-permute-start | bytes 589832 | tf_op jit(solution)/shard_map/ppermute | solution.py:293
  70.7 0.9 copy-start.7
  73.1 6.6 %collective-permute-start.7 = (bf16[1024,768]{1,0:T(8,128)(2,1)S(1)}, bf16[1024,768]{1,0:T(8,128)(2,1)S(1)}, u32[]{:S(2)}, u32[]{:S(2)}) collective-permute-start(bf16[1024,768]{1,0:T(8,128)(2,1)S(1)} %shard_map.78.refs_1_), channel_id=1, source_target_pairs={{0,32},{32,0},{64,96},{96,64},{128,160},{160,128},{192,224},{224,1... | collective-permute-start | bytes 4718600 | tf_op jit(solution)/shard_map/ppermute | solution.py:296
  80.4 1.7 copy-start.2
  89.7 9.7 %copy-start = (bf16[32,24,2048]{2,1,0:T(8,128)(2,1)}, bf16[32,24,2048]{2,1,0:T(8,128)(2,1)S(1)}, u32[]{:S(2)}) copy-start(bf16[32,24,2048]{2,1,0:T(8,128)(2,1)S(1)} %all-to-all-done) | copy-start | bytes 9437188
  99.4 1.5 copy-start.3
  100.9 1.0 copy-start.11
  101.9 73.1 %all-to-all-start.1 = ((bf16[32,40,1024]{2,1,0:T(8,128)(2,1)}), bf16[32,40,1024]{2,1,0:T(8,128)(2,1)S(1)}, u32[]{:S(2)}, u32[]{:S(2)}) async-start(bf16[32,40,1024]{2,1,0:T(8,128)(2,1)} %bitcast.16), calls=%async_computation.1 | async-start | bytes 5242880 | tf_op jit(solution)/shard_map/all_to_all | solution.py:284
  108.4 1.9 %copy-start.1 = (bf16[32,24,2048]{2,1,0:T(8,128)(2,1)S(1)}, bf16[32,24,2048]{2,1,0:T(8,128)(2,1)}, u32[]{:S(2)}) copy-start(bf16[32,24,2048]{2,1,0:T(8,128)(2,1)} %copy-done) | copy-start | bytes 9437188
  110.3 1.3 copy-start.12
  113.6 6.5 %collective-permute-start.8 = (bf16[1024,768]{1,0:T(8,128)(2,1)S(1)}, bf16[1024,768]{1,0:T(8,128)(2,1)S(1)}, u32[]{:S(2)}, u32[]{:S(2)}) collective-permute-start(bf16[1024,768]{1,0:T(8,128)(2,1)S(1)} %shard_map.83), channel_id=1, source_target_pairs={{0,32},{32,0},{64,96},{96,64},{128,160},{160,128},{192,224},{224,1... | collective-permute-start | bytes 4718600 | tf_op jit(solution)/shard_map/ppermute | solution.py:296
  121.0 19.2 %collective-permute-start.9 = (bf16[128,768]{1,0:T(8,128)(2,1)S(1)}, bf16[128,768]{1,0:T(8,128)(2,1)S(1)}, u32[]{:S(2)}, u32[]{:S(2)}) collective-permute-start(bf16[128,768]{1,0:T(8,128)(2,1)S(1)} %get-tuple-element.22), channel_id=1, source_target_pairs={{0,64},{32,96},{64,128},{96,160},{128,192},{160,224},{192,256},{22... | collective-permute-start | bytes 589832 | tf_op jit(solution)/shard_map/ppermute | solution.py:293
  124.2 20.2 %collective-permute-start.10 = (bf16[128,768]{1,0:T(8,128)(2,1)S(1)}, bf16[128,768]{1,0:T(8,128)(2,1)S(1)}, u32[]{:S(2)}, u32[]{:S(2)}) collective-permute-start(bf16[128,768]{1,0:T(8,128)(2,1)S(1)} %get-tuple-element.23), channel_id=1, source_target_pairs={{0,128},{32,160},{64,192},{96,224},{128,256},{160,288},{192,320},{... | collective-permute-start | bytes 589832 | tf_op jit(solution)/shard_map/ppermute | solution.py:293
  129.7 23.7 %collective-permute-start.11 = (bf16[128,768]{1,0:T(8,128)(2,1)S(1)}, bf16[128,768]{1,0:T(8,128)(2,1)S(1)}, u32[]{:S(2)}, u32[]{:S(2)}) collective-permute-start(bf16[128,768]{1,0:T(8,128)(2,1)S(1)} %get-tuple-element.24), channel_id=1, source_target_pairs={{0,192},{32,224},{64,256},{96,288},{128,320},{160,352},{192,384},{... | collective-permute-start | bytes 589832 | tf_op jit(solution)/shard_map/ppermute | solution.py:293
  132.2 21.1 %collective-permute-start.12 = (bf16[128,768]{1,0:T(8,128)(2,1)S(1)}, bf16[128,768]{1,0:T(8,128)(2,1)S(1)}, u32[]{:S(2)}, u32[]{:S(2)}) collective-permute-start(bf16[128,768]{1,0:T(8,128)(2,1)S(1)} %get-tuple-element.25), channel_id=1, source_target_pairs={{0,256},{32,288},{64,320},{96,352},{128,384},{160,416},{192,448},{... | collective-permute-start | bytes 589832 | tf_op jit(solution)/shard_map/ppermute | solution.py:293
  136.7 25.8 %collective-permute-start.13 = (bf16[128,768]{1,0:T(8,128)(2,1)S(1)}, bf16[128,768]{1,0:T(8,128)(2,1)S(1)}, u32[]{:S(2)}, u32[]{:S(2)}) collective-permute-start(bf16[128,768]{1,0:T(8,128)(2,1)S(1)} %get-tuple-element.26), channel_id=1, source_target_pairs={{0,320},{32,352},{64,384},{96,416},{128,448},{160,480},{192,0},{22... | collective-permute-start | bytes 589832 | tf_op jit(solution)/shard_map/ppermute | solution.py:293
  140.3 24.8 %collective-permute-start.14 = (bf16[128,768]{1,0:T(8,128)(2,1)S(1)}, bf16[128,768]{1,0:T(8,128)(2,1)S(1)}, u32[]{:S(2)}, u32[]{:S(2)}) collective-permute-start(bf16[128,768]{1,0:T(8,128)(2,1)S(1)} %get-tuple-element.27), channel_id=1, source_target_pairs={{0,384},{32,416},{64,448},{96,480},{128,0},{160,32},{192,64},{224,... | collective-permute-start | bytes 589832 | tf_op jit(solution)/shard_map/ppermute | solution.py:293
  144.4 29.7 %collective-permute-start.15 = (bf16[128,768]{1,0:T(8,128)(2,1)S(1)}, bf16[128,768]{1,0:T(8,128)(2,1)S(1)}, u32[]{:S(2)}, u32[]{:S(2)}) collective-permute-start(bf16[128,768]{1,0:T(8,128)(2,1)S(1)} %get-tuple-element.28), channel_id=1, source_target_pairs={{0,448},{32,480},{64,0},{96,32},{128,64},{160,96},{192,128},{224,1... | collective-permute-start | bytes 589832 | tf_op jit(solution)/shard_map/ppermute | solution.py:293
  175.0 1.1 copy-start.5

commit v3 on v2

--- a/solution.py
+++ b/solution.py
@@ -15,7 +15,7 @@
 FETCHES = 4
 VMEM = 32 * 2**20
 BIG = 60 * 2**20
-MIDDLE = 46 * 2**20
+MIDDLE = 32 * 2**20
 
 
 def iota(shape, axis):
@@ -59,7 +59,13 @@
     return one_if((row >= first) & (row < first + rows))
 
 
-def pack_kernel(experts, routes_ref, tokens_ref, cot_ref, out_ref, held, sems):
+def pack_kernel(experts, routes_ref, tokens_hbm, cot_hbm, out_ref, held, sems, tokens_ref, cot_ref, in_sems):
+    fetches = (
+        pltpu.make_async_copy(tokens_hbm, tokens_ref, in_sems.at[0]),
+        pltpu.make_async_copy(cot_hbm, cot_ref, in_sems.at[1]),
+    )
+    for fetch in fetches:
+        fetch.start()
     routes = routes_ref[...]
     top, count = routes.shape
     width = tokens_ref.shape[1]
@@ -79,6 +85,8 @@
     )
     slot_at = dot(repeat_rows(experts, TAIL), slot_place.astype(jnp.bfloat16))
     offset = slot_at - (iota(slot_at.shape, 0) & (TAIL - 1)).astype(jnp.float32)
+    for fetch in fetches:
+        fetch.wait()
     cot = cot_ref[...]
     copies = []
     for i in range(PER_ROW + 1):
@@ -101,9 +109,13 @@
         copy.wait()
 
 
-def prepare_kernel(experts, routes_ref, gate_ref, up_ref, out_ref, stacked_ref):
+def stack_kernel(gate_ref, up_ref, stacked_ref):
+    stacked_ref[...] = jnp.concatenate((gate_ref[...], up_ref[...]), axis=1)
+
+
+def combine_kernel(experts, routes_ref, returned_ref, out_ref):
     _, place = ranks(routes_ref[...], experts)
-    count = place.shape[1]
+    half = returned_ref.shape[1]
     lane = iota((experts, experts * BACK), 1)
     first = iota((experts, experts * BACK), 0) * BACK
     mine = (lane >= first) & (lane < first + BACK)
@@ -112,35 +124,36 @@
     low = jnp.where(within < CAP, within, -2.0)
     high = jnp.where(within < BLOCK, within - TAIL, within - BLOCK)
     high = jnp.where(within < CAP, -2.0, high)
-    out_ref[:count] = one_if(at == low)
-    out_ref[count:] = one_if(at == high)
-    stacked_ref[...] = jnp.concatenate((gate_ref[...], up_ref[...]), axis=1)
-
-
-def middle_kernel(received_ref, source_ref, delta_ref, back_ref, held, sems, weight_ref, weight_sems):
+    returned = returned_ref[...]
+    out_ref[:, :half] = dot(one_if(at == low), returned).astype(jnp.bfloat16)
+    out_ref[:, half:] = dot(one_if(at == high), returned).astype(jnp.bfloat16)
+
+
+def middle_kernel(
+    received_ref, weight_hbm, delta_hbm, back_hbm, weight_ref, in_sems, delta_ref, delta_sems, held, sems, pre_ref
+):
     rows = received_ref.shape[0] // STEPS
     width = received_ref.shape[1]
     hidden = weight_ref.shape[1] // 2
     blocks = rows // BLOCK
     half = width // 2
     full = BLOCK - 8
-    copies = []
     depth = width // FETCHES
-    fetches = []
+    fetches, copies = [], []
     for k in range(FETCHES):
         at = pl.ds(k * depth, depth)
-        fetch = pltpu.make_async_copy(source_ref.at[at], weight_ref.at[at], weight_sems.at[k])
+        fetch = pltpu.make_async_copy(weight_hbm.at[at], weight_ref.at[at], in_sems.at[k])
         fetch.start()
         fetches.append(fetch)
+    for k, fetch in enumerate(fetches):
+        fetch.wait()
+        at = slice(k * depth, (k + 1) * depth)
+        pre = dot(received_ref[:, at], weight_ref[at])
+        pre_ref[...] = pre if k == 0 else pre_ref[...] + pre
     for step in range(STEPS):
         part = slice(step * rows, (step + 1) * rows)
         received = received_ref[part]
-        pre = jnp.zeros((rows, 2 * hidden), jnp.float32)
-        for k, fetch in enumerate(fetches):
-            if step == 0:
-                fetch.wait()
-            at = slice(k * depth, (k + 1) * depth)
-            pre += dot(received[:, at], weight_ref[at])
+        pre = pre_ref[part]
         gate_pre, up_pre = pre[:, :hidden], pre[:, hidden:]
         tail = received.astype(jnp.float32).reshape(blocks, BLOCK, width)[:, full:]
         first = iota((blocks, 8, hidden), 1) < TAIL
@@ -161,6 +174,10 @@
         up_delta = grad_out * gate_pre * sigmoid_gate
         delta = jnp.concatenate((gate_delta, up_delta), axis=1)
         delta_ref[part] = delta.astype(jnp.bfloat16)
+        at = pl.ds(step * rows, rows)
+        copy = pltpu.make_async_copy(delta_ref.at[at], delta_hbm.at[at], delta_sems.at[step])
+        copy.start()
+        copies.append(copy)
         delta = delta.reshape(blocks, BLOCK, 2 * hidden)
         last = delta[:, full:]
         last = jnp.where(iota(last.shape, 1) < TAIL, last, pltpu.roll(last, TAIL, 1))
@@ -173,19 +190,11 @@
         size = blocks * BACK
         held[step * size : (step + 1) * size] = back.reshape(size, half).astype(jnp.bfloat16)
         at = pl.ds(step * size, size)
-        copy = pltpu.make_async_copy(held.at[at], back_ref.at[at], sems.at[step])
+        copy = pltpu.make_async_copy(held.at[at], back_hbm.at[at], sems.at[step])
         copy.start()
         copies.append(copy)
     for copy in copies:
         copy.wait()
-
-
-def combine_kernel(matrix_ref, returned_ref, out_ref):
-    count = out_ref.shape[0]
-    half = returned_ref.shape[1]
-    returned = returned_ref[...]
-    out_ref[:, :half] = dot(matrix_ref[:count], returned).astype(jnp.bfloat16)
-    out_ref[:, half:] = dot(matrix_ref[count:], returned).astype(jnp.bfloat16)
 
 
 def aligned(index, size):
@@ -220,31 +229,48 @@
         out_ref[first * share : (first + batch) * share] = grad.astype(jnp.bfloat16)
 
 
-def add_kernel(place_ref, mine_ref, other_ref, *out_refs):
-    size = out_refs[0].shape[0]
-    for k, out_ref in enumerate(out_refs):
-        at = aligned(lax.rem(place_ref[0] + k, len(out_refs)), size)
-        total = mine_ref[at].astype(jnp.float32) + other_ref[at].astype(jnp.float32)
+def place_back(place_ref, k, count):
+    return lax.rem(place_ref[0] + k + count, count)
+
+
+def add_kernel(place_ref, mine_ref, other_ref, sum_ref, up_ref, down_ref):
+    total = mine_ref[...].astype(jnp.float32) + other_ref[...].astype(jnp.float32)
+    sum_ref[...] = total.astype(jnp.bfloat16)
+    size = up_ref.shape[0]
+    ys = sum_ref.shape[0] // size
+    up_ref[...] = sum_ref[aligned(place_back(place_ref, ys // 2, ys), size)]
+    down_ref[...] = sum_ref[aligned(place_back(place_ref, 1 - ys // 2, ys), size)]
+
+
+def pass_kernel(ks, place_ref, sum_ref, *refs):
+    size = refs[0].shape[0]
+    ys = sum_ref.shape[0] // size
+    for k, arrived_ref, out_ref in zip(ks, refs[: len(ks)], refs[len(ks) :]):
+        own = sum_ref[aligned(place_back(place_ref, k, ys), size)]
+        total = arrived_ref[...].astype(jnp.float32) + own.astype(jnp.float32)
         out_ref[...] = total.astype(jnp.bfloat16)
 
 
-def total_kernel(groups, *refs):
-    *terms, gate_ref, up_ref = refs
-    hidden = gate_ref.shape[1]
-    total = terms[0][...].astype(jnp.float32)
-    for term in terms[1:]:
-        total += term[...].astype(jnp.float32)
+def total_kernel(groups, place_ref, sum_ref, up_ref, down_ref, gate_grad_ref, up_grad_ref):
+    hidden = gate_grad_ref.shape[1]
+    total = sum_ref[aligned(place_ref[0], up_ref.shape[0])].astype(jnp.float32)
+    total += up_ref[...].astype(jnp.float32)
+    total += down_ref[...].astype(jnp.float32)
     total *= 1.0 / groups
-    gate_ref[...] = total[:, :hidden]
-    up_ref[...] = total[:, hidden:]
+    gate_grad_ref[...] = total[:, :hidden]
+    up_grad_ref[...] = total[:, hidden:]
 
 
 def whole():
     return pl.BlockSpec(memory_space=pltpu.VMEM)
 
 
-def in_hbm():
-    return pl.BlockSpec(memory_space=pltpu.HBM)
+def anywhere():
+    return pl.BlockSpec(memory_space=pl.ANY)
+
+
+def hbm(array):
+    return pltpu.with_memory_space_constraint(array, pltpu.HBM)
 
 
 def call(kernel, out_shape, flops, moved, vmem=VMEM, **more):
@@ -297,23 +323,27 @@
 
     packed = call(
         lambda *refs: pack_kernel(peers, *refs),
-        shape(rows, width),
+        pltpu.HBM((rows, width), bf16),
         2 * 10**9,
         5 * 10**6,
         BIG,
-        in_specs=[whole()] * 3,
-        out_specs=in_hbm(),
-        scratch_shapes=held_and_sems((rows, width), PER_ROW + 1),
-    )(routes, tokens, cotangent.reshape(count * top, hidden))
+        in_specs=[whole(), anywhere(), anywhere()],
+        out_specs=anywhere(),
+        scratch_shapes=[
+            *held_and_sems((rows, width), PER_ROW + 1),
+            pltpu.VMEM((count, width), bf16),
+            *held_and_sems((count * top, hidden), 2),
+        ],
+    )(routes, hbm(tokens), hbm(cotangent.reshape(count * top, hidden)))
     received = exchange(packed, BLOCK)
-    matrix, stacked = call(
-        lambda *refs: prepare_kernel(peers, *refs),
-        (shape(2 * count, peers * BACK), shape(share, 2 * hidden)),
+    stacked = call(
+        stack_kernel,
+        shape(share, 2 * hidden),
         2 * 10**9,
         10**6,
-        in_specs=[whole()] * 3,
-        out_specs=(whole(), whole()),
-    )(routes, gate_weight[0], up_weight[0])
+        in_specs=[whole()] * 2,
+        out_specs=whole(),
+    )(gate_weight[0], up_weight[0])
     blocks = [stacked] + [along_y(stacked, k) for k in range(1, ys)]
     of_core = call(
         collect_kernel,
@@ -333,15 +363,19 @@
     )(place, of_core, other_core(of_core))
     delta, back = call(
         middle_kernel,
-        (shape(rows, 2 * hidden), shape(peers * BACK, half)),
+        (pltpu.HBM((rows, 2 * hidden), bf16), pltpu.HBM((peers * BACK, half), bf16)),
         5 * 10**9,
         10**7,
         MIDDLE,
-        in_specs=[whole(), pl.BlockSpec(memory_space=pl.ANY)],
-        out_specs=(whole(), in_hbm()),
-        scratch_shapes=held_and_sems((peers * BACK, half), STEPS)
-        + held_and_sems((width, 2 * hidden), FETCHES),
-    )(received, weight)
+        in_specs=[whole(), anywhere()],
+        out_specs=(anywhere(), anywhere()),
+        scratch_shapes=[
+            *held_and_sems((width, 2 * hidden), FETCHES),
+            *held_and_sems((rows, 2 * hidden), STEPS),
+            *held_and_sems((peers * BACK, half), STEPS),
+            pltpu.VMEM((rows, 2 * hidden), jnp.float32),
+        ],
+    )(received, hbm(weight))
     returned = exchange(back, BACK)
     grads = [
         call(
@@ -354,32 +388,51 @@
         )(place, received, delta)
         for other in (True, False)
     ]
-    sums = call(
+    block = shape(share, 2 * hidden)
+    summed, up, down = call(
         add_kernel,
-        (shape(share, 2 * hidden),) * ys,
+        (shape(ys * share, 2 * hidden), block, block),
         10**6,
         5 * 10**6,
         in_specs=[scalars] + [whole()] * 2,
-        out_specs=(whole(),) * ys,
+        out_specs=(whole(),) * 3,
     )(place, grads[1], other_core(grads[0]))
-    terms = [sums[0]] + [along_y(sums[k], k) for k in range(1, ys)]
+    for hop in range(1, ys // 2 + 1):
+        up = along_y(up, 1)
+        travelling, ks = (up,), (ys // 2 - hop,)
+        if hop < ys // 2:
+            down = along_y(down, -1)
+            travelling, ks = (up, down), (ks[0], hop + 1 - ys // 2)
+        if hop == ys // 2:
+            break
+        if hop == ys // 2 - 1:
+            travelling, ks = travelling[:1], ks[:1]
+        out = call(
+            lambda *refs, ks=ks: pass_kernel(ks, *refs),
+            (block,) * len(ks),
+            10**5,
+            10**6,
+            in_specs=[scalars] + [whole()] * (1 + len(ks)),
+            out_specs=(whole(),) * len(ks),
+        )(place, summed, *travelling)
+        up, down = out[0], out[1] if len(ks) == 2 else down
     weight_shape = shape(share, hidden, kind=jnp.float32)
     gate_grad, up_grad = call(
         lambda *refs: total_kernel(groups, *refs),
         (weight_shape, weight_shape),
         10**6,
         2 * 10**6,
-        in_specs=[whole()] * ys,
+        in_specs=[scalars] + [whole()] * 3,
         out_specs=(whole(), whole()),
-    )(*terms)
+    )(place, summed, up, down)
     token_grad = call(
-        combine_kernel,
+        lambda *refs: combine_kernel(peers, *refs),
         shape(count, width),
         10**9,
         4 * 10**6,
         in_specs=[whole()] * 2,
         out_specs=whole(),
-    )(matrix, returned)
+    )(routes, returned)
     return (token_grad, gate_grad[None], up_grad[None])
 
 

time: 179 us -> 173 us (0.966)
  the two profiles are of different devices: /device:TPU:11 before, /device:TPU:45 now
where the time goes in v3:
time: 173 us; the launch traced here: 172 us
  starting transfers between devices  68.7 us (40%)
  waiting for transfers between devices  68.6 us (40%)
  Pallas kernels  28.9 us (17%)
  local copies, waits for them, and re-layouts  4.56 us (3%)
    ppermute x14, starting transfers between devices, along_y(): return lax.ppermute(block, 'dp', pairs)  42.9 us
    ppermute x14, waiting for transfers between devices, along_y(): return lax.ppermute(block, 'dp', pairs)  40.4 us
    all_to_all x2, waiting for transfers between devices, exchange(): lax.all_to_all(block.reshape(peers, size, -1), 'expert', split_axis=0, co...  24.3 us
    all_to_all x2, starting transfers between devices, exchange(): lax.all_to_all(block.reshape(peers, size, -1), 'expert', split_axis=0, co...  19.5 us
    pallas_call x1, Pallas kernels, on_device(): call(middle_kernel, (pltpu.HBM((rows, 2 * hidden), bf16), pltpu.HBM((peer...  9.83 us
    ppermute x2, starting transfers between devices, other_core(): return lax.ppermute(block, 'dp', [(d, d ^ 1) for d in range(groups)])  6.24 us
    pallas_call x1, Pallas kernels, on_device(): call(lambda *refs: pack_kernel(peers, *refs), pltpu.HBM((rows, width), bf...  4.62 us
    unnamed x16, local copies, waits for them, and re-layouts  4.56 us
  transfers between devices with their start and end apart: 18, of which 14 were waited for; matrix products, arithmetic and copies ran while one was open for 0% of the time, Pallas kernels for 6%

profile of v3, /device:TPU:45, one launch (start us, length us, event | category | flops | bytes accessed | tf_op | source)
XLA Modules:
  0.0 171.7 jit_solution(10060977847158578808)
XLA Ops:
  0.6 4.6 %shard_map.76 = bf16[768,2048]{1,0:T(8,128)(2,1)} custom-call(s32[8,128]{1,0:T(8,128)} %bitcast.17, bf16[128,2048]{1,0:T(8,128)(2,1)} %refs_1_.1, bf16[1024,384]{1,0:T(8,128)(2,1)} %bitcast.21), custom_call_target="tpu_custom_call" | custom-call | flops 2000000000 | bytes 5000000 | tf_op jit(solution)/shard_map/pallas_call | solution.py:324
  5.3 13.0 %all-to-all-start = ((bf16[32,24,2048]{2,1,0:T(8,128)(2,1)}), bf16[32,24,2048]{2,1,0:T(8,128)(2,1)S(1)}, u32[]{:S(2)}, u32[]{:S(2)}) async-start(bf16[32,24,2048]{2,1,0:T(8,128)(2,1)} %bitcast.19), calls=%async_computation | async-start | bytes 6291456 | tf_op jit(solution)/shard_map/all_to_all | solution.py:310
  18.4 3.0 %collective-permute-start.6 = (bf16[128,768]{1,0:T(8,128)(2,1)S(1)}, bf16[128,768]{1,0:T(8,128)(2,1)S(1)}, u32[]{:S(2)}, u32[]{:S(2)}) collective-permute-start(bf16[128,768]{1,0:T(8,128)(2,1)S(1)} %shard_map.77.refs_0_), channel_id=1, source_target_pairs={{0,448},{32,480},{64,0},{96,32},{128,64},{160,96},{192,128},{224,1... | collective-permute-start | bytes 589832 | tf_op jit(solution)/shard_map/ppermute | solution.py:319
  21.3 2.0 %collective-permute-start.5 = (bf16[128,768]{1,0:T(8,128)(2,1)S(1)}, bf16[128,768]{1,0:T(8,128)(2,1)S(1)}, u32[]{:S(2)}, u32[]{:S(2)}) collective-permute-start(bf16[128,768]{1,0:T(8,128)(2,1)S(1)} %shard_map.77.refs_0_), channel_id=1, source_target_pairs={{0,384},{32,416},{64,448},{96,480},{128,0},{160,32},{192,64},{224,... | collective-permute-start | bytes 589832 | tf_op jit(solution)/shard_map/ppermute | solution.py:319
  23.3 4.9 %collective-permute-start.4 = (bf16[128,768]{1,0:T(8,128)(2,1)S(1)}, bf16[128,768]{1,0:T(8,128)(2,1)}, u32[]{:S(2)}, u32[]{:S(2)}) collective-permute-start(bf16[128,768]{1,0:T(8,128)(2,1)S(1)} %shard_map.77.refs_0_), channel_id=1, source_target_pairs={{0,320},{32,352},{64,384},{96,416},{128,448},{160,480},{192,0},{22... | collective-permute-start | bytes 589832 | tf_op jit(solution)/shard_map/ppermute | solution.py:319
  28.2 4.4 %collective-permute-start.3 = (bf16[128,768]{1,0:T(8,128)(2,1)S(1)}, bf16[128,768]{1,0:T(8,128)(2,1)}, u32[]{:S(2)}, u32[]{:S(2)}) collective-permute-start(bf16[128,768]{1,0:T(8,128)(2,1)S(1)} %shard_map.77.refs_0_), channel_id=1, source_target_pairs={{0,256},{32,288},{64,320},{96,352},{128,384},{160,416},{192,448},{... | collective-permute-start | bytes 589832 | tf_op jit(solution)/shard_map/ppermute | solution.py:319
  32.6 4.6 %collective-permute-start.2 = (bf16[128,768]{1,0:T(8,128)(2,1)S(1)}, bf16[128,768]{1,0:T(8,128)(2,1)}, u32[]{:S(2)}, u32[]{:S(2)}) collective-permute-start(bf16[128,768]{1,0:T(8,128)(2,1)S(1)} %shard_map.77.refs_0_), channel_id=1, source_target_pairs={{0,192},{32,224},{64,256},{96,288},{128,320},{160,352},{192,384},{... | collective-permute-start | bytes 589832 | tf_op jit(solution)/shard_map/ppermute | solution.py:319
  39.9 2.3 %collective-permute-start = (bf16[128,768]{1,0:T(8,128)(2,1)S(1)}, bf16[128,768]{1,0:T(8,128)(2,1)}, u32[]{:S(2)}, u32[]{:S(2)}) collective-permute-start(bf16[128,768]{1,0:T(8,128)(2,1)S(1)} %shard_map.77.refs_0_), channel_id=1, source_target_pairs={{0,64},{32,96},{64,128},{96,160},{128,192},{160,224},{192,256},{22... | collective-permute-start | bytes 589832 | tf_op jit(solution)/shard_map/ppermute | solution.py:319
  42.3 5.5 %collective-permute-done.4.refs_5_ = bf16[128,768]{1,0:T(8,128)(2,1)} collective-permute-done((bf16[128,768]{1,0:T(8,128)(2,1)S(1)}, bf16[128,768]{1,0:T(8,128)(2,1)}, u32[]{:S(2)}, u32[]{:S(2)}) %collective-permute-start.4) | collective-permute-done | bytes 196640 | tf_op jit(solution)/shard_map/ppermute | solution.py:319
  47.8 9.2 %collective-permute-done.3.refs_4_ = bf16[128,768]{1,0:T(8,128)(2,1)} collective-permute-done((bf16[128,768]{1,0:T(8,128)(2,1)S(1)}, bf16[128,768]{1,0:T(8,128)(2,1)}, u32[]{:S(2)}, u32[]{:S(2)}) %collective-permute-start.3) | collective-permute-done | bytes 196640 | tf_op jit(solution)/shard_map/ppermute | solution.py:319
  57.0 6.8 %collective-permute-done.1.refs_2_ = bf16[128,768]{1,0:T(8,128)(2,1)} collective-permute-done((bf16[128,768]{1,0:T(8,128)(2,1)S(1)}, bf16[128,768]{1,0:T(8,128)(2,1)}, u32[]{:S(2)}, u32[]{:S(2)}) %collective-permute-start.1) | collective-permute-done | bytes 196640 | tf_op jit(solution)/shard_map/ppermute | solution.py:319
  63.8 3.7 %collective-permute-done.refs_1_ = bf16[128,768]{1,0:T(8,128)(2,1)} collective-permute-done((bf16[128,768]{1,0:T(8,128)(2,1)S(1)}, bf16[128,768]{1,0:T(8,128)(2,1)}, u32[]{:S(2)}, u32[]{:S(2)}) %collective-permute-start) | collective-permute-done | bytes 196640 | tf_op jit(solution)/shard_map/ppermute | solution.py:319
  69.9 2.5 %collective-permute-start.7 = (bf16[1024,768]{1,0:T(8,128)(2,1)S(1)}, bf16[1024,768]{1,0:T(8,128)(2,1)S(1)}, u32[]{:S(2)}, u32[]{:S(2)}) collective-permute-start(bf16[1024,768]{1,0:T(8,128)(2,1)S(1)} %shard_map.78.refs_1_), channel_id=1, source_target_pairs={{0,32},{32,0},{64,96},{96,64},{128,160},{160,128},{192,224},{224,1... | collective-permute-start | bytes 4718600 | tf_op jit(solution)/shard_map/ppermute | solution.py:322
  72.4 3.0 %collective-permute-done.7.refs_2_ = bf16[1024,768]{1,0:T(8,128)(2,1)S(1)} collective-permute-done((bf16[1024,768]{1,0:T(8,128)(2,1)S(1)}, bf16[1024,768]{1,0:T(8,128)(2,1)S(1)}, u32[]{:S(2)}, u32[]{:S(2)}) %collective-permute-start.7) | collective-permute-done | bytes 1572896 | tf_op jit(solution)/shard_map/ppermute | solution.py:322
  77.9 12.2 %all-to-all-done = bf16[32,24,2048]{2,1,0:T(8,128)(2,1)S(1)} async-done(((bf16[32,24,2048]{2,1,0:T(8,128)(2,1)}), bf16[32,24,2048]{2,1,0:T(8,128)(2,1)S(1)}, u32[]{:S(2)}, u32[]{:S(2)}) %all-to-all-start) | async-done | bytes 3145760 | tf_op jit(solution)/shard_map/all_to_all | solution.py:310
  90.1 9.8 %shard_map.80 = (bf16[768,768]{1,0:T(8,128)(2,1)}, bf16[1280,1024]{1,0:T(8,128)(2,1)}) custom-call(bf16[768,2048]{1,0:T(8,128)(2,1)S(1)} %bitcast.12, bf16[2048,768]{1,0:T(8,128)(2,1)} %copy-done), custom_call_target="tpu_custom_call" | custom-call | flops 5000000000 | bytes 10000000 | tf_op jit(solution)/shard_map/pallas_call | solution.py:364
  100.0 6.5 %all-to-all-start.1 = ((bf16[32,40,1024]{2,1,0:T(8,128)(2,1)}), bf16[32,40,1024]{2,1,0:T(8,128)(2,1)}, u32[]{:S(2)}, u32[]{:S(2)}) async-start(bf16[32,40,1024]{2,1,0:T(8,128)(2,1)} %bitcast.20), calls=%async_computation.1 | async-start | bytes 5242880 | tf_op jit(solution)/shard_map/all_to_all | solution.py:310
  109.7 3.7 %collective-permute-start.8 = (bf16[1024,768]{1,0:T(8,128)(2,1)S(1)}, bf16[1024,768]{1,0:T(8,128)(2,1)S(1)}, u32[]{:S(2)}, u32[]{:S(2)}) collective-permute-start(bf16[1024,768]{1,0:T(8,128)(2,1)S(1)} %shard_map.83), channel_id=1, source_target_pairs={{0,32},{32,0},{64,96},{96,64},{128,160},{160,128},{192,224},{224,1... | collective-permute-start | bytes 4718600 | tf_op jit(solution)/shard_map/ppermute | solution.py:322
  113.4 2.0 %shard_map.82.mine_ref = bf16[1024,768]{1,0:T(8,128)(2,1)S(1)} custom-call(s32[2]{0:T(128)S(1)} %pad_add_fusion.place_ref.refs_0_, bf16[768,2048]{1,0:T(8,128)(2,1)S(1)} %bitcast.14, bf16[768,768]{1,0:T(8,128)(2,1)S(1)} %copy-done.7), custom_call_target="tpu_custom_call" | custom-call | flops 2000000000 | bytes 5000000 | tf_op jit(solution)/shard_map/pallas_call | solution.py:381
  117.6 2.3 %collective-permute-start.9 = (bf16[128,768]{1,0:T(8,128)(2,1)S(1)}, bf16[128,768]{1,0:T(8,128)(2,1)S(1)}, u32[]{:S(2)}, u32[]{:S(2)}) collective-permute-start(bf16[128,768]{1,0:T(8,128)(2,1)S(1)} %get-tuple-element.17), channel_id=1, source_target_pairs={{0,64},{32,96},{64,128},{96,160},{128,192},{160,224},{192,256},{22... | collective-permute-start | bytes 589832 | tf_op jit(solution)/shard_map/ppermute | solution.py:319
  119.9 3.0 %collective-permute-start.10 = (bf16[128,768]{1,0:T(8,128)(2,1)S(1)}, bf16[128,768]{1,0:T(8,128)(2,1)S(1)}, u32[]{:S(2)}, u32[]{:S(2)}) collective-permute-start(bf16[128,768]{1,0:T(8,128)(2,1)S(1)} %get-tuple-element.18), channel_id=1, source_target_pairs={{0,448},{32,480},{64,0},{96,32},{128,64},{160,96},{192,128},{224,1... | collective-permute-start | bytes 589832 | tf_op jit(solution)/shard_map/ppermute | solution.py:319
  122.9 2.8 %collective-permute-done.9.refs_2_ = bf16[128,768]{1,0:T(8,128)(2,1)S(1)} collective-permute-done((bf16[128,768]{1,0:T(8,128)(2,1)S(1)}, bf16[128,768]{1,0:T(8,128)(2,1)S(1)}, u32[]{:S(2)}, u32[]{:S(2)}) %collective-permute-start.9) | collective-permute-done | bytes 196640 | tf_op jit(solution)/shard_map/ppermute | solution.py:319
  125.7 2.0 %collective-permute-done.10.refs_3_ = bf16[128,768]{1,0:T(8,128)(2,1)S(1)} collective-permute-done((bf16[128,768]{1,0:T(8,128)(2,1)S(1)}, bf16[128,768]{1,0:T(8,128)(2,1)S(1)}, u32[]{:S(2)}, u32[]{:S(2)}) %collective-permute-start.10) | collective-permute-done | bytes 196640 | tf_op jit(solution)/shard_map/ppermute | solution.py:319
  128.4 2.3 %collective-permute-start.11 = (bf16[128,768]{1,0:T(8,128)(2,1)S(1)}, bf16[128,768]{1,0:T(8,128)(2,1)S(1)}, u32[]{:S(2)}, u32[]{:S(2)}) collective-permute-start(bf16[128,768]{1,0:T(8,128)(2,1)S(1)} %get-tuple-element.19), channel_id=1, source_target_pairs={{0,64},{32,96},{64,128},{96,160},{128,192},{160,224},{192,256},{22... | collective-permute-start | bytes 589832 | tf_op jit(solution)/shard_map/ppermute | solution.py:319
  130.7 3.0 %collective-permute-start.12 = (bf16[128,768]{1,0:T(8,128)(2,1)S(1)}, bf16[128,768]{1,0:T(8,128)(2,1)S(1)}, u32[]{:S(2)}, u32[]{:S(2)}) collective-permute-start(bf16[128,768]{1,0:T(8,128)(2,1)S(1)} %get-tuple-element.20), channel_id=1, source_target_pairs={{0,448},{32,480},{64,0},{96,32},{128,64},{160,96},{192,128},{224,1... | collective-permute-start | bytes 589832 | tf_op jit(solution)/shard_map/ppermute | solution.py:319
  135.4 2.2 %collective-permute-done.12.refs_3_ = bf16[128,768]{1,0:T(8,128)(2,1)S(1)} collective-permute-done((bf16[128,768]{1,0:T(8,128)(2,1)S(1)}, bf16[128,768]{1,0:T(8,128)(2,1)S(1)}, u32[]{:S(2)}, u32[]{:S(2)}) %collective-permute-start.12) | collective-permute-done | bytes 196640 | tf_op jit(solution)/shard_map/ppermute | solution.py:319
  138.2 3.6 %collective-permute-start.13 = (bf16[128,768]{1,0:T(8,128)(2,1)S(1)}, bf16[128,768]{1,0:T(8,128)(2,1)S(1)}, u32[]{:S(2)}, u32[]{:S(2)}) collective-permute-start(bf16[128,768]{1,0:T(8,128)(2,1)S(1)} %get-tuple-element.21), channel_id=1, source_target_pairs={{0,64},{32,96},{64,128},{96,160},{128,192},{160,224},{192,256},{22... | collective-permute-start | bytes 589832 | tf_op jit(solution)/shard_map/ppermute | solution.py:319
  141.8 2.0 %collective-permute-start.15 = (bf16[128,768]{1,0:T(8,128)(2,1)S(1)}, bf16[128,768]{1,0:T(8,128)(2,1)S(1)}, u32[]{:S(2)}, u32[]{:S(2)}) collective-permute-start(bf16[128,768]{1,0:T(8,128)(2,1)S(1)} %get-tuple-element.22), channel_id=1, source_target_pairs={{0,448},{32,480},{64,0},{96,32},{128,64},{160,96},{192,128},{224,1... | collective-permute-start | bytes 589832 | tf_op jit(solution)/shard_map/ppermute | solution.py:319
  145.6 3.6 %collective-permute-start.14 = (bf16[128,768]{1,0:T(8,128)(2,1)S(1)}, bf16[128,768]{1,0:T(8,128)(2,1)S(1)}, u32[]{:S(2)}, u32[]{:S(2)}) collective-permute-start(bf16[128,768]{1,0:T(8,128)(2,1)S(1)} %shard_map.87), channel_id=1, source_target_pairs={{0,64},{32,96},{64,128},{96,160},{128,192},{160,224},{192,256},{22... | collective-permute-start | bytes 589832 | tf_op jit(solution)/shard_map/ppermute | solution.py:319
  149.2 5.4 %collective-permute-done.14.refs_2_ = bf16[128,768]{1,0:T(8,128)(2,1)S(1)} collective-permute-done((bf16[128,768]{1,0:T(8,128)(2,1)S(1)}, bf16[128,768]{1,0:T(8,128)(2,1)S(1)}, u32[]{:S(2)}, u32[]{:S(2)}) %collective-permute-start.14) | collective-permute-done | bytes 196640 | tf_op jit(solution)/shard_map/ppermute | solution.py:319
  155.9 12.1 %all-to-all-done.1 = bf16[32,40,1024]{2,1,0:T(8,128)(2,1)} async-done(((bf16[32,40,1024]{2,1,0:T(8,128)(2,1)}), bf16[32,40,1024]{2,1,0:T(8,128)(2,1)}, u32[]{:S(2)}, u32[]{:S(2)}) %all-to-all-start.1) | async-done | bytes 2621472 | tf_op jit(solution)/shard_map/all_to_all | solution.py:310
  168.0 3.7 %shard_map.81 = bf16[128,2048]{1,0:T(8,128)(2,1)} custom-call(s32[8,128]{1,0:T(8,128)S(1)} %bitcast.18, bf16[1280,1024]{1,0:T(8,128)(2,1)} %bitcast.9.refs_1_), custom_call_target="tpu_custom_call" | custom-call | flops 1000000000 | bytes 4000000 | tf_op jit(solution)/shard_map/pallas_call | solution.py:428
  (34 shorter events, 18.9 us)
Async XLA Ops:
  5.3 13.1 %copy-start.3 = (bf16[1,128,384]{2,1,0:T(8,128)(2,1)S(1)}, bf16[1,128,384]{2,1,0:T(8,128)(2,1)}, u32[]{:S(2)}) copy-start(bf16[1,128,384]{2,1,0:T(8,128)(2,1)} %param.8) | copy-start | bytes 294916
  5.3 13.1 %copy-start.4 = (bf16[1,128,384]{2,1,0:T(8,128)(2,1)S(1)}, bf16[1,128,384]{2,1,0:T(8,128)(2,1)}, u32[]{:S(2)}) copy-start(bf16[1,128,384]{2,1,0:T(8,128)(2,1)} %param.9) | copy-start | bytes 294916
  5.3 84.8 %all-to-all-start = ((bf16[32,24,2048]{2,1,0:T(8,128)(2,1)}), bf16[32,24,2048]{2,1,0:T(8,128)(2,1)S(1)}, u32[]{:S(2)}, u32[]{:S(2)}) async-start(bf16[32,24,2048]{2,1,0:T(8,128)(2,1)} %bitcast.19), calls=%async_computation | async-start | bytes 6291456 | tf_op jit(solution)/shard_map/all_to_all | solution.py:310
  18.4 18.9 %collective-permute-start.6 = (bf16[128,768]{1,0:T(8,128)(2,1)S(1)}, bf16[128,768]{1,0:T(8,128)(2,1)S(1)}, u32[]{:S(2)}, u32[]{:S(2)}) collective-permute-start(bf16[128,768]{1,0:T(8,128)(2,1)S(1)} %shard_map.77.refs_0_), channel_id=1, source_target_pairs={{0,448},{32,480},{64,0},{96,32},{128,64},{160,96},{192,128},{224,1... | collective-permute-start | bytes 589832 | tf_op jit(solution)/shard_map/ppermute | solution.py:319
  21.3 17.9 %collective-permute-start.5 = (bf16[128,768]{1,0:T(8,128)(2,1)S(1)}, bf16[128,768]{1,0:T(8,128)(2,1)S(1)}, u32[]{:S(2)}, u32[]{:S(2)}) collective-permute-start(bf16[128,768]{1,0:T(8,128)(2,1)S(1)} %shard_map.77.refs_0_), channel_id=1, source_target_pairs={{0,384},{32,416},{64,448},{96,480},{128,0},{160,32},{192,64},{224,... | collective-permute-start | bytes 589832 | tf_op jit(solution)/shard_map/ppermute | solution.py:319
  23.3 24.5 %collective-permute-start.4 = (bf16[128,768]{1,0:T(8,128)(2,1)S(1)}, bf16[128,768]{1,0:T(8,128)(2,1)}, u32[]{:S(2)}, u32[]{:S(2)}) collective-permute-start(bf16[128,768]{1,0:T(8,128)(2,1)S(1)} %shard_map.77.refs_0_), channel_id=1, source_target_pairs={{0,320},{32,352},{64,384},{96,416},{128,448},{160,480},{192,0},{22... | collective-permute-start | bytes 589832 | tf_op jit(solution)/shard_map/ppermute | solution.py:319
  28.2 28.8 %collective-permute-start.3 = (bf16[128,768]{1,0:T(8,128)(2,1)S(1)}, bf16[128,768]{1,0:T(8,128)(2,1)}, u32[]{:S(2)}, u32[]{:S(2)}) collective-permute-start(bf16[128,768]{1,0:T(8,128)(2,1)S(1)} %shard_map.77.refs_0_), channel_id=1, source_target_pairs={{0,256},{32,288},{64,320},{96,352},{128,384},{160,416},{192,448},{... | collective-permute-start | bytes 589832 | tf_op jit(solution)/shard_map/ppermute | solution.py:319
  32.6 24.4 %collective-permute-start.2 = (bf16[128,768]{1,0:T(8,128)(2,1)S(1)}, bf16[128,768]{1,0:T(8,128)(2,1)}, u32[]{:S(2)}, u32[]{:S(2)}) collective-permute-start(bf16[128,768]{1,0:T(8,128)(2,1)S(1)} %shard_map.77.refs_0_), channel_id=1, source_target_pairs={{0,192},{32,224},{64,256},{96,288},{128,320},{160,352},{192,384},{... | collective-permute-start | bytes 589832 | tf_op jit(solution)/shard_map/ppermute | solution.py:319
  37.3 26.6 %collective-permute-start.1 = (bf16[128,768]{1,0:T(8,128)(2,1)S(1)}, bf16[128,768]{1,0:T(8,128)(2,1)}, u32[]{:S(2)}, u32[]{:S(2)}) collective-permute-start(bf16[128,768]{1,0:T(8,128)(2,1)S(1)} %shard_map.77.refs_0_), channel_id=1, source_target_pairs={{0,128},{32,160},{64,192},{96,224},{128,256},{160,288},{192,320},{... | collective-permute-start | bytes 589832 | tf_op jit(solution)/shard_map/ppermute | solution.py:319
  39.2 0.7 copy-start.1
  39.9 27.6 %collective-permute-start = (bf16[128,768]{1,0:T(8,128)(2,1)S(1)}, bf16[128,768]{1,0:T(8,128)(2,1)}, u32[]{:S(2)}, u32[]{:S(2)}) collective-permute-start(bf16[128,768]{1,0:T(8,128)(2,1)S(1)} %shard_map.77.refs_0_), channel_id=1, source_target_pairs={{0,64},{32,96},{64,128},{96,160},{128,192},{160,224},{192,256},{22... | collective-permute-start | bytes 589832 | tf_op jit(solution)/shard_map/ppermute | solution.py:319
  67.5 0.9 copy-start.2
  69.9 5.6 %collective-permute-start.7 = (bf16[1024,768]{1,0:T(8,128)(2,1)S(1)}, bf16[1024,768]{1,0:T(8,128)(2,1)S(1)}, u32[]{:S(2)}, u32[]{:S(2)}) collective-permute-start(bf16[1024,768]{1,0:T(8,128)(2,1)S(1)} %shard_map.78.refs_1_), channel_id=1, source_target_pairs={{0,32},{32,0},{64,96},{96,64},{128,160},{160,128},{192,224},{224,1... | collective-permute-start | bytes 4718600 | tf_op jit(solution)/shard_map/ppermute | solution.py:322
  76.2 1.7 copy-start
  100.0 68.1 %all-to-all-start.1 = ((bf16[32,40,1024]{2,1,0:T(8,128)(2,1)}), bf16[32,40,1024]{2,1,0:T(8,128)(2,1)}, u32[]{:S(2)}, u32[]{:S(2)}) async-start(bf16[32,40,1024]{2,1,0:T(8,128)(2,1)} %bitcast.20), calls=%async_computation.1 | async-start | bytes 5242880 | tf_op jit(solution)/shard_map/all_to_all | solution.py:310
  106.4 1.3 copy-start.6
  107.7 5.7 %copy-start.7 = (bf16[768,768]{1,0:T(8,128)(2,1)S(1)}, bf16[768,768]{1,0:T(8,128)(2,1)}, u32[]{:S(2)}) copy-start(bf16[768,768]{1,0:T(8,128)(2,1)} %get-tuple-element.15.refs_2_) | copy-start | bytes 3538948
  109.7 6.5 %collective-permute-start.8 = (bf16[1024,768]{1,0:T(8,128)(2,1)S(1)}, bf16[1024,768]{1,0:T(8,128)(2,1)S(1)}, u32[]{:S(2)}, u32[]{:S(2)}) collective-permute-start(bf16[1024,768]{1,0:T(8,128)(2,1)S(1)} %shard_map.83), channel_id=1, source_target_pairs={{0,32},{32,0},{64,96},{96,64},{128,160},{160,128},{192,224},{224,1... | collective-permute-start | bytes 4718600 | tf_op jit(solution)/shard_map/ppermute | solution.py:322
  117.6 8.1 %collective-permute-start.9 = (bf16[128,768]{1,0:T(8,128)(2,1)S(1)}, bf16[128,768]{1,0:T(8,128)(2,1)S(1)}, u32[]{:S(2)}, u32[]{:S(2)}) collective-permute-start(bf16[128,768]{1,0:T(8,128)(2,1)S(1)} %get-tuple-element.17), channel_id=1, source_target_pairs={{0,64},{32,96},{64,128},{96,160},{128,192},{160,224},{192,256},{22... | collective-permute-start | bytes 589832 | tf_op jit(solution)/shard_map/ppermute | solution.py:319
  119.9 7.8 %collective-permute-start.10 = (bf16[128,768]{1,0:T(8,128)(2,1)S(1)}, bf16[128,768]{1,0:T(8,128)(2,1)S(1)}, u32[]{:S(2)}, u32[]{:S(2)}) collective-permute-start(bf16[128,768]{1,0:T(8,128)(2,1)S(1)} %get-tuple-element.18), channel_id=1, source_target_pairs={{0,448},{32,480},{64,0},{96,32},{128,64},{160,96},{192,128},{224,1... | collective-permute-start | bytes 589832 | tf_op jit(solution)/shard_map/ppermute | solution.py:319
  128.4 7.0 %collective-permute-start.11 = (bf16[128,768]{1,0:T(8,128)(2,1)S(1)}, bf16[128,768]{1,0:T(8,128)(2,1)S(1)}, u32[]{:S(2)}, u32[]{:S(2)}) collective-permute-start(bf16[128,768]{1,0:T(8,128)(2,1)S(1)} %get-tuple-element.19), channel_id=1, source_target_pairs={{0,64},{32,96},{64,128},{96,160},{128,192},{160,224},{192,256},{22... | collective-permute-start | bytes 589832 | tf_op jit(solution)/shard_map/ppermute | solution.py:319
  130.7 6.9 %collective-permute-start.12 = (bf16[128,768]{1,0:T(8,128)(2,1)S(1)}, bf16[128,768]{1,0:T(8,128)(2,1)S(1)}, u32[]{:S(2)}, u32[]{:S(2)}) collective-permute-start(bf16[128,768]{1,0:T(8,128)(2,1)S(1)} %get-tuple-element.20), channel_id=1, source_target_pairs={{0,448},{32,480},{64,0},{96,32},{128,64},{160,96},{192,128},{224,1... | collective-permute-start | bytes 589832 | tf_op jit(solution)/shard_map/ppermute | solution.py:319
  138.2 6.7 %collective-permute-start.13 = (bf16[128,768]{1,0:T(8,128)(2,1)S(1)}, bf16[128,768]{1,0:T(8,128)(2,1)S(1)}, u32[]{:S(2)}, u32[]{:S(2)}) collective-permute-start(bf16[128,768]{1,0:T(8,128)(2,1)S(1)} %get-tuple-element.21), channel_id=1, source_target_pairs={{0,64},{32,96},{64,128},{96,160},{128,192},{160,224},{192,256},{22... | collective-permute-start | bytes 589832 | tf_op jit(solution)/shard_map/ppermute | solution.py:319
  141.8 26.2 %copy-start.5 = (s32[128,8]{0,1:T(8,128)S(1)}, s32[128,8]{0,1:T(8,128)}, u32[]{:S(2)}) copy-start(s32[128,8]{0,1:T(8,128)} %param.6) | copy-start | bytes 12292
  141.8 7.4 %collective-permute-start.15 = (bf16[128,768]{1,0:T(8,128)(2,1)S(1)}, bf16[128,768]{1,0:T(8,128)(2,1)S(1)}, u32[]{:S(2)}, u32[]{:S(2)}) collective-permute-start(bf16[128,768]{1,0:T(8,128)(2,1)S(1)} %get-tuple-element.22), channel_id=1, source_target_pairs={{0,448},{32,480},{64,0},{96,32},{128,64},{160,96},{192,128},{224,1... | collective-permute-start | bytes 589832 | tf_op jit(solution)/shard_map/ppermute | solution.py:319
  145.6 9.0 %collective-permute-start.14 = (bf16[128,768]{1,0:T(8,128)(2,1)S(1)}, bf16[128,768]{1,0:T(8,128)(2,1)S(1)}, u32[]{:S(2)}, u32[]{:S(2)}) collective-permute-start(bf16[128,768]{1,0:T(8,128)(2,1)S(1)} %shard_map.87), channel_id=1, source_target_pairs={{0,64},{32,96},{64,128},{96,160},{128,192},{160,224},{192,256},{22... | collective-permute-start | bytes 589832 | tf_op jit(solution)/shard_map/ppermute | solution.py:319

commit v4 on v3

--- a/solution.py
+++ b/solution.py
@@ -11,8 +11,10 @@
 PER_ROW = 5
 BACK = 40
 STEPS = 2
+PIECES = 4
 CORES = 2
 FETCHES = 4
+RETURNED = 5
 VMEM = 32 * 2**20
 BIG = 60 * 2**20
 MIDDLE = 32 * 2**20
@@ -53,12 +55,6 @@
     return rank, jnp.where(routed > 0.5, rank, -1.0)
 
 
-def repeat_rows(experts, rows):
-    row = iota((experts * rows, experts), 0)
-    first = iota((experts * rows, experts), 1) * rows
-    return one_if((row >= first) & (row < first + rows))
-
-
 def pack_kernel(experts, routes_ref, tokens_hbm, cot_hbm, out_ref, held, sems, tokens_ref, cot_ref, in_sems):
     fetches = (
         pltpu.make_async_copy(tokens_hbm, tokens_ref, in_sems.at[0]),
@@ -71,9 +67,14 @@
     width = tokens_ref.shape[1]
     hidden = cot_ref.shape[1]
     rank, place = ranks(routes, experts)
-    at = dot(repeat_rows(experts, BLOCK), place.astype(jnp.bfloat16))
-    row = iota((experts, BLOCK, count), 1).reshape(experts * BLOCK, count)
-    pick = one_if(at == row.astype(jnp.float32))
+    row = iota((BLOCK, count), 0).astype(jnp.float32)
+    pick = jnp.concatenate(
+        [
+            jnp.where(jnp.broadcast_to(place[e : e + 1], row.shape) == row, 1.0, 0.0)
+            for e in range(experts)
+        ],
+        axis=0,
+    ).astype(jnp.bfloat16)
     slots = count * top
     spread = one_if(lax.shift_right_logical(iota((count, slots), 1), 3) == iota((count, slots), 0))
     both = jnp.concatenate((routes.astype(jnp.float32), rank), axis=0).astype(jnp.bfloat16)
@@ -83,17 +84,30 @@
     slot_place = jnp.where(
         named == iota((experts, slots), 0).astype(jnp.float32), wide[top:], -8.0
     )
-    slot_at = dot(repeat_rows(experts, TAIL), slot_place.astype(jnp.bfloat16))
-    offset = slot_at - (iota(slot_at.shape, 0) & (TAIL - 1)).astype(jnp.float32)
-    for fetch in fetches:
-        fetch.wait()
-    cot = cot_ref[...]
+    upper = iota((8, slots), 0) < TAIL
+    behind = (iota((8, slots), 0) & (TAIL - 1)).astype(jnp.float32)
+    offset = jnp.concatenate(
+        [
+            jnp.where(
+                upper,
+                jnp.broadcast_to(slot_place[e : e + 1], upper.shape),
+                jnp.broadcast_to(slot_place[e + 1 : e + 2], upper.shape),
+            )
+            - behind
+            for e in range(0, experts, 2)
+        ],
+        axis=0,
+    )
+    fetches[0].wait()
     copies = []
-    for i in range(PER_ROW + 1):
+    for i in (PER_ROW, *range(PER_ROW)):
         low, high = i * hidden, min((i + 1) * hidden, width)
         rows = dot(pick, tokens_ref[:, low:high])
+        if i == 0:
+            fetches[1].wait()
         if i < PER_ROW:
-            tail = dot(one_if(offset == float(TAIL * i)), cot).reshape(experts // 2, 8, hidden)
+            tail = dot(one_if(offset == float(TAIL * i)), cot_ref[...])
+            tail = tail.reshape(experts // 2, 8, hidden)
             tail = jnp.stack((pltpu.roll(tail, TAIL, 1), tail), axis=1).reshape(experts, 8, hidden)
             rows = rows.reshape(experts, BLOCK, hidden)
             last = rows[:, BLOCK - 8 :]
@@ -113,9 +127,17 @@
     stacked_ref[...] = jnp.concatenate((gate_ref[...], up_ref[...]), axis=1)
 
 
-def combine_kernel(experts, routes_ref, returned_ref, out_ref):
+def combine_kernel(experts, routes_ref, returned_hbm, out_ref, returned_ref, sems):
+    half = returned_ref.shape[1]
+    count = sems.shape[0]
+    size = returned_ref.shape[0] // count
+    fetches = []
+    for k in range(count):
+        at = pl.ds(k * size, size)
+        fetch = pltpu.make_async_copy(returned_hbm.at[at], returned_ref.at[at], sems.at[k])
+        fetch.start()
+        fetches.append(fetch)
     _, place = ranks(routes_ref[...], experts)
-    half = returned_ref.shape[1]
     lane = iota((experts, experts * BACK), 1)
     first = iota((experts, experts * BACK), 0) * BACK
     mine = (lane >= first) & (lane < first + BACK)
@@ -124,18 +146,46 @@
     low = jnp.where(within < CAP, within, -2.0)
     high = jnp.where(within < BLOCK, within - TAIL, within - BLOCK)
     high = jnp.where(within < CAP, -2.0, high)
-    returned = returned_ref[...]
-    out_ref[:, :half] = dot(one_if(at == low), returned).astype(jnp.bfloat16)
-    out_ref[:, half:] = dot(one_if(at == high), returned).astype(jnp.bfloat16)
+    both = jnp.concatenate((one_if(at == low), one_if(at == high)), axis=0)
+    total = 0.0
+    for k, fetch in enumerate(fetches):
+        fetch.wait()
+        part = slice(k * size, (k + 1) * size)
+        total += dot(both[:, part], returned_ref[part])
+    count = out_ref.shape[0]
+    out_ref[:, :half] = total[:count].astype(jnp.bfloat16)
+    out_ref[:, half:] = total[count:].astype(jnp.bfloat16)
+
+
+def make_deltas(received, pre):
+    rows, hidden = received.shape[0], pre.shape[1] // 2
+    blocks = rows // BLOCK
+    tail = received[:, : PER_ROW * hidden].astype(jnp.float32)
+    tail = tail.reshape(blocks, BLOCK, PER_ROW * hidden)[:, BLOCK - 8 :]
+    first = iota((blocks, 8, hidden), 1) < TAIL
+
+    def cot(i):
+        return tail[:, :, i * hidden : (i + 1) * hidden]
+
+    grad_out = jnp.concatenate(
+        (
+            jnp.where(first, pltpu.roll(cot(0), TAIL, 1), cot(1)),
+            jnp.where(first, pltpu.roll(cot(2), TAIL, 1), cot(3)),
+            jnp.where(first, pltpu.roll(cot(4), TAIL, 1), 0.0),
+        ),
+        axis=1,
+    ).reshape(rows, hidden)
+    gate_pre, up_pre = pre[:, :hidden], pre[:, hidden:]
+    sigmoid_gate = jax.nn.sigmoid(gate_pre)
+    gate_delta = grad_out * up_pre * sigmoid_gate * (1.0 + gate_pre * (1.0 - sigmoid_gate))
+    up_delta = grad_out * gate_pre * sigmoid_gate
+    return jnp.concatenate((gate_delta, up_delta), axis=1)
 
 
 def middle_kernel(
-    received_ref, weight_hbm, delta_hbm, back_hbm, weight_ref, in_sems, delta_ref, delta_sems, held, sems, pre_ref
+    received_ref, weight_hbm, delta_hbm, back_hbm, weight_ref, in_sems, delta_ref, delta_sems, held, sems, pre_ref, twice_ref
 ):
-    rows = received_ref.shape[0] // STEPS
     width = received_ref.shape[1]
-    hidden = weight_ref.shape[1] // 2
-    blocks = rows // BLOCK
     half = width // 2
     full = BLOCK - 8
     depth = width // FETCHES
@@ -145,52 +195,44 @@
         fetch = pltpu.make_async_copy(weight_hbm.at[at], weight_ref.at[at], in_sems.at[k])
         fetch.start()
         fetches.append(fetch)
+    rows = received_ref.shape[0] // STEPS
     for k, fetch in enumerate(fetches):
         fetch.wait()
         at = slice(k * depth, (k + 1) * depth)
-        pre = dot(received_ref[:, at], weight_ref[at])
-        pre_ref[...] = pre if k == 0 else pre_ref[...] + pre
-    for step in range(STEPS):
-        part = slice(step * rows, (step + 1) * rows)
-        received = received_ref[part]
-        pre = pre_ref[part]
-        gate_pre, up_pre = pre[:, :hidden], pre[:, hidden:]
-        tail = received.astype(jnp.float32).reshape(blocks, BLOCK, width)[:, full:]
-        first = iota((blocks, 8, hidden), 1) < TAIL
-
-        def cot(i, tail=tail):
-            return tail[:, :, i * hidden : (i + 1) * hidden]
-
-        grad_out = jnp.concatenate(
-            (
-                jnp.where(first, pltpu.roll(cot(0), TAIL, 1), cot(1)),
-                jnp.where(first, pltpu.roll(cot(2), TAIL, 1), cot(3)),
-                jnp.where(first, pltpu.roll(cot(4), TAIL, 1), 0.0),
-            ),
-            axis=1,
-        ).reshape(rows, hidden)
-        sigmoid_gate = jax.nn.sigmoid(gate_pre)
-        gate_delta = grad_out * up_pre * sigmoid_gate * (1.0 + gate_pre * (1.0 - sigmoid_gate))
-        up_delta = grad_out * gate_pre * sigmoid_gate
-        delta = jnp.concatenate((gate_delta, up_delta), axis=1)
-        delta_ref[part] = delta.astype(jnp.bfloat16)
-        at = pl.ds(step * rows, rows)
-        copy = pltpu.make_async_copy(delta_ref.at[at], delta_hbm.at[at], delta_sems.at[step])
-        copy.start()
-        copies.append(copy)
-        delta = delta.reshape(blocks, BLOCK, 2 * hidden)
-        last = delta[:, full:]
-        last = jnp.where(iota(last.shape, 1) < TAIL, last, pltpu.roll(last, TAIL, 1))
-        delta = jnp.concatenate((delta[:, :full], last), axis=1)
-        delta = delta.reshape(rows, 2 * hidden).astype(jnp.bfloat16)
-        low = times_transposed(delta, weight_ref[:half]).reshape(blocks, BLOCK, half)
-        high = times_transposed(delta, weight_ref[half:]).reshape(blocks, BLOCK, half)
-        shared = jnp.where(iota((blocks, 8, half), 1) < TAIL, low[:, full:], high[:, full:])
+        for step in range(STEPS):
+            part = slice(step * rows, (step + 1) * rows)
+            pre = dot(received_ref[part, at], weight_ref[at])
+            if k:
+                pre += pre_ref[part]
+            if k < FETCHES - 1:
+                pre_ref[part] = pre
+                continue
+            delta = make_deltas(received_ref[part], pre)
+            delta_ref[part] = delta.astype(jnp.bfloat16)
+            copy = pltpu.make_async_copy(
+                delta_ref.at[pl.ds(step * rows, rows)], delta_hbm.at[pl.ds(step * rows, rows)], delta_sems.at[step]
+            )
+            copy.start()
+            copies.append(copy)
+            delta = delta.reshape(rows // BLOCK, BLOCK, delta.shape[1])
+            last = delta[:, full:]
+            last = jnp.where(iota(last.shape, 1) < TAIL, last, pltpu.roll(last, TAIL, 1))
+            delta = jnp.concatenate((delta[:, :full], last), axis=1)
+            twice_ref[part] = delta.reshape(rows, delta.shape[2]).astype(jnp.bfloat16)
+    twice = twice_ref[...]
+    blocks = twice.shape[0] // BLOCK
+    piece = half // PIECES
+    for index in range(PIECES):
+        start = index * piece
+        low = times_transposed(twice, weight_ref[start : start + piece])
+        high = times_transposed(twice, weight_ref[half + start : half + start + piece])
+        low = low.reshape(blocks, BLOCK, piece)
+        high = high.reshape(blocks, BLOCK, piece)
+        shared = jnp.where(iota((blocks, 8, piece), 1) < TAIL, low[:, full:], high[:, full:])
         back = jnp.concatenate((low[:, :full], shared, high[:, :full]), axis=1)
-        size = blocks * BACK
-        held[step * size : (step + 1) * size] = back.reshape(size, half).astype(jnp.bfloat16)
-        at = pl.ds(step * size, size)
-        copy = pltpu.make_async_copy(held.at[at], back_hbm.at[at], sems.at[step])
+        held[:, start : start + piece] = back.reshape(blocks * BACK, piece).astype(jnp.bfloat16)
+        at = pl.ds(start, piece)
+        copy = pltpu.make_async_copy(held.at[:, at], back_hbm.at[:, at], sems.at[index])
         copy.start()
         copies.append(copy)
     for copy in copies:
@@ -372,8 +414,9 @@
         scratch_shapes=[
             *held_and_sems((width, 2 * hidden), FETCHES),
             *held_and_sems((rows, 2 * hidden), STEPS),
-            *held_and_sems((peers * BACK, half), STEPS),
+            *held_and_sems((peers * BACK, half), PIECES),
             pltpu.VMEM((rows, 2 * hidden), jnp.float32),
+            pltpu.VMEM((rows, 2 * hidden), bf16),
         ],
     )(received, hbm(weight))
     returned = exchange(back, BACK)
@@ -430,9 +473,10 @@
         shape(count, width),
         10**9,
         4 * 10**6,
-        in_specs=[whole()] * 2,
+        in_specs=[whole(), anywhere()],
         out_specs=whole(),
-    )(routes, returned)
+        scratch_shapes=held_and_sems((peers * BACK, half), RETURNED),
+    )(routes, hbm(returned))
     return (token_grad, gate_grad[None], up_grad[None])
 
 

time: 173 us -> 170 us (0.983)
  the two profiles are of different devices: /device:TPU:45 before, /device:TPU:32 now
where the time goes in v4:
time: 170 us; the launch traced here: 169 us
  starting transfers between devices  72.5 us (43%)
  waiting for transfers between devices  64.8 us (38%)
  Pallas kernels  25.9 us (15%)
  local copies, waits for them, and re-layouts  4.56 us (3%)
    ppermute x14, starting transfers between devices, along_y(): return lax.ppermute(block, 'dp', pairs)  48.9 us
    ppermute x14, waiting for transfers between devices, along_y(): return lax.ppermute(block, 'dp', pairs)  38.8 us
    all_to_all x2, waiting for transfers between devices, exchange(): lax.all_to_all(block.reshape(peers, size, -1), 'expert', split_axis=0, co...  21.2 us
    all_to_all x2, starting transfers between devices, exchange(): lax.all_to_all(block.reshape(peers, size, -1), 'expert', split_axis=0, co...  19.7 us
    pallas_call x1, Pallas kernels, on_device(): call(middle_kernel, (pltpu.HBM((rows, 2 * hidden), bf16), pltpu.HBM((peer...  7.63 us
    ppermute x2, waiting for transfers between devices, other_core(): return lax.ppermute(block, 'dp', [(d, d ^ 1) for d in range(groups)])  4.77 us
    unnamed x16, local copies, waits for them, and re-layouts  4.56 us
    pallas_call x1, Pallas kernels, on_device(): call(lambda *refs: pack_kernel(peers, *refs), pltpu.HBM((rows, width), bf...  4.52 us
  transfers between devices with their start and end apart: 18, of which 15 were waited for; matrix products, arithmetic and copies ran while one was open for 0% of the time, Pallas kernels for 6%

profile of v4, /device:TPU:32, one launch (start us, length us, event | category | flops | bytes accessed | tf_op | source)
XLA Modules:
  0.0 168.8 jit_solution(8269688714815451183)
XLA Ops:
  0.6 4.5 %shard_map.76 = bf16[768,2048]{1,0:T(8,128)(2,1)} custom-call(s32[8,128]{1,0:T(8,128)} %bitcast.17, bf16[128,2048]{1,0:T(8,128)(2,1)} %refs_1_.1, bf16[1024,384]{1,0:T(8,128)(2,1)} %bitcast.21), custom_call_target="tpu_custom_call" | custom-call | flops 2000000000 | bytes 5000000 | tf_op jit(solution)/shard_map/pallas_call | solution.py:366
  5.2 13.3 %all-to-all-start = ((bf16[32,24,2048]{2,1,0:T(8,128)(2,1)}), bf16[32,24,2048]{2,1,0:T(8,128)(2,1)S(1)}, u32[]{:S(2)}, u32[]{:S(2)}) async-start(bf16[32,24,2048]{2,1,0:T(8,128)(2,1)} %bitcast.19), calls=%async_computation | async-start | bytes 6291456 | tf_op jit(solution)/shard_map/all_to_all | solution.py:352
  18.5 2.4 %collective-permute-start.6 = (bf16[128,768]{1,0:T(8,128)(2,1)S(1)}, bf16[128,768]{1,0:T(8,128)(2,1)S(1)}, u32[]{:S(2)}, u32[]{:S(2)}) collective-permute-start(bf16[128,768]{1,0:T(8,128)(2,1)S(1)} %shard_map.77.refs_0_), channel_id=1, source_target_pairs={{0,448},{32,480},{64,0},{96,32},{128,64},{160,96},{192,128},{224,1... | collective-permute-start | bytes 589832 | tf_op jit(solution)/shard_map/ppermute | solution.py:361
  20.9 2.2 %collective-permute-start.5 = (bf16[128,768]{1,0:T(8,128)(2,1)S(1)}, bf16[128,768]{1,0:T(8,128)(2,1)S(1)}, u32[]{:S(2)}, u32[]{:S(2)}) collective-permute-start(bf16[128,768]{1,0:T(8,128)(2,1)S(1)} %shard_map.77.refs_0_), channel_id=1, source_target_pairs={{0,384},{32,416},{64,448},{96,480},{128,0},{160,32},{192,64},{224,... | collective-permute-start | bytes 589832 | tf_op jit(solution)/shard_map/ppermute | solution.py:361
  23.2 6.0 %collective-permute-start.4 = (bf16[128,768]{1,0:T(8,128)(2,1)S(1)}, bf16[128,768]{1,0:T(8,128)(2,1)}, u32[]{:S(2)}, u32[]{:S(2)}) collective-permute-start(bf16[128,768]{1,0:T(8,128)(2,1)S(1)} %shard_map.77.refs_0_), channel_id=1, source_target_pairs={{0,320},{32,352},{64,384},{96,416},{128,448},{160,480},{192,0},{22... | collective-permute-start | bytes 589832 | tf_op jit(solution)/shard_map/ppermute | solution.py:361
  29.2 3.8 %collective-permute-start.3 = (bf16[128,768]{1,0:T(8,128)(2,1)S(1)}, bf16[128,768]{1,0:T(8,128)(2,1)}, u32[]{:S(2)}, u32[]{:S(2)}) collective-permute-start(bf16[128,768]{1,0:T(8,128)(2,1)S(1)} %shard_map.77.refs_0_), channel_id=1, source_target_pairs={{0,256},{32,288},{64,320},{96,352},{128,384},{160,416},{192,448},{... | collective-permute-start | bytes 589832 | tf_op jit(solution)/shard_map/ppermute | solution.py:361
  33.1 4.6 %collective-permute-start.2 = (bf16[128,768]{1,0:T(8,128)(2,1)S(1)}, bf16[128,768]{1,0:T(8,128)(2,1)}, u32[]{:S(2)}, u32[]{:S(2)}) collective-permute-start(bf16[128,768]{1,0:T(8,128)(2,1)S(1)} %shard_map.77.refs_0_), channel_id=1, source_target_pairs={{0,192},{32,224},{64,256},{96,288},{128,320},{160,352},{192,384},{... | collective-permute-start | bytes 589832 | tf_op jit(solution)/shard_map/ppermute | solution.py:361
  37.7 3.9 %collective-permute-start.1 = (bf16[128,768]{1,0:T(8,128)(2,1)S(1)}, bf16[128,768]{1,0:T(8,128)(2,1)}, u32[]{:S(2)}, u32[]{:S(2)}) collective-permute-start(bf16[128,768]{1,0:T(8,128)(2,1)S(1)} %shard_map.77.refs_0_), channel_id=1, source_target_pairs={{0,128},{32,160},{64,192},{96,224},{128,256},{160,288},{192,320},{... | collective-permute-start | bytes 589832 | tf_op jit(solution)/shard_map/ppermute | solution.py:361
  44.6 3.6 %collective-permute-done.4.refs_5_ = bf16[128,768]{1,0:T(8,128)(2,1)} collective-permute-done((bf16[128,768]{1,0:T(8,128)(2,1)S(1)}, bf16[128,768]{1,0:T(8,128)(2,1)}, u32[]{:S(2)}, u32[]{:S(2)}) %collective-permute-start.4) | collective-permute-done | bytes 196640 | tf_op jit(solution)/shard_map/ppermute | solution.py:361
  48.2 10.9 %collective-permute-done.2.refs_3_ = bf16[128,768]{1,0:T(8,128)(2,1)} collective-permute-done((bf16[128,768]{1,0:T(8,128)(2,1)S(1)}, bf16[128,768]{1,0:T(8,128)(2,1)}, u32[]{:S(2)}, u32[]{:S(2)}) %collective-permute-start.2) | collective-permute-done | bytes 196640 | tf_op jit(solution)/shard_map/ppermute | solution.py:361
  59.0 3.6 %collective-permute-done.1.refs_2_ = bf16[128,768]{1,0:T(8,128)(2,1)} collective-permute-done((bf16[128,768]{1,0:T(8,128)(2,1)S(1)}, bf16[128,768]{1,0:T(8,128)(2,1)}, u32[]{:S(2)}, u32[]{:S(2)}) %collective-permute-start.1) | collective-permute-done | bytes 196640 | tf_op jit(solution)/shard_map/ppermute | solution.py:361
  62.6 4.4 %collective-permute-done.refs_1_ = bf16[128,768]{1,0:T(8,128)(2,1)} collective-permute-done((bf16[128,768]{1,0:T(8,128)(2,1)S(1)}, bf16[128,768]{1,0:T(8,128)(2,1)}, u32[]{:S(2)}, u32[]{:S(2)}) %collective-permute-start) | collective-permute-done | bytes 196640 | tf_op jit(solution)/shard_map/ppermute | solution.py:361
  69.3 1.9 %collective-permute-start.7 = (bf16[1024,768]{1,0:T(8,128)(2,1)S(1)}, bf16[1024,768]{1,0:T(8,128)(2,1)S(1)}, u32[]{:S(2)}, u32[]{:S(2)}) collective-permute-start(bf16[1024,768]{1,0:T(8,128)(2,1)S(1)} %shard_map.78.refs_1_), channel_id=1, source_target_pairs={{0,32},{32,0},{64,96},{96,64},{128,160},{160,128},{192,224},{224,1... | collective-permute-start | bytes 4718600 | tf_op jit(solution)/shard_map/ppermute | solution.py:364
  71.3 3.4 %collective-permute-done.7.refs_2_ = bf16[1024,768]{1,0:T(8,128)(2,1)S(1)} collective-permute-done((bf16[1024,768]{1,0:T(8,128)(2,1)S(1)}, bf16[1024,768]{1,0:T(8,128)(2,1)S(1)}, u32[]{:S(2)}, u32[]{:S(2)}) %collective-permute-start.7) | collective-permute-done | bytes 1572896 | tf_op jit(solution)/shard_map/ppermute | solution.py:364
  77.1 13.7 %all-to-all-done = bf16[32,24,2048]{2,1,0:T(8,128)(2,1)S(1)} async-done(((bf16[32,24,2048]{2,1,0:T(8,128)(2,1)}), bf16[32,24,2048]{2,1,0:T(8,128)(2,1)S(1)}, u32[]{:S(2)}, u32[]{:S(2)}) %all-to-all-start) | async-done | bytes 3145760 | tf_op jit(solution)/shard_map/all_to_all | solution.py:352
  90.8 7.6 %shard_map.80 = (bf16[768,768]{1,0:T(8,128)(2,1)}, bf16[1280,1024]{1,0:T(8,128)(2,1)}) custom-call(bf16[768,2048]{1,0:T(8,128)(2,1)S(1)} %bitcast.12, bf16[2048,768]{1,0:T(8,128)(2,1)} %copy-done), custom_call_target="tpu_custom_call" | custom-call | flops 5000000000 | bytes 10000000 | tf_op jit(solution)/shard_map/pallas_call | solution.py:406
  98.4 6.4 %all-to-all-start.1 = ((bf16[32,40,1024]{2,1,0:T(8,128)(2,1)}), bf16[32,40,1024]{2,1,0:T(8,128)(2,1)}, u32[]{:S(2)}, u32[]{:S(2)}) async-start(bf16[32,40,1024]{2,1,0:T(8,128)(2,1)} %bitcast.20), calls=%async_computation.1 | async-start | bytes 5242880 | tf_op jit(solution)/shard_map/all_to_all | solution.py:352
  106.1 2.0 %shard_map.83 = bf16[1024,768]{1,0:T(8,128)(2,1)S(1)} custom-call(s32[2]{0:T(128)S(1)} %pad_add_fusion.place_ref.refs_0_, bf16[768,2048]{1,0:T(8,128)(2,1)S(1)} %bitcast.13, bf16[768,768]{1,0:T(8,128)(2,1)S(1)} %copy-done.6), custom_call_target="tpu_custom_call" | custom-call | flops 2000000000 | bytes 5000000 | tf_op jit(solution)/shard_map/pallas_call | solution.py:424
  108.1 1.9 %collective-permute-start.8 = (bf16[1024,768]{1,0:T(8,128)(2,1)S(1)}, bf16[1024,768]{1,0:T(8,128)(2,1)S(1)}, u32[]{:S(2)}, u32[]{:S(2)}) collective-permute-start(bf16[1024,768]{1,0:T(8,128)(2,1)S(1)} %shard_map.83), channel_id=1, source_target_pairs={{0,32},{32,0},{64,96},{96,64},{128,160},{160,128},{192,224},{224,1... | collective-permute-start | bytes 4718600 | tf_op jit(solution)/shard_map/ppermute | solution.py:364
  110.1 2.0 %shard_map.82.mine_ref = bf16[1024,768]{1,0:T(8,128)(2,1)S(1)} custom-call(s32[2]{0:T(128)S(1)} %pad_add_fusion.place_ref.refs_0_, bf16[768,2048]{1,0:T(8,128)(2,1)S(1)} %bitcast.14, bf16[768,768]{1,0:T(8,128)(2,1)S(1)} %copy-done.7), custom_call_target="tpu_custom_call" | custom-call | flops 2000000000 | bytes 5000000 | tf_op jit(solution)/shard_map/pallas_call | solution.py:424
  114.8 2.6 %collective-permute-start.9 = (bf16[128,768]{1,0:T(8,128)(2,1)S(1)}, bf16[128,768]{1,0:T(8,128)(2,1)S(1)}, u32[]{:S(2)}, u32[]{:S(2)}) collective-permute-start(bf16[128,768]{1,0:T(8,128)(2,1)S(1)} %get-tuple-element.17), channel_id=1, source_target_pairs={{0,64},{32,96},{64,128},{96,160},{128,192},{160,224},{192,256},{22... | collective-permute-start | bytes 589832 | tf_op jit(solution)/shard_map/ppermute | solution.py:361
  117.4 4.5 %collective-permute-start.10 = (bf16[128,768]{1,0:T(8,128)(2,1)S(1)}, bf16[128,768]{1,0:T(8,128)(2,1)S(1)}, u32[]{:S(2)}, u32[]{:S(2)}) collective-permute-start(bf16[128,768]{1,0:T(8,128)(2,1)S(1)} %get-tuple-element.18), channel_id=1, source_target_pairs={{0,448},{32,480},{64,0},{96,32},{128,64},{160,96},{192,128},{224,1... | collective-permute-start | bytes 589832 | tf_op jit(solution)/shard_map/ppermute | solution.py:361
  121.9 3.0 %collective-permute-done.9.refs_2_ = bf16[128,768]{1,0:T(8,128)(2,1)S(1)} collective-permute-done((bf16[128,768]{1,0:T(8,128)(2,1)S(1)}, bf16[128,768]{1,0:T(8,128)(2,1)S(1)}, u32[]{:S(2)}, u32[]{:S(2)}) %collective-permute-start.9) | collective-permute-done | bytes 196640 | tf_op jit(solution)/shard_map/ppermute | solution.py:361
  126.7 2.5 %collective-permute-start.11 = (bf16[128,768]{1,0:T(8,128)(2,1)S(1)}, bf16[128,768]{1,0:T(8,128)(2,1)S(1)}, u32[]{:S(2)}, u32[]{:S(2)}) collective-permute-start(bf16[128,768]{1,0:T(8,128)(2,1)S(1)} %get-tuple-element.19), channel_id=1, source_target_pairs={{0,64},{32,96},{64,128},{96,160},{128,192},{160,224},{192,256},{22... | collective-permute-start | bytes 589832 | tf_op jit(solution)/shard_map/ppermute | solution.py:361
  129.2 5.0 %collective-permute-start.12 = (bf16[128,768]{1,0:T(8,128)(2,1)S(1)}, bf16[128,768]{1,0:T(8,128)(2,1)S(1)}, u32[]{:S(2)}, u32[]{:S(2)}) collective-permute-start(bf16[128,768]{1,0:T(8,128)(2,1)S(1)} %get-tuple-element.20), channel_id=1, source_target_pairs={{0,448},{32,480},{64,0},{96,32},{128,64},{160,96},{192,128},{224,1... | collective-permute-start | bytes 589832 | tf_op jit(solution)/shard_map/ppermute | solution.py:361
  134.2 2.2 %collective-permute-done.11.refs_2_ = bf16[128,768]{1,0:T(8,128)(2,1)S(1)} collective-permute-done((bf16[128,768]{1,0:T(8,128)(2,1)S(1)}, bf16[128,768]{1,0:T(8,128)(2,1)S(1)}, u32[]{:S(2)}, u32[]{:S(2)}) %collective-permute-start.11) | collective-permute-done | bytes 196640 | tf_op jit(solution)/shard_map/ppermute | solution.py:361
  138.3 1.9 %collective-permute-start.13 = (bf16[128,768]{1,0:T(8,128)(2,1)S(1)}, bf16[128,768]{1,0:T(8,128)(2,1)S(1)}, u32[]{:S(2)}, u32[]{:S(2)}) collective-permute-start(bf16[128,768]{1,0:T(8,128)(2,1)S(1)} %get-tuple-element.21), channel_id=1, source_target_pairs={{0,64},{32,96},{64,128},{96,160},{128,192},{160,224},{192,256},{22... | collective-permute-start | bytes 589832 | tf_op jit(solution)/shard_map/ppermute | solution.py:361
  140.2 5.6 %collective-permute-start.15 = (bf16[128,768]{1,0:T(8,128)(2,1)S(1)}, bf16[128,768]{1,0:T(8,128)(2,1)S(1)}, u32[]{:S(2)}, u32[]{:S(2)}) collective-permute-start(bf16[128,768]{1,0:T(8,128)(2,1)S(1)} %get-tuple-element.22), channel_id=1, source_target_pairs={{0,448},{32,480},{64,0},{96,32},{128,64},{160,96},{192,128},{224,1... | collective-permute-start | bytes 589832 | tf_op jit(solution)/shard_map/ppermute | solution.py:361
  148.1 1.9 %collective-permute-start.14 = (bf16[128,768]{1,0:T(8,128)(2,1)S(1)}, bf16[128,768]{1,0:T(8,128)(2,1)S(1)}, u32[]{:S(2)}, u32[]{:S(2)}) collective-permute-start(bf16[128,768]{1,0:T(8,128)(2,1)S(1)} %shard_map.87), channel_id=1, source_target_pairs={{0,64},{32,96},{64,128},{96,160},{128,192},{160,224},{192,256},{22... | collective-permute-start | bytes 589832 | tf_op jit(solution)/shard_map/ppermute | solution.py:361
  150.1 6.8 %collective-permute-done.14.refs_2_ = bf16[128,768]{1,0:T(8,128)(2,1)S(1)} collective-permute-done((bf16[128,768]{1,0:T(8,128)(2,1)S(1)}, bf16[128,768]{1,0:T(8,128)(2,1)S(1)}, u32[]{:S(2)}, u32[]{:S(2)}) %collective-permute-start.14) | collective-permute-done | bytes 196640 | tf_op jit(solution)/shard_map/ppermute | solution.py:361
  158.2 7.5 %all-to-all-done.1 = bf16[32,40,1024]{2,1,0:T(8,128)(2,1)} async-done(((bf16[32,40,1024]{2,1,0:T(8,128)(2,1)}), bf16[32,40,1024]{2,1,0:T(8,128)(2,1)}, u32[]{:S(2)}, u32[]{:S(2)}) %all-to-all-start.1) | async-done | bytes 2621472 | tf_op jit(solution)/shard_map/all_to_all | solution.py:352
  165.7 3.1 %shard_map.81 = bf16[128,2048]{1,0:T(8,128)(2,1)} custom-call(s32[8,128]{1,0:T(8,128)S(1)} %bitcast.18, bf16[1280,1024]{1,0:T(8,128)(2,1)} %bitcast.9.refs_1_), custom_call_target="tpu_custom_call" | custom-call | flops 1000000000 | bytes 4000000 | tf_op jit(solution)/shard_map/pallas_call | solution.py:471
  (34 shorter events, 19.0 us)
Async XLA Ops:
  5.2 13.3 %copy-start.3 = (bf16[1,128,384]{2,1,0:T(8,128)(2,1)S(1)}, bf16[1,128,384]{2,1,0:T(8,128)(2,1)}, u32[]{:S(2)}) copy-start(bf16[1,128,384]{2,1,0:T(8,128)(2,1)} %param.8) | copy-start | bytes 294916
  5.2 13.3 %copy-start.4 = (bf16[1,128,384]{2,1,0:T(8,128)(2,1)S(1)}, bf16[1,128,384]{2,1,0:T(8,128)(2,1)}, u32[]{:S(2)}) copy-start(bf16[1,128,384]{2,1,0:T(8,128)(2,1)} %param.9) | copy-start | bytes 294916
  5.2 85.6 %all-to-all-start = ((bf16[32,24,2048]{2,1,0:T(8,128)(2,1)}), bf16[32,24,2048]{2,1,0:T(8,128)(2,1)S(1)}, u32[]{:S(2)}, u32[]{:S(2)}) async-start(bf16[32,24,2048]{2,1,0:T(8,128)(2,1)} %bitcast.19), calls=%async_computation | async-start | bytes 6291456 | tf_op jit(solution)/shard_map/all_to_all | solution.py:352
  18.5 19.1 %collective-permute-start.6 = (bf16[128,768]{1,0:T(8,128)(2,1)S(1)}, bf16[128,768]{1,0:T(8,128)(2,1)S(1)}, u32[]{:S(2)}, u32[]{:S(2)}) collective-permute-start(bf16[128,768]{1,0:T(8,128)(2,1)S(1)} %shard_map.77.refs_0_), channel_id=1, source_target_pairs={{0,448},{32,480},{64,0},{96,32},{128,64},{160,96},{192,128},{224,1... | collective-permute-start | bytes 589832 | tf_op jit(solution)/shard_map/ppermute | solution.py:361
  20.9 20.9 %collective-permute-start.5 = (bf16[128,768]{1,0:T(8,128)(2,1)S(1)}, bf16[128,768]{1,0:T(8,128)(2,1)S(1)}, u32[]{:S(2)}, u32[]{:S(2)}) collective-permute-start(bf16[128,768]{1,0:T(8,128)(2,1)S(1)} %shard_map.77.refs_0_), channel_id=1, source_target_pairs={{0,384},{32,416},{64,448},{96,480},{128,0},{160,32},{192,64},{224,... | collective-permute-start | bytes 589832 | tf_op jit(solution)/shard_map/ppermute | solution.py:361
  23.2 25.0 %collective-permute-start.4 = (bf16[128,768]{1,0:T(8,128)(2,1)S(1)}, bf16[128,768]{1,0:T(8,128)(2,1)}, u32[]{:S(2)}, u32[]{:S(2)}) collective-permute-start(bf16[128,768]{1,0:T(8,128)(2,1)S(1)} %shard_map.77.refs_0_), channel_id=1, source_target_pairs={{0,320},{32,352},{64,384},{96,416},{128,448},{160,480},{192,0},{22... | collective-permute-start | bytes 589832 | tf_op jit(solution)/shard_map/ppermute | solution.py:361
  29.2 18.9 %collective-permute-start.3 = (bf16[128,768]{1,0:T(8,128)(2,1)S(1)}, bf16[128,768]{1,0:T(8,128)(2,1)}, u32[]{:S(2)}, u32[]{:S(2)}) collective-permute-start(bf16[128,768]{1,0:T(8,128)(2,1)S(1)} %shard_map.77.refs_0_), channel_id=1, source_target_pairs={{0,256},{32,288},{64,320},{96,352},{128,384},{160,416},{192,448},{... | collective-permute-start | bytes 589832 | tf_op jit(solution)/shard_map/ppermute | solution.py:361
  33.1 26.0 %collective-permute-start.2 = (bf16[128,768]{1,0:T(8,128)(2,1)S(1)}, bf16[128,768]{1,0:T(8,128)(2,1)}, u32[]{:S(2)}, u32[]{:S(2)}) collective-permute-start(bf16[128,768]{1,0:T(8,128)(2,1)S(1)} %shard_map.77.refs_0_), channel_id=1, source_target_pairs={{0,192},{32,224},{64,256},{96,288},{128,320},{160,352},{192,384},{... | collective-permute-start | bytes 589832 | tf_op jit(solution)/shard_map/ppermute | solution.py:361
  37.7 24.9 %collective-permute-start.1 = (bf16[128,768]{1,0:T(8,128)(2,1)S(1)}, bf16[128,768]{1,0:T(8,128)(2,1)}, u32[]{:S(2)}, u32[]{:S(2)}) collective-permute-start(bf16[128,768]{1,0:T(8,128)(2,1)S(1)} %shard_map.77.refs_0_), channel_id=1, source_target_pairs={{0,128},{32,160},{64,192},{96,224},{128,256},{160,288},{192,320},{... | collective-permute-start | bytes 589832 | tf_op jit(solution)/shard_map/ppermute | solution.py:361
  41.9 0.7 copy-start.1
  42.5 24.5 %collective-permute-start = (bf16[128,768]{1,0:T(8,128)(2,1)S(1)}, bf16[128,768]{1,0:T(8,128)(2,1)}, u32[]{:S(2)}, u32[]{:S(2)}) collective-permute-start(bf16[128,768]{1,0:T(8,128)(2,1)S(1)} %shard_map.77.refs_0_), channel_id=1, source_target_pairs={{0,64},{32,96},{64,128},{96,160},{128,192},{160,224},{192,256},{22... | collective-permute-start | bytes 589832 | tf_op jit(solution)/shard_map/ppermute | solution.py:361
  67.0 0.9 copy-start.2
  69.3 5.3 %collective-permute-start.7 = (bf16[1024,768]{1,0:T(8,128)(2,1)S(1)}, bf16[1024,768]{1,0:T(8,128)(2,1)S(1)}, u32[]{:S(2)}, u32[]{:S(2)}) collective-permute-start(bf16[1024,768]{1,0:T(8,128)(2,1)S(1)} %shard_map.78.refs_1_), channel_id=1, source_target_pairs={{0,32},{32,0},{64,96},{96,64},{128,160},{160,128},{192,224},{224,1... | collective-permute-start | bytes 4718600 | tf_op jit(solution)/shard_map/ppermute | solution.py:364
  75.4 1.7 copy-start
  98.4 67.3 %all-to-all-start.1 = ((bf16[32,40,1024]{2,1,0:T(8,128)(2,1)}), bf16[32,40,1024]{2,1,0:T(8,128)(2,1)}, u32[]{:S(2)}, u32[]{:S(2)}) async-start(bf16[32,40,1024]{2,1,0:T(8,128)(2,1)} %bitcast.20), calls=%async_computation.1 | async-start | bytes 5242880 | tf_op jit(solution)/shard_map/all_to_all | solution.py:352
  104.9 1.3 copy-start.6
  106.1 3.9 %copy-start.7 = (bf16[768,768]{1,0:T(8,128)(2,1)S(1)}, bf16[768,768]{1,0:T(8,128)(2,1)}, u32[]{:S(2)}) copy-start(bf16[768,768]{1,0:T(8,128)(2,1)} %get-tuple-element.15.refs_2_) | copy-start | bytes 3538948
  108.1 5.3 %collective-permute-start.8 = (bf16[1024,768]{1,0:T(8,128)(2,1)S(1)}, bf16[1024,768]{1,0:T(8,128)(2,1)S(1)}, u32[]{:S(2)}, u32[]{:S(2)}) collective-permute-start(bf16[1024,768]{1,0:T(8,128)(2,1)S(1)} %shard_map.83), channel_id=1, source_target_pairs={{0,32},{32,0},{64,96},{96,64},{128,160},{160,128},{192,224},{224,1... | collective-permute-start | bytes 4718600 | tf_op jit(solution)/shard_map/ppermute | solution.py:364
  114.8 10.0 %collective-permute-start.9 = (bf16[128,768]{1,0:T(8,128)(2,1)S(1)}, bf16[128,768]{1,0:T(8,128)(2,1)S(1)}, u32[]{:S(2)}, u32[]{:S(2)}) collective-permute-start(bf16[128,768]{1,0:T(8,128)(2,1)S(1)} %get-tuple-element.17), channel_id=1, source_target_pairs={{0,64},{32,96},{64,128},{96,160},{128,192},{160,224},{192,256},{22... | collective-permute-start | bytes 589832 | tf_op jit(solution)/shard_map/ppermute | solution.py:361
  117.4 8.6 %collective-permute-start.10 = (bf16[128,768]{1,0:T(8,128)(2,1)S(1)}, bf16[128,768]{1,0:T(8,128)(2,1)S(1)}, u32[]{:S(2)}, u32[]{:S(2)}) collective-permute-start(bf16[128,768]{1,0:T(8,128)(2,1)S(1)} %get-tuple-element.18), channel_id=1, source_target_pairs={{0,448},{32,480},{64,0},{96,32},{128,64},{160,96},{192,128},{224,1... | collective-permute-start | bytes 589832 | tf_op jit(solution)/shard_map/ppermute | solution.py:361
  126.7 9.7 %collective-permute-start.11 = (bf16[128,768]{1,0:T(8,128)(2,1)S(1)}, bf16[128,768]{1,0:T(8,128)(2,1)S(1)}, u32[]{:S(2)}, u32[]{:S(2)}) collective-permute-start(bf16[128,768]{1,0:T(8,128)(2,1)S(1)} %get-tuple-element.19), channel_id=1, source_target_pairs={{0,64},{32,96},{64,128},{96,160},{128,192},{160,224},{192,256},{22... | collective-permute-start | bytes 589832 | tf_op jit(solution)/shard_map/ppermute | solution.py:361
  129.2 8.4 %collective-permute-start.12 = (bf16[128,768]{1,0:T(8,128)(2,1)S(1)}, bf16[128,768]{1,0:T(8,128)(2,1)S(1)}, u32[]{:S(2)}, u32[]{:S(2)}) collective-permute-start(bf16[128,768]{1,0:T(8,128)(2,1)S(1)} %get-tuple-element.20), channel_id=1, source_target_pairs={{0,448},{32,480},{64,0},{96,32},{128,64},{160,96},{192,128},{224,1... | collective-permute-start | bytes 589832 | tf_op jit(solution)/shard_map/ppermute | solution.py:361
  138.3 9.2 %collective-permute-start.13 = (bf16[128,768]{1,0:T(8,128)(2,1)S(1)}, bf16[128,768]{1,0:T(8,128)(2,1)S(1)}, u32[]{:S(2)}, u32[]{:S(2)}) collective-permute-start(bf16[128,768]{1,0:T(8,128)(2,1)S(1)} %get-tuple-element.21), channel_id=1, source_target_pairs={{0,64},{32,96},{64,128},{96,160},{128,192},{160,224},{192,256},{22... | collective-permute-start | bytes 589832 | tf_op jit(solution)/shard_map/ppermute | solution.py:361
  140.2 25.5 %copy-start.5 = (s32[128,8]{0,1:T(8,128)S(1)}, s32[128,8]{0,1:T(8,128)}, u32[]{:S(2)}) copy-start(s32[128,8]{0,1:T(8,128)} %param.6) | copy-start | bytes 12292
  140.2 9.8 %collective-permute-start.15 = (bf16[128,768]{1,0:T(8,128)(2,1)S(1)}, bf16[128,768]{1,0:T(8,128)(2,1)S(1)}, u32[]{:S(2)}, u32[]{:S(2)}) collective-permute-start(bf16[128,768]{1,0:T(8,128)(2,1)S(1)} %get-tuple-element.22), channel_id=1, source_target_pairs={{0,448},{32,480},{64,0},{96,32},{128,64},{160,96},{192,128},{224,1... | collective-permute-start | bytes 589832 | tf_op jit(solution)/shard_map/ppermute | solution.py:361
  148.1 8.8 %collective-permute-start.14 = (bf16[128,768]{1,0:T(8,128)(2,1)S(1)}, bf16[128,768]{1,0:T(8,128)(2,1)S(1)}, u32[]{:S(2)}, u32[]{:S(2)}) collective-permute-start(bf16[128,768]{1,0:T(8,128)(2,1)S(1)} %shard_map.87), channel_id=1, source_target_pairs={{0,64},{32,96},{64,128},{96,160},{128,192},{160,224},{192,256},{22... | collective-permute-start | bytes 589832 | tf_op jit(solution)/shard_map/ppermute | solution.py:361

commit v5 on v4

--- a/solution.py
+++ b/solution.py
@@ -14,7 +14,6 @@
 PIECES = 4
 CORES = 2
 FETCHES = 4
-RETURNED = 5
 VMEM = 32 * 2**20
 BIG = 60 * 2**20
 MIDDLE = 32 * 2**20
@@ -55,13 +54,15 @@
     return rank, jnp.where(routed > 0.5, rank, -1.0)
 
 
-def pack_kernel(experts, routes_ref, tokens_hbm, cot_hbm, out_ref, held, sems, tokens_ref, cot_ref, in_sems):
+def pack_kernel(experts, routes_hbm, tokens_hbm, cot_hbm, out_ref, held, sems, tokens_ref, cot_ref, in_sems, routes_ref):
     fetches = (
+        pltpu.make_async_copy(routes_hbm, routes_ref, in_sems.at[2]),
         pltpu.make_async_copy(tokens_hbm, tokens_ref, in_sems.at[0]),
         pltpu.make_async_copy(cot_hbm, cot_ref, in_sems.at[1]),
     )
     for fetch in fetches:
         fetch.start()
+    fetches[0].wait()
     routes = routes_ref[...]
     top, count = routes.shape
     width = tokens_ref.shape[1]
@@ -98,13 +99,13 @@
         ],
         axis=0,
     )
-    fetches[0].wait()
+    fetches[1].wait()
     copies = []
     for i in (PER_ROW, *range(PER_ROW)):
         low, high = i * hidden, min((i + 1) * hidden, width)
         rows = dot(pick, tokens_ref[:, low:high])
         if i == 0:
-            fetches[1].wait()
+            fetches[2].wait()
         if i < PER_ROW:
             tail = dot(one_if(offset == float(TAIL * i)), cot_ref[...])
             tail = tail.reshape(experts // 2, 8, hidden)
@@ -127,16 +128,8 @@
     stacked_ref[...] = jnp.concatenate((gate_ref[...], up_ref[...]), axis=1)
 
 
-def combine_kernel(experts, routes_ref, returned_hbm, out_ref, returned_ref, sems):
+def combine_kernel(experts, routes_ref, returned_ref, out_ref):
     half = returned_ref.shape[1]
-    count = sems.shape[0]
-    size = returned_ref.shape[0] // count
-    fetches = []
-    for k in range(count):
-        at = pl.ds(k * size, size)
-        fetch = pltpu.make_async_copy(returned_hbm.at[at], returned_ref.at[at], sems.at[k])
-        fetch.start()
-        fetches.append(fetch)
     _, place = ranks(routes_ref[...], experts)
     lane = iota((experts, experts * BACK), 1)
     first = iota((experts, experts * BACK), 0) * BACK
@@ -147,11 +140,7 @@
     high = jnp.where(within < BLOCK, within - TAIL, within - BLOCK)
     high = jnp.where(within < CAP, -2.0, high)
     both = jnp.concatenate((one_if(at == low), one_if(at == high)), axis=0)
-    total = 0.0
-    for k, fetch in enumerate(fetches):
-        fetch.wait()
-        part = slice(k * size, (k + 1) * size)
-        total += dot(both[:, part], returned_ref[part])
+    total = dot(both, returned_ref[...])
     count = out_ref.shape[0]
     out_ref[:, :half] = total[:count].astype(jnp.bfloat16)
     out_ref[:, half:] = total[count:].astype(jnp.bfloat16)
@@ -183,7 +172,7 @@
 
 
 def middle_kernel(
-    received_ref, weight_hbm, delta_hbm, back_hbm, weight_ref, in_sems, delta_ref, delta_sems, held, sems, pre_ref, twice_ref
+    received_ref, weight_hbm, delta_hbm, back_hbm, kept_hbm, weight_ref, in_sems, delta_ref, delta_sems, held, sems, pre_ref, twice_ref, kept_sem
 ):
     width = received_ref.shape[1]
     half = width // 2
@@ -198,6 +187,10 @@
     rows = received_ref.shape[0] // STEPS
     for k, fetch in enumerate(fetches):
         fetch.wait()
+        if k == FETCHES - 1:
+            keep = pltpu.make_async_copy(received_ref, kept_hbm, kept_sem.at[0])
+            keep.start()
+            copies.append(keep)
         at = slice(k * depth, (k + 1) * depth)
         for step in range(STEPS):
             part = slice(step * rows, (step + 1) * rows)
@@ -369,14 +362,15 @@
         2 * 10**9,
         5 * 10**6,
         BIG,
-        in_specs=[whole(), anywhere(), anywhere()],
+        in_specs=[anywhere()] * 3,
         out_specs=anywhere(),
         scratch_shapes=[
             *held_and_sems((rows, width), PER_ROW + 1),
             pltpu.VMEM((count, width), bf16),
-            *held_and_sems((count * top, hidden), 2),
+            *held_and_sems((count * top, hidden), 3),
+            pltpu.VMEM((top, count), jnp.int32),
         ],
-    )(routes, hbm(tokens), hbm(cotangent.reshape(count * top, hidden)))
+    )(hbm(routes), hbm(tokens), hbm(cotangent.reshape(count * top, hidden)))
     received = exchange(packed, BLOCK)
     stacked = call(
         stack_kernel,
@@ -403,20 +397,25 @@
         in_specs=[scalars] + [whole()] * 2,
         out_specs=whole(),
     )(place, of_core, other_core(of_core))
-    delta, back = call(
+    delta, back, kept = call(
         middle_kernel,
-        (pltpu.HBM((rows, 2 * hidden), bf16), pltpu.HBM((peers * BACK, half), bf16)),
+        (
+            pltpu.HBM((rows, 2 * hidden), bf16),
+            pltpu.HBM((peers * BACK, half), bf16),
+            pltpu.HBM((rows, width), bf16),
+        ),
         5 * 10**9,
         10**7,
         MIDDLE,
         in_specs=[whole(), anywhere()],
-        out_specs=(anywhere(), anywhere()),
+        out_specs=(anywhere(),) * 3,
         scratch_shapes=[
             *held_and_sems((width, 2 * hidden), FETCHES),
             *held_and_sems((rows, 2 * hidden), STEPS),
             *held_and_sems((peers * BACK, half), PIECES),
             pltpu.VMEM((rows, 2 * hidden), jnp.float32),
             pltpu.VMEM((rows, 2 * hidden), bf16),
+            pltpu.SemaphoreType.DMA((1,)),
         ],
     )(received, hbm(weight))
     returned = exchange(back, BACK)
@@ -428,7 +427,7 @@
             5 * 10**6,
             in_specs=[scalars] + [whole()] * 2,
             out_specs=whole(),
-        )(place, received, delta)
+        )(place, kept, delta)
         for other in (True, False)
     ]
     block = shape(share, 2 * hidden)
@@ -473,10 +472,9 @@
         shape(count, width),
         10**9,
         4 * 10**6,
-        in_specs=[whole(), anywhere()],
+        in_specs=[whole()] * 2,
         out_specs=whole(),
-        scratch_shapes=held_and_sems((peers * BACK, half), RETURNED),
-    )(routes, hbm(returned))
+    )(routes, returned)
     return (token_grad, gate_grad[None], up_grad[None])
 
 

time: 170 us -> 168 us (0.988)
  waiting for transfers between devices: 64.8 us -> 62.9 us
  local copies, waits for them, and re-layouts: 4.56 us -> 6.45 us
    unnamed x16, local copies, waits for them, and re-layouts: 4.56 us -> 6.45 us
    all_to_all x2, waiting for transfers between devices: 21.2 us -> 19.4 us  [exchange(): lax.all_to_all(block.reshape(peers, size, -1), 'expert', split_axis=0, co...]
where the time goes in v5:
time: 168 us; the launch traced here: 167 us
  starting transfers between devices  72.4 us (43%)
  waiting for transfers between devices  62.9 us (37%)
  Pallas kernels  24.2 us (14%)
  local copies, waits for them, and re-layouts  6.45 us (4%)
    ppermute x14, starting transfers between devices, along_y(): return lax.ppermute(block, 'dp', pairs)  48.9 us
    ppermute x14, waiting for transfers between devices, along_y(): return lax.ppermute(block, 'dp', pairs)  38.7 us
    all_to_all x2, starting transfers between devices, exchange(): lax.all_to_all(block.reshape(peers, size, -1), 'expert', split_axis=0, co...  19.6 us
    all_to_all x2, waiting for transfers between devices, exchange(): lax.all_to_all(block.reshape(peers, size, -1), 'expert', split_axis=0, co...  19.4 us
    pallas_call x1, Pallas kernels, on_device(): call(middle_kernel, (pltpu.HBM((rows, 2 * hidden), bf16), pltpu.HBM((peer...  7.67 us
    unnamed x16, local copies, waits for them, and re-layouts  6.45 us
    ppermute x2, waiting for transfers between devices, other_core(): return lax.ppermute(block, 'dp', [(d, d ^ 1) for d in range(groups)])  4.78 us
    pallas_call x2, Pallas kernels, on_device(): call(lambda *refs, other=other: weight_grad_kernel(other, share, *refs),...  3.94 us
  transfers between devices with their start and end apart: 18, of which 15 were waited for; matrix products, arithmetic and copies ran while one was open for 0% of the time, Pallas kernels for 6%

profile of v5, /device:TPU:32, one launch (start us, length us, event | category | flops | bytes accessed | tf_op | source)
XLA Modules:
  0.0 167.0 jit_solution(6708333828360692773)
XLA Ops:
  0.6 3.9 %shard_map.76 = bf16[768,2048]{1,0:T(8,128)(2,1)} custom-call(s32[8,128]{1,0:T(8,128)} %bitcast.16, bf16[128,2048]{1,0:T(8,128)(2,1)} %refs_1_.1, bf16[1024,384]{1,0:T(8,128)(2,1)} %bitcast.20), custom_call_target="tpu_custom_call" | custom-call | flops 2000000000 | bytes 5000000 | tf_op jit(solution)/shard_map/pallas_call | solution.py:359
  4.5 13.3 %all-to-all-start = ((bf16[32,24,2048]{2,1,0:T(8,128)(2,1)}), bf16[32,24,2048]{2,1,0:T(8,128)(2,1)S(1)}, u32[]{:S(2)}, u32[]{:S(2)}) async-start(bf16[32,24,2048]{2,1,0:T(8,128)(2,1)} %bitcast.18), calls=%async_computation | async-start | bytes 6291456 | tf_op jit(solution)/shard_map/all_to_all | solution.py:345
  17.9 2.4 %collective-permute-start.6 = (bf16[128,768]{1,0:T(8,128)(2,1)S(1)}, bf16[128,768]{1,0:T(8,128)(2,1)S(1)}, u32[]{:S(2)}, u32[]{:S(2)}) collective-permute-start(bf16[128,768]{1,0:T(8,128)(2,1)S(1)} %shard_map.77.refs_0_), channel_id=1, source_target_pairs={{0,448},{32,480},{64,0},{96,32},{128,64},{160,96},{192,128},{224,1... | collective-permute-start | bytes 589832 | tf_op jit(solution)/shard_map/ppermute | solution.py:354
  20.2 2.2 %collective-permute-start.5 = (bf16[128,768]{1,0:T(8,128)(2,1)S(1)}, bf16[128,768]{1,0:T(8,128)(2,1)S(1)}, u32[]{:S(2)}, u32[]{:S(2)}) collective-permute-start(bf16[128,768]{1,0:T(8,128)(2,1)S(1)} %shard_map.77.refs_0_), channel_id=1, source_target_pairs={{0,384},{32,416},{64,448},{96,480},{128,0},{160,32},{192,64},{224,... | collective-permute-start | bytes 589832 | tf_op jit(solution)/shard_map/ppermute | solution.py:354
  22.5 6.0 %collective-permute-start.4 = (bf16[128,768]{1,0:T(8,128)(2,1)S(1)}, bf16[128,768]{1,0:T(8,128)(2,1)}, u32[]{:S(2)}, u32[]{:S(2)}) collective-permute-start(bf16[128,768]{1,0:T(8,128)(2,1)S(1)} %shard_map.77.refs_0_), channel_id=1, source_target_pairs={{0,320},{32,352},{64,384},{96,416},{128,448},{160,480},{192,0},{22... | collective-permute-start | bytes 589832 | tf_op jit(solution)/shard_map/ppermute | solution.py:354
  28.6 3.8 %collective-permute-start.3 = (bf16[128,768]{1,0:T(8,128)(2,1)S(1)}, bf16[128,768]{1,0:T(8,128)(2,1)}, u32[]{:S(2)}, u32[]{:S(2)}) collective-permute-start(bf16[128,768]{1,0:T(8,128)(2,1)S(1)} %shard_map.77.refs_0_), channel_id=1, source_target_pairs={{0,256},{32,288},{64,320},{96,352},{128,384},{160,416},{192,448},{... | collective-permute-start | bytes 589832 | tf_op jit(solution)/shard_map/ppermute | solution.py:354
  32.4 4.6 %collective-permute-start.2 = (bf16[128,768]{1,0:T(8,128)(2,1)S(1)}, bf16[128,768]{1,0:T(8,128)(2,1)}, u32[]{:S(2)}, u32[]{:S(2)}) collective-permute-start(bf16[128,768]{1,0:T(8,128)(2,1)S(1)} %shard_map.77.refs_0_), channel_id=1, source_target_pairs={{0,192},{32,224},{64,256},{96,288},{128,320},{160,352},{192,384},{... | collective-permute-start | bytes 589832 | tf_op jit(solution)/shard_map/ppermute | solution.py:354
  37.0 3.9 %collective-permute-start.1 = (bf16[128,768]{1,0:T(8,128)(2,1)S(1)}, bf16[128,768]{1,0:T(8,128)(2,1)}, u32[]{:S(2)}, u32[]{:S(2)}) collective-permute-start(bf16[128,768]{1,0:T(8,128)(2,1)S(1)} %shard_map.77.refs_0_), channel_id=1, source_target_pairs={{0,128},{32,160},{64,192},{96,224},{128,256},{160,288},{192,320},{... | collective-permute-start | bytes 589832 | tf_op jit(solution)/shard_map/ppermute | solution.py:354
  43.9 3.6 %collective-permute-done.4.refs_5_ = bf16[128,768]{1,0:T(8,128)(2,1)} collective-permute-done((bf16[128,768]{1,0:T(8,128)(2,1)S(1)}, bf16[128,768]{1,0:T(8,128)(2,1)}, u32[]{:S(2)}, u32[]{:S(2)}) %collective-permute-start.4) | collective-permute-done | bytes 196640 | tf_op jit(solution)/shard_map/ppermute | solution.py:354
  47.5 10.9 %collective-permute-done.2.refs_3_ = bf16[128,768]{1,0:T(8,128)(2,1)} collective-permute-done((bf16[128,768]{1,0:T(8,128)(2,1)S(1)}, bf16[128,768]{1,0:T(8,128)(2,1)}, u32[]{:S(2)}, u32[]{:S(2)}) %collective-permute-start.2) | collective-permute-done | bytes 196640 | tf_op jit(solution)/shard_map/ppermute | solution.py:354
  58.3 3.6 %collective-permute-done.1.refs_2_ = bf16[128,768]{1,0:T(8,128)(2,1)} collective-permute-done((bf16[128,768]{1,0:T(8,128)(2,1)S(1)}, bf16[128,768]{1,0:T(8,128)(2,1)}, u32[]{:S(2)}, u32[]{:S(2)}) %collective-permute-start.1) | collective-permute-done | bytes 196640 | tf_op jit(solution)/shard_map/ppermute | solution.py:354
  62.0 4.4 %collective-permute-done.refs_1_ = bf16[128,768]{1,0:T(8,128)(2,1)} collective-permute-done((bf16[128,768]{1,0:T(8,128)(2,1)S(1)}, bf16[128,768]{1,0:T(8,128)(2,1)}, u32[]{:S(2)}, u32[]{:S(2)}) %collective-permute-start) | collective-permute-done | bytes 196640 | tf_op jit(solution)/shard_map/ppermute | solution.py:354
  68.7 1.9 %collective-permute-start.7 = (bf16[1024,768]{1,0:T(8,128)(2,1)S(1)}, bf16[1024,768]{1,0:T(8,128)(2,1)S(1)}, u32[]{:S(2)}, u32[]{:S(2)}) collective-permute-start(bf16[1024,768]{1,0:T(8,128)(2,1)S(1)} %shard_map.78.refs_1_), channel_id=1, source_target_pairs={{0,32},{32,0},{64,96},{96,64},{128,160},{160,128},{192,224},{224,1... | collective-permute-start | bytes 4718600 | tf_op jit(solution)/shard_map/ppermute | solution.py:357
  70.6 3.4 %collective-permute-done.7.refs_2_ = bf16[1024,768]{1,0:T(8,128)(2,1)S(1)} collective-permute-done((bf16[1024,768]{1,0:T(8,128)(2,1)S(1)}, bf16[1024,768]{1,0:T(8,128)(2,1)S(1)}, u32[]{:S(2)}, u32[]{:S(2)}) %collective-permute-start.7) | collective-permute-done | bytes 1572896 | tf_op jit(solution)/shard_map/ppermute | solution.py:357
  76.4 13.7 %all-to-all-done = bf16[32,24,2048]{2,1,0:T(8,128)(2,1)S(1)} async-done(((bf16[32,24,2048]{2,1,0:T(8,128)(2,1)}), bf16[32,24,2048]{2,1,0:T(8,128)(2,1)S(1)}, u32[]{:S(2)}, u32[]{:S(2)}) %all-to-all-start) | async-done | bytes 3145760 | tf_op jit(solution)/shard_map/all_to_all | solution.py:345
  90.1 7.7 %shard_map.80 = (bf16[768,768]{1,0:T(8,128)(2,1)}, bf16[1280,1024]{1,0:T(8,128)(2,1)}, bf16[768,2048]{1,0:T(8,128)(2,1)}) custom-call(bf16[768,2048]{1,0:T(8,128)(2,1)S(1)} %bitcast.12, bf16[2048,768]{1,0:T(8,128)(2,1)} %copy-done), custom_call_target="tpu_custom_call" | custom-call | flops 5000000000 | bytes 10000000 | tf_op jit(solution)/shard_map/pallas_call | solution.py:400
  97.8 6.3 %all-to-all-start.1 = ((bf16[32,40,1024]{2,1,0:T(8,128)(2,1)}), bf16[32,40,1024]{2,1,0:T(8,128)(2,1)S(1)}, u32[]{:S(2)}, u32[]{:S(2)}) async-start(bf16[32,40,1024]{2,1,0:T(8,128)(2,1)} %bitcast.19), calls=%async_computation.1 | async-start | bytes 5242880 | tf_op jit(solution)/shard_map/all_to_all | solution.py:345
  107.3 2.0 %shard_map.83 = bf16[1024,768]{1,0:T(8,128)(2,1)S(1)} custom-call(s32[2]{0:T(128)S(1)} %pad_add_fusion.place_ref.refs_0_, bf16[768,2048]{1,0:T(8,128)(2,1)S(1)} %copy-done.6, bf16[768,768]{1,0:T(8,128)(2,1)S(1)} %copy-done.7), custom_call_target="tpu_custom_call" | custom-call | flops 2000000000 | bytes 5000000 | tf_op jit(solution)/shard_map/pallas_call | solution.py:423
  109.3 1.9 %collective-permute-start.8 = (bf16[1024,768]{1,0:T(8,128)(2,1)S(1)}, bf16[1024,768]{1,0:T(8,128)(2,1)S(1)}, u32[]{:S(2)}, u32[]{:S(2)}) collective-permute-start(bf16[1024,768]{1,0:T(8,128)(2,1)S(1)} %shard_map.83), channel_id=1, source_target_pairs={{0,32},{32,0},{64,96},{96,64},{128,160},{160,128},{192,224},{224,1... | collective-permute-start | bytes 4718600 | tf_op jit(solution)/shard_map/ppermute | solution.py:357
  111.2 2.0 %shard_map.82.mine_ref = bf16[1024,768]{1,0:T(8,128)(2,1)S(1)} custom-call(s32[2]{0:T(128)S(1)} %pad_add_fusion.place_ref.refs_0_, bf16[768,2048]{1,0:T(8,128)(2,1)S(1)} %copy-done.6, bf16[768,768]{1,0:T(8,128)(2,1)S(1)} %copy-done.7), custom_call_target="tpu_custom_call" | custom-call | flops 2000000000 | bytes 5000000 | tf_op jit(solution)/shard_map/pallas_call | solution.py:423
  116.0 2.6 %collective-permute-start.9 = (bf16[128,768]{1,0:T(8,128)(2,1)S(1)}, bf16[128,768]{1,0:T(8,128)(2,1)S(1)}, u32[]{:S(2)}, u32[]{:S(2)}) collective-permute-start(bf16[128,768]{1,0:T(8,128)(2,1)S(1)} %get-tuple-element.19), channel_id=1, source_target_pairs={{0,64},{32,96},{64,128},{96,160},{128,192},{160,224},{192,256},{22... | collective-permute-start | bytes 589832 | tf_op jit(solution)/shard_map/ppermute | solution.py:354
  118.6 4.5 %collective-permute-start.10 = (bf16[128,768]{1,0:T(8,128)(2,1)S(1)}, bf16[128,768]{1,0:T(8,128)(2,1)S(1)}, u32[]{:S(2)}, u32[]{:S(2)}) collective-permute-start(bf16[128,768]{1,0:T(8,128)(2,1)S(1)} %get-tuple-element.20), channel_id=1, source_target_pairs={{0,448},{32,480},{64,0},{96,32},{128,64},{160,96},{192,128},{224,1... | collective-permute-start | bytes 589832 | tf_op jit(solution)/shard_map/ppermute | solution.py:354
  123.0 3.0 %collective-permute-done.9.refs_2_ = bf16[128,768]{1,0:T(8,128)(2,1)S(1)} collective-permute-done((bf16[128,768]{1,0:T(8,128)(2,1)S(1)}, bf16[128,768]{1,0:T(8,128)(2,1)S(1)}, u32[]{:S(2)}, u32[]{:S(2)}) %collective-permute-start.9) | collective-permute-done | bytes 196640 | tf_op jit(solution)/shard_map/ppermute | solution.py:354
  127.8 2.5 %collective-permute-start.11 = (bf16[128,768]{1,0:T(8,128)(2,1)S(1)}, bf16[128,768]{1,0:T(8,128)(2,1)S(1)}, u32[]{:S(2)}, u32[]{:S(2)}) collective-permute-start(bf16[128,768]{1,0:T(8,128)(2,1)S(1)} %get-tuple-element.21), channel_id=1, source_target_pairs={{0,64},{32,96},{64,128},{96,160},{128,192},{160,224},{192,256},{22... | collective-permute-start | bytes 589832 | tf_op jit(solution)/shard_map/ppermute | solution.py:354
  130.3 5.0 %collective-permute-start.12 = (bf16[128,768]{1,0:T(8,128)(2,1)S(1)}, bf16[128,768]{1,0:T(8,128)(2,1)S(1)}, u32[]{:S(2)}, u32[]{:S(2)}) collective-permute-start(bf16[128,768]{1,0:T(8,128)(2,1)S(1)} %get-tuple-element.22), channel_id=1, source_target_pairs={{0,448},{32,480},{64,0},{96,32},{128,64},{160,96},{192,128},{224,1... | collective-permute-start | bytes 589832 | tf_op jit(solution)/shard_map/ppermute | solution.py:354
  135.4 2.1 %collective-permute-done.11.refs_2_ = bf16[128,768]{1,0:T(8,128)(2,1)S(1)} collective-permute-done((bf16[128,768]{1,0:T(8,128)(2,1)S(1)}, bf16[128,768]{1,0:T(8,128)(2,1)S(1)}, u32[]{:S(2)}, u32[]{:S(2)}) %collective-permute-start.11) | collective-permute-done | bytes 196640 | tf_op jit(solution)/shard_map/ppermute | solution.py:354
  139.3 1.9 %collective-permute-start.13 = (bf16[128,768]{1,0:T(8,128)(2,1)S(1)}, bf16[128,768]{1,0:T(8,128)(2,1)S(1)}, u32[]{:S(2)}, u32[]{:S(2)}) collective-permute-start(bf16[128,768]{1,0:T(8,128)(2,1)S(1)} %get-tuple-element.23), channel_id=1, source_target_pairs={{0,64},{32,96},{64,128},{96,160},{128,192},{160,224},{192,256},{22... | collective-permute-start | bytes 589832 | tf_op jit(solution)/shard_map/ppermute | solution.py:354
  141.2 5.6 %collective-permute-start.15 = (bf16[128,768]{1,0:T(8,128)(2,1)S(1)}, bf16[128,768]{1,0:T(8,128)(2,1)S(1)}, u32[]{:S(2)}, u32[]{:S(2)}) collective-permute-start(bf16[128,768]{1,0:T(8,128)(2,1)S(1)} %get-tuple-element.24), channel_id=1, source_target_pairs={{0,448},{32,480},{64,0},{96,32},{128,64},{160,96},{192,128},{224,1... | collective-permute-start | bytes 589832 | tf_op jit(solution)/shard_map/ppermute | solution.py:354
  149.2 1.9 %collective-permute-start.14 = (bf16[128,768]{1,0:T(8,128)(2,1)S(1)}, bf16[128,768]{1,0:T(8,128)(2,1)S(1)}, u32[]{:S(2)}, u32[]{:S(2)}) collective-permute-start(bf16[128,768]{1,0:T(8,128)(2,1)S(1)} %shard_map.87), channel_id=1, source_target_pairs={{0,64},{32,96},{64,128},{96,160},{128,192},{160,224},{192,256},{22... | collective-permute-start | bytes 589832 | tf_op jit(solution)/shard_map/ppermute | solution.py:354
  151.1 6.8 %collective-permute-done.14.refs_2_ = bf16[128,768]{1,0:T(8,128)(2,1)S(1)} collective-permute-done((bf16[128,768]{1,0:T(8,128)(2,1)S(1)}, bf16[128,768]{1,0:T(8,128)(2,1)S(1)}, u32[]{:S(2)}, u32[]{:S(2)}) %collective-permute-start.14) | collective-permute-done | bytes 196640 | tf_op jit(solution)/shard_map/ppermute | solution.py:354
  159.3 5.7 %all-to-all-done.1 = bf16[32,40,1024]{2,1,0:T(8,128)(2,1)S(1)} async-done(((bf16[32,40,1024]{2,1,0:T(8,128)(2,1)}), bf16[32,40,1024]{2,1,0:T(8,128)(2,1)S(1)}, u32[]{:S(2)}, u32[]{:S(2)}) %all-to-all-start.1) | async-done | bytes 2621472 | tf_op jit(solution)/shard_map/all_to_all | solution.py:345
  165.0 2.0 %shard_map.81 = bf16[128,2048]{1,0:T(8,128)(2,1)} custom-call(s32[8,128]{1,0:T(8,128)S(1)} %bitcast.17, bf16[1280,1024]{1,0:T(8,128)(2,1)S(1)} %bitcast.13), custom_call_target="tpu_custom_call" | custom-call | flops 1000000000 | bytes 4000000 | tf_op jit(solution)/shard_map/pallas_call | solution.py:470
  (34 shorter events, 20.9 us)
Async XLA Ops:
  4.5 13.3 %copy-start.3 = (bf16[1,128,384]{2,1,0:T(8,128)(2,1)S(1)}, bf16[1,128,384]{2,1,0:T(8,128)(2,1)}, u32[]{:S(2)}) copy-start(bf16[1,128,384]{2,1,0:T(8,128)(2,1)} %param.8) | copy-start | bytes 294916
  4.5 13.3 %copy-start.4 = (bf16[1,128,384]{2,1,0:T(8,128)(2,1)S(1)}, bf16[1,128,384]{2,1,0:T(8,128)(2,1)}, u32[]{:S(2)}) copy-start(bf16[1,128,384]{2,1,0:T(8,128)(2,1)} %param.9) | copy-start | bytes 294916
  4.5 85.6 %all-to-all-start = ((bf16[32,24,2048]{2,1,0:T(8,128)(2,1)}), bf16[32,24,2048]{2,1,0:T(8,128)(2,1)S(1)}, u32[]{:S(2)}, u32[]{:S(2)}) async-start(bf16[32,24,2048]{2,1,0:T(8,128)(2,1)} %bitcast.18), calls=%async_computation | async-start | bytes 6291456 | tf_op jit(solution)/shard_map/all_to_all | solution.py:345
  17.9 19.1 %collective-permute-start.6 = (bf16[128,768]{1,0:T(8,128)(2,1)S(1)}, bf16[128,768]{1,0:T(8,128)(2,1)S(1)}, u32[]{:S(2)}, u32[]{:S(2)}) collective-permute-start(bf16[128,768]{1,0:T(8,128)(2,1)S(1)} %shard_map.77.refs_0_), channel_id=1, source_target_pairs={{0,448},{32,480},{64,0},{96,32},{128,64},{160,96},{192,128},{224,1... | collective-permute-start | bytes 589832 | tf_op jit(solution)/shard_map/ppermute | solution.py:354
  20.2 20.9 %collective-permute-start.5 = (bf16[128,768]{1,0:T(8,128)(2,1)S(1)}, bf16[128,768]{1,0:T(8,128)(2,1)S(1)}, u32[]{:S(2)}, u32[]{:S(2)}) collective-permute-start(bf16[128,768]{1,0:T(8,128)(2,1)S(1)} %shard_map.77.refs_0_), channel_id=1, source_target_pairs={{0,384},{32,416},{64,448},{96,480},{128,0},{160,32},{192,64},{224,... | collective-permute-start | bytes 589832 | tf_op jit(solution)/shard_map/ppermute | solution.py:354
  22.5 25.0 %collective-permute-start.4 = (bf16[128,768]{1,0:T(8,128)(2,1)S(1)}, bf16[128,768]{1,0:T(8,128)(2,1)}, u32[]{:S(2)}, u32[]{:S(2)}) collective-permute-start(bf16[128,768]{1,0:T(8,128)(2,1)S(1)} %shard_map.77.refs_0_), channel_id=1, source_target_pairs={{0,320},{32,352},{64,384},{96,416},{128,448},{160,480},{192,0},{22... | collective-permute-start | bytes 589832 | tf_op jit(solution)/shard_map/ppermute | solution.py:354
  28.6 18.9 %collective-permute-start.3 = (bf16[128,768]{1,0:T(8,128)(2,1)S(1)}, bf16[128,768]{1,0:T(8,128)(2,1)}, u32[]{:S(2)}, u32[]{:S(2)}) collective-permute-start(bf16[128,768]{1,0:T(8,128)(2,1)S(1)} %shard_map.77.refs_0_), channel_id=1, source_target_pairs={{0,256},{32,288},{64,320},{96,352},{128,384},{160,416},{192,448},{... | collective-permute-start | bytes 589832 | tf_op jit(solution)/shard_map/ppermute | solution.py:354
  32.4 26.0 %collective-permute-start.2 = (bf16[128,768]{1,0:T(8,128)(2,1)S(1)}, bf16[128,768]{1,0:T(8,128)(2,1)}, u32[]{:S(2)}, u32[]{:S(2)}) collective-permute-start(bf16[128,768]{1,0:T(8,128)(2,1)S(1)} %shard_map.77.refs_0_), channel_id=1, source_target_pairs={{0,192},{32,224},{64,256},{96,288},{128,320},{160,352},{192,384},{... | collective-permute-start | bytes 589832 | tf_op jit(solution)/shard_map/ppermute | solution.py:354
  37.0 25.0 %collective-permute-start.1 = (bf16[128,768]{1,0:T(8,128)(2,1)S(1)}, bf16[128,768]{1,0:T(8,128)(2,1)}, u32[]{:S(2)}, u32[]{:S(2)}) collective-permute-start(bf16[128,768]{1,0:T(8,128)(2,1)S(1)} %shard_map.77.refs_0_), channel_id=1, source_target_pairs={{0,128},{32,160},{64,192},{96,224},{128,256},{160,288},{192,320},{... | collective-permute-start | bytes 589832 | tf_op jit(solution)/shard_map/ppermute | solution.py:354
  41.2 0.7 copy-start.1
  41.9 24.5 %collective-permute-start = (bf16[128,768]{1,0:T(8,128)(2,1)S(1)}, bf16[128,768]{1,0:T(8,128)(2,1)}, u32[]{:S(2)}, u32[]{:S(2)}) collective-permute-start(bf16[128,768]{1,0:T(8,128)(2,1)S(1)} %shard_map.77.refs_0_), channel_id=1, source_target_pairs={{0,64},{32,96},{64,128},{96,160},{128,192},{160,224},{192,256},{22... | collective-permute-start | bytes 589832 | tf_op jit(solution)/shard_map/ppermute | solution.py:354
  66.3 0.9 copy-start.2
  68.7 5.3 %collective-permute-start.7 = (bf16[1024,768]{1,0:T(8,128)(2,1)S(1)}, bf16[1024,768]{1,0:T(8,128)(2,1)S(1)}, u32[]{:S(2)}, u32[]{:S(2)}) collective-permute-start(bf16[1024,768]{1,0:T(8,128)(2,1)S(1)} %shard_map.78.refs_1_), channel_id=1, source_target_pairs={{0,32},{32,0},{64,96},{96,64},{128,160},{160,128},{192,224},{224,1... | collective-permute-start | bytes 4718600 | tf_op jit(solution)/shard_map/ppermute | solution.py:357
  74.7 1.7 %copy-start = (bf16[2048,768]{1,0:T(8,128)(2,1)}, bf16[2048,768]{1,0:T(8,128)(2,1)S(1)}, u32[]{:S(2)}) copy-start(bf16[2048,768]{1,0:T(8,128)(2,1)S(1)} %shard_map.79.weight_hbm) | copy-start | bytes 9437188
  97.8 67.2 %all-to-all-start.1 = ((bf16[32,40,1024]{2,1,0:T(8,128)(2,1)}), bf16[32,40,1024]{2,1,0:T(8,128)(2,1)S(1)}, u32[]{:S(2)}, u32[]{:S(2)}) async-start(bf16[32,40,1024]{2,1,0:T(8,128)(2,1)} %bitcast.19), calls=%async_computation.1 | async-start | bytes 5242880 | tf_op jit(solution)/shard_map/all_to_all | solution.py:345
  104.1 1.9 %copy-start.6 = (bf16[768,2048]{1,0:T(8,128)(2,1)S(1)}, bf16[768,2048]{1,0:T(8,128)(2,1)}, u32[]{:S(2)}) copy-start(bf16[768,2048]{1,0:T(8,128)(2,1)} %get-tuple-element.16.refs_1_) | copy-start | bytes 9437188
  106.0 1.3 copy-start.7
  109.3 5.3 %collective-permute-start.8 = (bf16[1024,768]{1,0:T(8,128)(2,1)S(1)}, bf16[1024,768]{1,0:T(8,128)(2,1)S(1)}, u32[]{:S(2)}, u32[]{:S(2)}) collective-permute-start(bf16[1024,768]{1,0:T(8,128)(2,1)S(1)} %shard_map.83), channel_id=1, source_target_pairs={{0,32},{32,0},{64,96},{96,64},{128,160},{160,128},{192,224},{224,1... | collective-permute-start | bytes 4718600 | tf_op jit(solution)/shard_map/ppermute | solution.py:357
  116.0 10.0 %collective-permute-start.9 = (bf16[128,768]{1,0:T(8,128)(2,1)S(1)}, bf16[128,768]{1,0:T(8,128)(2,1)S(1)}, u32[]{:S(2)}, u32[]{:S(2)}) collective-permute-start(bf16[128,768]{1,0:T(8,128)(2,1)S(1)} %get-tuple-element.19), channel_id=1, source_target_pairs={{0,64},{32,96},{64,128},{96,160},{128,192},{160,224},{192,256},{22... | collective-permute-start | bytes 589832 | tf_op jit(solution)/shard_map/ppermute | solution.py:354
  118.6 8.6 %collective-permute-start.10 = (bf16[128,768]{1,0:T(8,128)(2,1)S(1)}, bf16[128,768]{1,0:T(8,128)(2,1)S(1)}, u32[]{:S(2)}, u32[]{:S(2)}) collective-permute-start(bf16[128,768]{1,0:T(8,128)(2,1)S(1)} %get-tuple-element.20), channel_id=1, source_target_pairs={{0,448},{32,480},{64,0},{96,32},{128,64},{160,96},{192,128},{224,1... | collective-permute-start | bytes 589832 | tf_op jit(solution)/shard_map/ppermute | solution.py:354
  127.8 9.6 %collective-permute-start.11 = (bf16[128,768]{1,0:T(8,128)(2,1)S(1)}, bf16[128,768]{1,0:T(8,128)(2,1)S(1)}, u32[]{:S(2)}, u32[]{:S(2)}) collective-permute-start(bf16[128,768]{1,0:T(8,128)(2,1)S(1)} %get-tuple-element.21), channel_id=1, source_target_pairs={{0,64},{32,96},{64,128},{96,160},{128,192},{160,224},{192,256},{22... | collective-permute-start | bytes 589832 | tf_op jit(solution)/shard_map/ppermute | solution.py:354
  130.3 8.3 %collective-permute-start.12 = (bf16[128,768]{1,0:T(8,128)(2,1)S(1)}, bf16[128,768]{1,0:T(8,128)(2,1)S(1)}, u32[]{:S(2)}, u32[]{:S(2)}) collective-permute-start(bf16[128,768]{1,0:T(8,128)(2,1)S(1)} %get-tuple-element.22), channel_id=1, source_target_pairs={{0,448},{32,480},{64,0},{96,32},{128,64},{160,96},{192,128},{224,1... | collective-permute-start | bytes 589832 | tf_op jit(solution)/shard_map/ppermute | solution.py:354
  139.3 9.2 %collective-permute-start.13 = (bf16[128,768]{1,0:T(8,128)(2,1)S(1)}, bf16[128,768]{1,0:T(8,128)(2,1)S(1)}, u32[]{:S(2)}, u32[]{:S(2)}) collective-permute-start(bf16[128,768]{1,0:T(8,128)(2,1)S(1)} %get-tuple-element.23), channel_id=1, source_target_pairs={{0,64},{32,96},{64,128},{96,160},{128,192},{160,224},{192,256},{22... | collective-permute-start | bytes 589832 | tf_op jit(solution)/shard_map/ppermute | solution.py:354
  141.2 23.8 %copy-start.5 = (s32[128,8]{0,1:T(8,128)S(1)}, s32[128,8]{0,1:T(8,128)}, u32[]{:S(2)}) copy-start(s32[128,8]{0,1:T(8,128)} %param.6) | copy-start | bytes 12292
  141.2 9.8 %collective-permute-start.15 = (bf16[128,768]{1,0:T(8,128)(2,1)S(1)}, bf16[128,768]{1,0:T(8,128)(2,1)S(1)}, u32[]{:S(2)}, u32[]{:S(2)}) collective-permute-start(bf16[128,768]{1,0:T(8,128)(2,1)S(1)} %get-tuple-element.24), channel_id=1, source_target_pairs={{0,448},{32,480},{64,0},{96,32},{128,64},{160,96},{192,128},{224,1... | collective-permute-start | bytes 589832 | tf_op jit(solution)/shard_map/ppermute | solution.py:354
  149.2 8.8 %collective-permute-start.14 = (bf16[128,768]{1,0:T(8,128)(2,1)S(1)}, bf16[128,768]{1,0:T(8,128)(2,1)S(1)}, u32[]{:S(2)}, u32[]{:S(2)}) collective-permute-start(bf16[128,768]{1,0:T(8,128)(2,1)S(1)} %shard_map.87), channel_id=1, source_target_pairs={{0,64},{32,96},{64,128},{96,160},{128,192},{160,224},{192,256},{22... | collective-permute-start | bytes 589832 | tf_op jit(solution)/shard_map/ppermute | solution.py:354

commit v6 on v5

--- a/solution.py
+++ b/solution.py
@@ -13,7 +13,7 @@
 STEPS = 2
 PIECES = 4
 CORES = 2
-FETCHES = 4
+FETCHES = (1, 2, 2, 3)
 VMEM = 32 * 2**20
 BIG = 60 * 2**20
 MIDDLE = 32 * 2**20
@@ -128,8 +128,7 @@
     stacked_ref[...] = jnp.concatenate((gate_ref[...], up_ref[...]), axis=1)
 
 
-def combine_kernel(experts, routes_ref, returned_ref, out_ref):
-    half = returned_ref.shape[1]
+def matrix_kernel(experts, routes_ref, after_ref, out_ref):
     _, place = ranks(routes_ref[...], experts)
     lane = iota((experts, experts * BACK), 1)
     first = iota((experts, experts * BACK), 0) * BACK
@@ -139,8 +138,12 @@
     low = jnp.where(within < CAP, within, -2.0)
     high = jnp.where(within < BLOCK, within - TAIL, within - BLOCK)
     high = jnp.where(within < CAP, -2.0, high)
-    both = jnp.concatenate((one_if(at == low), one_if(at == high)), axis=0)
-    total = dot(both, returned_ref[...])
+    out_ref[...] = jnp.concatenate((one_if(at == low), one_if(at == high)), axis=0)
+
+
+def combine_kernel(matrix_ref, returned_ref, out_ref):
+    half = returned_ref.shape[1]
+    total = dot(matrix_ref[...], returned_ref[...])
     count = out_ref.shape[0]
     out_ref[:, :half] = total[:count].astype(jnp.bfloat16)
     out_ref[:, half:] = total[count:].astype(jnp.bfloat16)
@@ -177,27 +180,28 @@
     width = received_ref.shape[1]
     half = width // 2
     full = BLOCK - 8
-    depth = width // FETCHES
+    unit = width // sum(FETCHES)
+    starts = [unit * sum(FETCHES[:k]) for k in range(len(FETCHES) + 1)]
     fetches, copies = [], []
-    for k in range(FETCHES):
-        at = pl.ds(k * depth, depth)
+    for k in range(len(FETCHES)):
+        at = pl.ds(starts[k], starts[k + 1] - starts[k])
         fetch = pltpu.make_async_copy(weight_hbm.at[at], weight_ref.at[at], in_sems.at[k])
         fetch.start()
         fetches.append(fetch)
     rows = received_ref.shape[0] // STEPS
     for k, fetch in enumerate(fetches):
         fetch.wait()
-        if k == FETCHES - 1:
+        if k == len(FETCHES) - 1:
             keep = pltpu.make_async_copy(received_ref, kept_hbm, kept_sem.at[0])
             keep.start()
             copies.append(keep)
-        at = slice(k * depth, (k + 1) * depth)
+        at = slice(starts[k], starts[k + 1])
         for step in range(STEPS):
             part = slice(step * rows, (step + 1) * rows)
             pre = dot(received_ref[part, at], weight_ref[at])
             if k:
                 pre += pre_ref[part]
-            if k < FETCHES - 1:
+            if k < len(FETCHES) - 1:
                 pre_ref[part] = pre
                 continue
             delta = make_deltas(received_ref[part], pre)
@@ -410,7 +414,7 @@
         in_specs=[whole(), anywhere()],
         out_specs=(anywhere(),) * 3,
         scratch_shapes=[
-            *held_and_sems((width, 2 * hidden), FETCHES),
+            *held_and_sems((width, 2 * hidden), len(FETCHES)),
             *held_and_sems((rows, 2 * hidden), STEPS),
             *held_and_sems((peers * BACK, half), PIECES),
             pltpu.VMEM((rows, 2 * hidden), jnp.float32),
@@ -467,14 +471,22 @@
         in_specs=[scalars] + [whole()] * 3,
         out_specs=(whole(), whole()),
     )(place, summed, up, down)
+    matrix = call(
+        lambda *refs: matrix_kernel(peers, *refs),
+        shape(2 * count, peers * BACK),
+        2 * 10**9,
+        10**6,
+        in_specs=[whole(), anywhere()],
+        out_specs=whole(),
+    )(routes, gate_grad)
     token_grad = call(
-        lambda *refs: combine_kernel(peers, *refs),
+        combine_kernel,
         shape(count, width),
         10**9,
         4 * 10**6,
         in_specs=[whole()] * 2,
         out_specs=whole(),
-    )(routes, returned)
+    )(matrix, returned)
     return (token_grad, gate_grad[None], up_grad[None])
 
 

time: 168 us -> 167 us (level)
  the two profiles are of different devices: /device:TPU:32 before, /device:TPU:8 now
where the time goes in v6:
time: 167 us; the launch traced here: 166 us
  starting transfers between devices  73.8 us (44%)
  waiting for transfers between devices  60 us (36%)
  Pallas kernels  24.2 us (14%)
  local copies, waits for them, and re-layouts  7.38 us (4%)
    ppermute x14, starting transfers between devices, along_y(): return lax.ppermute(block, 'dp', pairs)  50.2 us
    ppermute x14, waiting for transfers between devices, along_y(): return lax.ppermute(block, 'dp', pairs)  41.2 us
    all_to_all x2, starting transfers between devices, exchange(): lax.all_to_all(block.reshape(peers, size, -1), 'expert', split_axis=0, co...  19.6 us
    all_to_all x2, waiting for transfers between devices, exchange(): lax.all_to_all(block.reshape(peers, size, -1), 'expert', split_axis=0, co...  14.2 us
    pallas_call x1, Pallas kernels, on_device(): call(middle_kernel, (pltpu.HBM((rows, 2 * hidden), bf16), pltpu.HBM((peer...  7.49 us
    unnamed x18, local copies, waits for them, and re-layouts  7.38 us
    ppermute x2, waiting for transfers between devices, other_core(): return lax.ppermute(block, 'dp', [(d, d ^ 1) for d in range(groups)])  4.6 us
    ppermute x2, starting transfers between devices, other_core(): return lax.ppermute(block, 'dp', [(d, d ^ 1) for d in range(groups)])  4.02 us
  transfers between devices with their start and end apart: 18, of which 14 were waited for; matrix products, arithmetic and copies ran while one was open for 0% of the time, Pallas kernels for 7%

profile of v6, /device:TPU:8, one launch (start us, length us, event | category | flops | bytes accessed | tf_op | source)
XLA Modules:
  0.0 166.5 jit_solution(6580194704581729109)
XLA Ops:
  0.6 3.9 %shard_map.76 = bf16[768,2048]{1,0:T(8,128)(2,1)} custom-call(s32[8,128]{1,0:T(8,128)} %bitcast.17, bf16[128,2048]{1,0:T(8,128)(2,1)} %refs_1_.1, bf16[1024,384]{1,0:T(8,128)(2,1)} %bitcast.21), custom_call_target="tpu_custom_call" | custom-call | flops 2000000000 | bytes 5000000 | tf_op jit(solution)/shard_map/pallas_call | solution.py:363
  4.5 13.3 %all-to-all-start = ((bf16[32,24,2048]{2,1,0:T(8,128)(2,1)}), bf16[32,24,2048]{2,1,0:T(8,128)(2,1)S(1)}, u32[]{:S(2)}, u32[]{:S(2)}) async-start(bf16[32,24,2048]{2,1,0:T(8,128)(2,1)} %bitcast.19), calls=%async_computation | async-start | bytes 6291456 | tf_op jit(solution)/shard_map/all_to_all | solution.py:349
  17.9 2.4 %collective-permute-start.6 = (bf16[128,768]{1,0:T(8,128)(2,1)S(1)}, bf16[128,768]{1,0:T(8,128)(2,1)S(1)}, u32[]{:S(2)}, u32[]{:S(2)}) collective-permute-start(bf16[128,768]{1,0:T(8,128)(2,1)S(1)} %shard_map.77.refs_0_), channel_id=1, source_target_pairs={{0,448},{32,480},{64,0},{96,32},{128,64},{160,96},{192,128},{224,1... | collective-permute-start | bytes 589832 | tf_op jit(solution)/shard_map/ppermute | solution.py:358
  20.3 6.2 %collective-permute-start.5 = (bf16[128,768]{1,0:T(8,128)(2,1)S(1)}, bf16[128,768]{1,0:T(8,128)(2,1)S(1)}, u32[]{:S(2)}, u32[]{:S(2)}) collective-permute-start(bf16[128,768]{1,0:T(8,128)(2,1)S(1)} %shard_map.77.refs_0_), channel_id=1, source_target_pairs={{0,384},{32,416},{64,448},{96,480},{128,0},{160,32},{192,64},{224,... | collective-permute-start | bytes 589832 | tf_op jit(solution)/shard_map/ppermute | solution.py:358
  26.4 3.9 %collective-permute-start.4 = (bf16[128,768]{1,0:T(8,128)(2,1)S(1)}, bf16[128,768]{1,0:T(8,128)(2,1)}, u32[]{:S(2)}, u32[]{:S(2)}) collective-permute-start(bf16[128,768]{1,0:T(8,128)(2,1)S(1)} %shard_map.77.refs_0_), channel_id=1, source_target_pairs={{0,320},{32,352},{64,384},{96,416},{128,448},{160,480},{192,0},{22... | collective-permute-start | bytes 589832 | tf_op jit(solution)/shard_map/ppermute | solution.py:358
  30.4 5.0 %collective-permute-start.3 = (bf16[128,768]{1,0:T(8,128)(2,1)S(1)}, bf16[128,768]{1,0:T(8,128)(2,1)}, u32[]{:S(2)}, u32[]{:S(2)}) collective-permute-start(bf16[128,768]{1,0:T(8,128)(2,1)S(1)} %shard_map.77.refs_0_), channel_id=1, source_target_pairs={{0,256},{32,288},{64,320},{96,352},{128,384},{160,416},{192,448},{... | collective-permute-start | bytes 589832 | tf_op jit(solution)/shard_map/ppermute | solution.py:358
  35.4 3.7 %collective-permute-start.2 = (bf16[128,768]{1,0:T(8,128)(2,1)S(1)}, bf16[128,768]{1,0:T(8,128)(2,1)}, u32[]{:S(2)}, u32[]{:S(2)}) collective-permute-start(bf16[128,768]{1,0:T(8,128)(2,1)S(1)} %shard_map.77.refs_0_), channel_id=1, source_target_pairs={{0,192},{32,224},{64,256},{96,288},{128,320},{160,352},{192,384},{... | collective-permute-start | bytes 589832 | tf_op jit(solution)/shard_map/ppermute | solution.py:358
  39.2 4.5 %collective-permute-start.1 = (bf16[128,768]{1,0:T(8,128)(2,1)S(1)}, bf16[128,768]{1,0:T(8,128)(2,1)}, u32[]{:S(2)}, u32[]{:S(2)}) collective-permute-start(bf16[128,768]{1,0:T(8,128)(2,1)S(1)} %shard_map.77.refs_0_), channel_id=1, source_target_pairs={{0,128},{32,160},{64,192},{96,224},{128,256},{160,288},{192,320},{... | collective-permute-start | bytes 589832 | tf_op jit(solution)/shard_map/ppermute | solution.py:358
  44.3 2.6 %collective-permute-start = (bf16[128,768]{1,0:T(8,128)(2,1)S(1)}, bf16[128,768]{1,0:T(8,128)(2,1)}, u32[]{:S(2)}, u32[]{:S(2)}) collective-permute-start(bf16[128,768]{1,0:T(8,128)(2,1)S(1)} %shard_map.77.refs_0_), channel_id=1, source_target_pairs={{0,64},{32,96},{64,128},{96,160},{128,192},{160,224},{192,256},{22... | collective-permute-start | bytes 589832 | tf_op jit(solution)/shard_map/ppermute | solution.py:358
  47.0 4.7 %collective-permute-done.4.refs_5_ = bf16[128,768]{1,0:T(8,128)(2,1)} collective-permute-done((bf16[128,768]{1,0:T(8,128)(2,1)S(1)}, bf16[128,768]{1,0:T(8,128)(2,1)}, u32[]{:S(2)}, u32[]{:S(2)}) %collective-permute-start.4) | collective-permute-done | bytes 196640 | tf_op jit(solution)/shard_map/ppermute | solution.py:358
  51.8 8.2 %collective-permute-done.3.refs_4_ = bf16[128,768]{1,0:T(8,128)(2,1)} collective-permute-done((bf16[128,768]{1,0:T(8,128)(2,1)S(1)}, bf16[128,768]{1,0:T(8,128)(2,1)}, u32[]{:S(2)}, u32[]{:S(2)}) %collective-permute-start.3) | collective-permute-done | bytes 196640 | tf_op jit(solution)/shard_map/ppermute | solution.py:358
  60.0 7.0 %collective-permute-done.1.refs_2_ = bf16[128,768]{1,0:T(8,128)(2,1)} collective-permute-done((bf16[128,768]{1,0:T(8,128)(2,1)S(1)}, bf16[128,768]{1,0:T(8,128)(2,1)}, u32[]{:S(2)}, u32[]{:S(2)}) %collective-permute-start.1) | collective-permute-done | bytes 196640 | tf_op jit(solution)/shard_map/ppermute | solution.py:358
  67.0 2.9 %collective-permute-done.refs_1_ = bf16[128,768]{1,0:T(8,128)(2,1)} collective-permute-done((bf16[128,768]{1,0:T(8,128)(2,1)S(1)}, bf16[128,768]{1,0:T(8,128)(2,1)}, u32[]{:S(2)}, u32[]{:S(2)}) %collective-permute-start) | collective-permute-done | bytes 196640 | tf_op jit(solution)/shard_map/ppermute | solution.py:358
  72.3 1.9 %collective-permute-start.7 = (bf16[1024,768]{1,0:T(8,128)(2,1)S(1)}, bf16[1024,768]{1,0:T(8,128)(2,1)S(1)}, u32[]{:S(2)}, u32[]{:S(2)}) collective-permute-start(bf16[1024,768]{1,0:T(8,128)(2,1)S(1)} %shard_map.78.refs_1_), channel_id=1, source_target_pairs={{0,32},{32,0},{64,96},{96,64},{128,160},{160,128},{192,224},{224,1... | collective-permute-start | bytes 4718600 | tf_op jit(solution)/shard_map/ppermute | solution.py:361
  74.2 3.4 %collective-permute-done.7.refs_2_ = bf16[1024,768]{1,0:T(8,128)(2,1)S(1)} collective-permute-done((bf16[1024,768]{1,0:T(8,128)(2,1)S(1)}, bf16[1024,768]{1,0:T(8,128)(2,1)S(1)}, u32[]{:S(2)}, u32[]{:S(2)}) %collective-permute-start.7) | collective-permute-done | bytes 1572896 | tf_op jit(solution)/shard_map/ppermute | solution.py:361
  80.0 10.1 %all-to-all-done = bf16[32,24,2048]{2,1,0:T(8,128)(2,1)S(1)} async-done(((bf16[32,24,2048]{2,1,0:T(8,128)(2,1)}), bf16[32,24,2048]{2,1,0:T(8,128)(2,1)S(1)}, u32[]{:S(2)}, u32[]{:S(2)}) %all-to-all-start) | async-done | bytes 3145760 | tf_op jit(solution)/shard_map/all_to_all | solution.py:349
  90.1 7.5 %shard_map.80 = (bf16[768,768]{1,0:T(8,128)(2,1)}, bf16[1280,1024]{1,0:T(8,128)(2,1)}, bf16[768,2048]{1,0:T(8,128)(2,1)}) custom-call(bf16[768,2048]{1,0:T(8,128)(2,1)S(1)} %bitcast.13, bf16[2048,768]{1,0:T(8,128)(2,1)} %copy-done), custom_call_target="tpu_custom_call" | custom-call | flops 5000000000 | bytes 10000000 | tf_op jit(solution)/shard_map/pallas_call | solution.py:404
  97.6 6.3 %all-to-all-start.1 = ((bf16[32,40,1024]{2,1,0:T(8,128)(2,1)}), bf16[32,40,1024]{2,1,0:T(8,128)(2,1)S(1)}, u32[]{:S(2)}, u32[]{:S(2)}) async-start(bf16[32,40,1024]{2,1,0:T(8,128)(2,1)} %bitcast.20), calls=%async_computation.1 | async-start | bytes 5242880 | tf_op jit(solution)/shard_map/all_to_all | solution.py:349
  107.1 2.0 %shard_map.82 = bf16[1024,768]{1,0:T(8,128)(2,1)S(1)} custom-call(s32[2]{0:T(128)S(1)} %pad_add_fusion.place_ref.refs_0_, bf16[768,2048]{1,0:T(8,128)(2,1)S(1)} %copy-done.7, bf16[768,768]{1,0:T(8,128)(2,1)S(1)} %copy-done.8), custom_call_target="tpu_custom_call" | custom-call | flops 2000000000 | bytes 5000000 | tf_op jit(solution)/shard_map/pallas_call | solution.py:427
  109.1 2.1 %collective-permute-start.8 = (bf16[1024,768]{1,0:T(8,128)(2,1)S(1)}, bf16[1024,768]{1,0:T(8,128)(2,1)S(1)}, u32[]{:S(2)}, u32[]{:S(2)}) collective-permute-start(bf16[1024,768]{1,0:T(8,128)(2,1)S(1)} %shard_map.82), channel_id=1, source_target_pairs={{0,32},{32,0},{64,96},{96,64},{128,160},{160,128},{192,224},{224,1... | collective-permute-start | bytes 4718600 | tf_op jit(solution)/shard_map/ppermute | solution.py:361
  111.2 2.0 %shard_map.81.mine_ref = bf16[1024,768]{1,0:T(8,128)(2,1)S(1)} custom-call(s32[2]{0:T(128)S(1)} %pad_add_fusion.place_ref.refs_0_, bf16[768,2048]{1,0:T(8,128)(2,1)S(1)} %copy-done.7, bf16[768,768]{1,0:T(8,128)(2,1)S(1)} %copy-done.8), custom_call_target="tpu_custom_call" | custom-call | flops 2000000000 | bytes 5000000 | tf_op jit(solution)/shard_map/pallas_call | solution.py:427
  115.8 3.5 %collective-permute-start.9 = (bf16[128,768]{1,0:T(8,128)(2,1)S(1)}, bf16[128,768]{1,0:T(8,128)(2,1)S(1)}, u32[]{:S(2)}, u32[]{:S(2)}) collective-permute-start(bf16[128,768]{1,0:T(8,128)(2,1)S(1)} %get-tuple-element.18), channel_id=1, source_target_pairs={{0,64},{32,96},{64,128},{96,160},{128,192},{160,224},{192,256},{22... | collective-permute-start | bytes 589832 | tf_op jit(solution)/shard_map/ppermute | solution.py:358
  119.3 2.4 %collective-permute-start.10 = (bf16[128,768]{1,0:T(8,128)(2,1)S(1)}, bf16[128,768]{1,0:T(8,128)(2,1)S(1)}, u32[]{:S(2)}, u32[]{:S(2)}) collective-permute-start(bf16[128,768]{1,0:T(8,128)(2,1)S(1)} %get-tuple-element.19), channel_id=1, source_target_pairs={{0,448},{32,480},{64,0},{96,32},{128,64},{160,96},{192,128},{224,1... | collective-permute-start | bytes 589832 | tf_op jit(solution)/shard_map/ppermute | solution.py:358
  121.7 3.0 %collective-permute-done.9.refs_2_ = bf16[128,768]{1,0:T(8,128)(2,1)S(1)} collective-permute-done((bf16[128,768]{1,0:T(8,128)(2,1)S(1)}, bf16[128,768]{1,0:T(8,128)(2,1)S(1)}, u32[]{:S(2)}, u32[]{:S(2)}) %collective-permute-start.9) | collective-permute-done | bytes 196640 | tf_op jit(solution)/shard_map/ppermute | solution.py:358
  124.7 3.2 %collective-permute-done.10.refs_3_ = bf16[128,768]{1,0:T(8,128)(2,1)S(1)} collective-permute-done((bf16[128,768]{1,0:T(8,128)(2,1)S(1)}, bf16[128,768]{1,0:T(8,128)(2,1)S(1)}, u32[]{:S(2)}, u32[]{:S(2)}) %collective-permute-start.10) | collective-permute-done | bytes 196640 | tf_op jit(solution)/shard_map/ppermute | solution.py:358
  128.5 4.5 %collective-permute-start.11 = (bf16[128,768]{1,0:T(8,128)(2,1)S(1)}, bf16[128,768]{1,0:T(8,128)(2,1)S(1)}, u32[]{:S(2)}, u32[]{:S(2)}) collective-permute-start(bf16[128,768]{1,0:T(8,128)(2,1)S(1)} %get-tuple-element.20), channel_id=1, source_target_pairs={{0,64},{32,96},{64,128},{96,160},{128,192},{160,224},{192,256},{22... | collective-permute-start | bytes 589832 | tf_op jit(solution)/shard_map/ppermute | solution.py:358
  136.7 5.0 %collective-permute-done.12.refs_3_ = bf16[128,768]{1,0:T(8,128)(2,1)S(1)} collective-permute-done((bf16[128,768]{1,0:T(8,128)(2,1)S(1)}, bf16[128,768]{1,0:T(8,128)(2,1)S(1)}, u32[]{:S(2)}, u32[]{:S(2)}) %collective-permute-start.12) | collective-permute-done | bytes 196640 | tf_op jit(solution)/shard_map/ppermute | solution.py:358
  142.3 3.8 %collective-permute-start.13 = (bf16[128,768]{1,0:T(8,128)(2,1)S(1)}, bf16[128,768]{1,0:T(8,128)(2,1)S(1)}, u32[]{:S(2)}, u32[]{:S(2)}) collective-permute-start(bf16[128,768]{1,0:T(8,128)(2,1)S(1)} %get-tuple-element.22), channel_id=1, source_target_pairs={{0,64},{32,96},{64,128},{96,160},{128,192},{160,224},{192,256},{22... | collective-permute-start | bytes 589832 | tf_op jit(solution)/shard_map/ppermute | solution.py:358
  146.1 2.0 %collective-permute-start.15 = (bf16[128,768]{1,0:T(8,128)(2,1)S(1)}, bf16[128,768]{1,0:T(8,128)(2,1)S(1)}, u32[]{:S(2)}, u32[]{:S(2)}) collective-permute-start(bf16[128,768]{1,0:T(8,128)(2,1)S(1)} %get-tuple-element.23), channel_id=1, source_target_pairs={{0,448},{32,480},{64,0},{96,32},{128,64},{160,96},{192,128},{224,1... | collective-permute-start | bytes 589832 | tf_op jit(solution)/shard_map/ppermute | solution.py:358
  150.5 3.8 %collective-permute-start.14 = (bf16[128,768]{1,0:T(8,128)(2,1)S(1)}, bf16[128,768]{1,0:T(8,128)(2,1)S(1)}, u32[]{:S(2)}, u32[]{:S(2)}) collective-permute-start(bf16[128,768]{1,0:T(8,128)(2,1)S(1)} %shard_map.86), channel_id=1, source_target_pairs={{0,64},{32,96},{64,128},{96,160},{128,192},{160,224},{192,256},{22... | collective-permute-start | bytes 589832 | tf_op jit(solution)/shard_map/ppermute | solution.py:358
  154.3 3.7 %collective-permute-done.14.refs_2_ = bf16[128,768]{1,0:T(8,128)(2,1)S(1)} collective-permute-done((bf16[128,768]{1,0:T(8,128)(2,1)S(1)}, bf16[128,768]{1,0:T(8,128)(2,1)S(1)}, u32[]{:S(2)}, u32[]{:S(2)}) %collective-permute-start.14) | collective-permute-done | bytes 196640 | tf_op jit(solution)/shard_map/ppermute | solution.py:358
  160.8 4.1 %all-to-all-done.1 = bf16[32,40,1024]{2,1,0:T(8,128)(2,1)S(1)} async-done(((bf16[32,40,1024]{2,1,0:T(8,128)(2,1)}), bf16[32,40,1024]{2,1,0:T(8,128)(2,1)S(1)}, u32[]{:S(2)}, u32[]{:S(2)}) %all-to-all-start.1) | async-done | bytes 2621472 | tf_op jit(solution)/shard_map/all_to_all | solution.py:349
  (37 shorter events, 22.9 us)
Async XLA Ops:
  4.5 13.3 %copy-start.4 = (bf16[1,128,384]{2,1,0:T(8,128)(2,1)S(1)}, bf16[1,128,384]{2,1,0:T(8,128)(2,1)}, u32[]{:S(2)}) copy-start(bf16[1,128,384]{2,1,0:T(8,128)(2,1)} %param.8) | copy-start | bytes 294916
  4.5 13.3 %copy-start.5 = (bf16[1,128,384]{2,1,0:T(8,128)(2,1)S(1)}, bf16[1,128,384]{2,1,0:T(8,128)(2,1)}, u32[]{:S(2)}) copy-start(bf16[1,128,384]{2,1,0:T(8,128)(2,1)} %param.9) | copy-start | bytes 294916
  4.5 85.6 %all-to-all-start = ((bf16[32,24,2048]{2,1,0:T(8,128)(2,1)}), bf16[32,24,2048]{2,1,0:T(8,128)(2,1)S(1)}, u32[]{:S(2)}, u32[]{:S(2)}) async-start(bf16[32,24,2048]{2,1,0:T(8,128)(2,1)} %bitcast.19), calls=%async_computation | async-start | bytes 6291456 | tf_op jit(solution)/shard_map/all_to_all | solution.py:349
  17.9 21.2 %collective-permute-start.6 = (bf16[128,768]{1,0:T(8,128)(2,1)S(1)}, bf16[128,768]{1,0:T(8,128)(2,1)S(1)}, u32[]{:S(2)}, u32[]{:S(2)}) collective-permute-start(bf16[128,768]{1,0:T(8,128)(2,1)S(1)} %shard_map.77.refs_0_), channel_id=1, source_target_pairs={{0,448},{32,480},{64,0},{96,32},{128,64},{160,96},{192,128},{224,1... | collective-permute-start | bytes 589832 | tf_op jit(solution)/shard_map/ppermute | solution.py:358
  20.3 23.4 %collective-permute-start.5 = (bf16[128,768]{1,0:T(8,128)(2,1)S(1)}, bf16[128,768]{1,0:T(8,128)(2,1)S(1)}, u32[]{:S(2)}, u32[]{:S(2)}) collective-permute-start(bf16[128,768]{1,0:T(8,128)(2,1)S(1)} %shard_map.77.refs_0_), channel_id=1, source_target_pairs={{0,384},{32,416},{64,448},{96,480},{128,0},{160,32},{192,64},{224,... | collective-permute-start | bytes 589832 | tf_op jit(solution)/shard_map/ppermute | solution.py:358
  26.4 25.3 %collective-permute-start.4 = (bf16[128,768]{1,0:T(8,128)(2,1)S(1)}, bf16[128,768]{1,0:T(8,128)(2,1)}, u32[]{:S(2)}, u32[]{:S(2)}) collective-permute-start(bf16[128,768]{1,0:T(8,128)(2,1)S(1)} %shard_map.77.refs_0_), channel_id=1, source_target_pairs={{0,320},{32,352},{64,384},{96,416},{128,448},{160,480},{192,0},{22... | collective-permute-start | bytes 589832 | tf_op jit(solution)/shard_map/ppermute | solution.py:358
  30.4 29.6 %collective-permute-start.3 = (bf16[128,768]{1,0:T(8,128)(2,1)S(1)}, bf16[128,768]{1,0:T(8,128)(2,1)}, u32[]{:S(2)}, u32[]{:S(2)}) collective-permute-start(bf16[128,768]{1,0:T(8,128)(2,1)S(1)} %shard_map.77.refs_0_), channel_id=1, source_target_pairs={{0,256},{32,288},{64,320},{96,352},{128,384},{160,416},{192,448},{... | collective-permute-start | bytes 589832 | tf_op jit(solution)/shard_map/ppermute | solution.py:358
  35.4 24.6 %collective-permute-start.2 = (bf16[128,768]{1,0:T(8,128)(2,1)S(1)}, bf16[128,768]{1,0:T(8,128)(2,1)}, u32[]{:S(2)}, u32[]{:S(2)}) collective-permute-start(bf16[128,768]{1,0:T(8,128)(2,1)S(1)} %shard_map.77.refs_0_), channel_id=1, source_target_pairs={{0,192},{32,224},{64,256},{96,288},{128,320},{160,352},{192,384},{... | collective-permute-start | bytes 589832 | tf_op jit(solution)/shard_map/ppermute | solution.py:358
  39.2 27.8 %collective-permute-start.1 = (bf16[128,768]{1,0:T(8,128)(2,1)S(1)}, bf16[128,768]{1,0:T(8,128)(2,1)}, u32[]{:S(2)}, u32[]{:S(2)}) collective-permute-start(bf16[128,768]{1,0:T(8,128)(2,1)S(1)} %shard_map.77.refs_0_), channel_id=1, source_target_pairs={{0,128},{32,160},{64,192},{96,224},{128,256},{160,288},{192,320},{... | collective-permute-start | bytes 589832 | tf_op jit(solution)/shard_map/ppermute | solution.py:358
  43.7 0.7 copy-start.1
  44.3 25.6 %collective-permute-start = (bf16[128,768]{1,0:T(8,128)(2,1)S(1)}, bf16[128,768]{1,0:T(8,128)(2,1)}, u32[]{:S(2)}, u32[]{:S(2)}) collective-permute-start(bf16[128,768]{1,0:T(8,128)(2,1)S(1)} %shard_map.77.refs_0_), channel_id=1, source_target_pairs={{0,64},{32,96},{64,128},{96,160},{128,192},{160,224},{192,256},{22... | collective-permute-start | bytes 589832 | tf_op jit(solution)/shard_map/ppermute | solution.py:358
  69.9 0.9 copy-start.2
  72.3 5.3 %collective-permute-start.7 = (bf16[1024,768]{1,0:T(8,128)(2,1)S(1)}, bf16[1024,768]{1,0:T(8,128)(2,1)S(1)}, u32[]{:S(2)}, u32[]{:S(2)}) collective-permute-start(bf16[1024,768]{1,0:T(8,128)(2,1)S(1)} %shard_map.78.refs_1_), channel_id=1, source_target_pairs={{0,32},{32,0},{64,96},{96,64},{128,160},{160,128},{192,224},{224,1... | collective-permute-start | bytes 4718600 | tf_op jit(solution)/shard_map/ppermute | solution.py:361
  78.3 1.7 %copy-start = (bf16[2048,768]{1,0:T(8,128)(2,1)}, bf16[2048,768]{1,0:T(8,128)(2,1)S(1)}, u32[]{:S(2)}) copy-start(bf16[2048,768]{1,0:T(8,128)(2,1)S(1)} %shard_map.79.weight_hbm) | copy-start | bytes 9437188
  97.6 67.2 %all-to-all-start.1 = ((bf16[32,40,1024]{2,1,0:T(8,128)(2,1)}), bf16[32,40,1024]{2,1,0:T(8,128)(2,1)S(1)}, u32[]{:S(2)}, u32[]{:S(2)}) async-start(bf16[32,40,1024]{2,1,0:T(8,128)(2,1)} %bitcast.20), calls=%async_computation.1 | async-start | bytes 5242880 | tf_op jit(solution)/shard_map/all_to_all | solution.py:349
  104.0 1.9 %copy-start.7 = (bf16[768,2048]{1,0:T(8,128)(2,1)S(1)}, bf16[768,2048]{1,0:T(8,128)(2,1)}, u32[]{:S(2)}) copy-start(bf16[768,2048]{1,0:T(8,128)(2,1)} %get-tuple-element.15.refs_1_) | copy-start | bytes 9437188
  105.8 1.3 copy-start.8
  109.1 5.3 %collective-permute-start.8 = (bf16[1024,768]{1,0:T(8,128)(2,1)S(1)}, bf16[1024,768]{1,0:T(8,128)(2,1)S(1)}, u32[]{:S(2)}, u32[]{:S(2)}) collective-permute-start(bf16[1024,768]{1,0:T(8,128)(2,1)S(1)} %shard_map.82), channel_id=1, source_target_pairs={{0,32},{32,0},{64,96},{96,64},{128,160},{160,128},{192,224},{224,1... | collective-permute-start | bytes 4718600 | tf_op jit(solution)/shard_map/ppermute | solution.py:361
  115.8 8.8 %collective-permute-start.9 = (bf16[128,768]{1,0:T(8,128)(2,1)S(1)}, bf16[128,768]{1,0:T(8,128)(2,1)S(1)}, u32[]{:S(2)}, u32[]{:S(2)}) collective-permute-start(bf16[128,768]{1,0:T(8,128)(2,1)S(1)} %get-tuple-element.18), channel_id=1, source_target_pairs={{0,64},{32,96},{64,128},{96,160},{128,192},{160,224},{192,256},{22... | collective-permute-start | bytes 589832 | tf_op jit(solution)/shard_map/ppermute | solution.py:358
  119.3 8.6 %collective-permute-start.10 = (bf16[128,768]{1,0:T(8,128)(2,1)S(1)}, bf16[128,768]{1,0:T(8,128)(2,1)S(1)}, u32[]{:S(2)}, u32[]{:S(2)}) collective-permute-start(bf16[128,768]{1,0:T(8,128)(2,1)S(1)} %get-tuple-element.19), channel_id=1, source_target_pairs={{0,448},{32,480},{64,0},{96,32},{128,64},{160,96},{192,128},{224,1... | collective-permute-start | bytes 589832 | tf_op jit(solution)/shard_map/ppermute | solution.py:358
  128.5 8.2 %collective-permute-start.11 = (bf16[128,768]{1,0:T(8,128)(2,1)S(1)}, bf16[128,768]{1,0:T(8,128)(2,1)S(1)}, u32[]{:S(2)}, u32[]{:S(2)}) collective-permute-start(bf16[128,768]{1,0:T(8,128)(2,1)S(1)} %get-tuple-element.20), channel_id=1, source_target_pairs={{0,64},{32,96},{64,128},{96,160},{128,192},{160,224},{192,256},{22... | collective-permute-start | bytes 589832 | tf_op jit(solution)/shard_map/ppermute | solution.py:358
  133.0 8.6 %collective-permute-start.12 = (bf16[128,768]{1,0:T(8,128)(2,1)S(1)}, bf16[128,768]{1,0:T(8,128)(2,1)S(1)}, u32[]{:S(2)}, u32[]{:S(2)}) collective-permute-start(bf16[128,768]{1,0:T(8,128)(2,1)S(1)} %get-tuple-element.21), channel_id=1, source_target_pairs={{0,448},{32,480},{64,0},{96,32},{128,64},{160,96},{192,128},{224,1... | collective-permute-start | bytes 589832 | tf_op jit(solution)/shard_map/ppermute | solution.py:358
  142.3 7.6 %collective-permute-start.13 = (bf16[128,768]{1,0:T(8,128)(2,1)S(1)}, bf16[128,768]{1,0:T(8,128)(2,1)S(1)}, u32[]{:S(2)}, u32[]{:S(2)}) collective-permute-start(bf16[128,768]{1,0:T(8,128)(2,1)S(1)} %get-tuple-element.22), channel_id=1, source_target_pairs={{0,64},{32,96},{64,128},{96,160},{128,192},{160,224},{192,256},{22... | collective-permute-start | bytes 589832 | tf_op jit(solution)/shard_map/ppermute | solution.py:358
  146.1 13.3 %copy-start.6 = (s32[128,8]{0,1:T(8,128)S(1)}, s32[128,8]{0,1:T(8,128)}, u32[]{:S(2)}) copy-start(s32[128,8]{0,1:T(8,128)} %param.6) | copy-start | bytes 12292
  146.1 8.2 %collective-permute-start.15 = (bf16[128,768]{1,0:T(8,128)(2,1)S(1)}, bf16[128,768]{1,0:T(8,128)(2,1)S(1)}, u32[]{:S(2)}, u32[]{:S(2)}) collective-permute-start(bf16[128,768]{1,0:T(8,128)(2,1)S(1)} %get-tuple-element.23), channel_id=1, source_target_pairs={{0,448},{32,480},{64,0},{96,32},{128,64},{160,96},{192,128},{224,1... | collective-permute-start | bytes 589832 | tf_op jit(solution)/shard_map/ppermute | solution.py:358
  150.5 7.6 %collective-permute-start.14 = (bf16[128,768]{1,0:T(8,128)(2,1)S(1)}, bf16[128,768]{1,0:T(8,128)(2,1)S(1)}, u32[]{:S(2)}, u32[]{:S(2)}) collective-permute-start(bf16[128,768]{1,0:T(8,128)(2,1)S(1)} %shard_map.86), channel_id=1, source_target_pairs={{0,64},{32,96},{64,128},{96,160},{128,192},{160,224},{192,256},{22... | collective-permute-start | bytes 589832 | tf_op jit(solution)/shard_map/ppermute | solution.py:358
  159.4 0.9 copy-start.3
